TPU v7x, 512 devices: a whole 4x4x16 slice. The times are simulated.
512 devices in a mesh: dp: 32 (over x, z_lo), leaf: 16 (over y, z_hi, core).
Axes of the slice: x: 4, y: 4, z: 16 (z_hi: 2, z_lo: 8; z = z_hi * 8 + z_lo), core: 2. Of those that a mesh axis runs over, the one named last changes fastest.
Arguments:
- hidden: bfloat16 [512, 128, 5120], P(('dp', 'leaf')), may hold values from -6 to 6
- queries: bfloat16 [512, 128, 4096], P(('dp', 'leaf')), may hold values from -80 to 80
- key_value_weight: bfloat16 [5120, 1024], P('dp'), may hold values from -0.078125 to 0.078125
- k_gain: float32 [128], replicated, may hold values from 0.1 to 1.9
- cached_ancestor_keys: bfloat16 [32, 16, 128, 512], P('dp', 'leaf'), may hold values from -6 to 6
- cached_ancestor_values: bfloat16 [32, 16, 128, 512], P('dp', 'leaf'), may hold values from -6 to 6
- ancestor_mask: int32 [512, 16], P(('dp', 'leaf')), may hold values from 0 to 1, as said below
- fork_offset: int32 [512], P(('dp', 'leaf')), may hold values from 0 to 2047
Outputs:
- attended: bfloat16 [512, 128, 4096], P(('dp', 'leaf'))
Inputs may be any that keep to these rules, and one draw needn't show every extreme that they name: `ancestor_mask`: for each branch the ones form one run of consecutive blocks whose last is block fork_offset // 128.
All inputs are finite; a program needn't handle non-finite values.
Results may differ from a plain program's by a relative error of at most 0.0057.
Values may be sent and summed in bfloat16 or wider, within the bound.
No kernel may reach another device: no remote copies, remote signals or barrier semaphores. Data moves between devices by JAX's collectives and lax.ppermute only.
A program may use at most 64 MiB of HBM per device.

v0:
```python
import jax
import jax.numpy as jnp
from jax import lax
from jax.sharding import PartitionSpec as P

EPS = 1e-06
THETA = 1000000.0
FLOOR = -1e30


def rotate_keys(segment_keys, positions):
    half = segment_keys.shape[-1] // 2
    freq = THETA ** (-jnp.arange(half, dtype=jnp.float32) * 2.0 / segment_keys.shape[-1])
    angle = positions.astype(jnp.float32)[..., None] * freq
    cosine = jnp.cos(angle)[..., None, :]
    sine = jnp.sin(angle)[..., None, :]
    first = segment_keys[..., :half]
    second = segment_keys[..., half:]
    return jnp.concatenate(
        [first * cosine - second * sine, second * cosine + first * sine], axis=-1
    )


def absorb(state, scores, segment_values, form):
    top, total, summed = state
    new_top = jnp.maximum(top, jnp.max(scores, axis=-1))
    factor = jnp.exp(top - new_top)
    weights = jnp.exp(scores - new_top[..., None])
    total = total * factor + jnp.sum(weights, axis=-1)
    update = jnp.einsum(
        form, weights.astype(jnp.bfloat16), segment_values, preferred_element_type=jnp.float32
    )
    summed = summed * jnp.transpose(factor, (0, 3, 1, 2))[..., None] + update
    return (new_top, total, summed)


def on_device(
    hidden,
    queries,
    key_value_weight,
    k_gain,
    cached_ancestor_keys,
    cached_ancestor_values,
    ancestor_mask,
    fork_offset,
):
    branches, seg, width = hidden.shape
    qwidth = queries.shape[2]
    head_dim = k_gain.shape[0]
    key_value_width = key_value_weight.shape[1] // 2
    kv_heads = key_value_width // head_dim
    query_groups = qwidth // key_value_width
    block = cached_ancestor_keys.shape[2]
    total_blocks = ancestor_mask.shape[1]
    scale = head_dim ** (-0.5)
    expanded = jnp.broadcast_to(ancestor_mask[:, :, None], (branches, total_blocks, block))
    expanded = expanded.reshape(branches, total_blocks * block)
    positions_all = jnp.arange(total_blocks * block, dtype=jnp.int32)
    visible = (expanded == 1) & (positions_all[None, :] <= fork_offset[:, None])
    starts = jnp.sum(visible.astype(jnp.int32), axis=1)
    grouped_queries = queries.reshape(branches, seg, kv_heads, query_groups, head_dim)
    initial = (
        jnp.full((branches, kv_heads, query_groups, seg), FLOOR, jnp.float32),
        jnp.zeros((branches, kv_heads, query_groups, seg), jnp.float32),
        jnp.zeros((branches, seg, kv_heads, query_groups, head_dim), jnp.float32),
    )
    keys_piece = lax.all_gather(cached_ancestor_keys, "leaf", axis=1, tiled=True)
    values_piece = lax.all_gather(cached_ancestor_values, "leaf", axis=1, tiled=True)
    count = keys_piece.shape[1]

    def one_block(index, inner):
        keys_block = lax.dynamic_index_in_dim(keys_piece[0], index, 0, keepdims=False)
        keys_block = keys_block.reshape(block, kv_heads, head_dim)
        values_block = lax.dynamic_index_in_dim(values_piece[0], index, 0, keepdims=False)
        values_block = values_block.reshape(block, kv_heads, head_dim)
        seen = lax.dynamic_slice_in_dim(visible, index * block, block, 1)
        scores = (
            jnp.einsum(
                "bsgjd,lgd->bgjsl", grouped_queries, keys_block, preferred_element_type=jnp.float32
            )
            * scale
        )
        scores = jnp.where(seen[:, None, None, None, :], scores, -jnp.inf)
        return absorb(inner, scores, values_block, "bgjsl,lgd->bsgjd")

    state = lax.fori_loop(0, count, one_block, initial)
    tokens = hidden.reshape(branches * seg, width)
    projected_rows = jnp.dot(
        tokens,
        lax.all_gather(key_value_weight, "dp", axis=0, tiled=True),
        preferred_element_type=jnp.float32,
    )
    segment_keys = projected_rows[:, :key_value_width].reshape(branches, seg, kv_heads, head_dim)
    segment_keys = (
        segment_keys
        * lax.rsqrt(jnp.mean(segment_keys * segment_keys, axis=-1, keepdims=True) + EPS)
        * k_gain
    )
    token_positions = starts[:, None] + jnp.arange(seg, dtype=jnp.int32)[None, :]
    segment_keys = rotate_keys(segment_keys, token_positions).astype(jnp.bfloat16)
    segment_values = (
        projected_rows[:, key_value_width:]
        .reshape(branches, seg, kv_heads, head_dim)
        .astype(jnp.bfloat16)
    )
    causal = jnp.arange(seg)[:, None] >= jnp.arange(seg)[None, :]
    scores = (
        jnp.einsum(
            "bsgjd,btgd->bgjst", grouped_queries, segment_keys, preferred_element_type=jnp.float32
        )
        * scale
    )
    scores = jnp.where(causal, scores, -jnp.inf)
    top, total, summed = absorb(state, scores, segment_values, "bgjst,btgd->bsgjd")
    result = summed / jnp.transpose(total, (0, 3, 1, 2))[..., None]
    return result.reshape(branches, seg, qwidth).astype(jnp.bfloat16)


def solution(mesh):
    in_specs = (
        P(("dp", "leaf"), None, None),
        P(("dp", "leaf"), None, None),
        P("dp", None),
        P(),
        P("dp", "leaf", None, None),
        P("dp", "leaf", None, None),
        P(("dp", "leaf"), None),
        P(("dp", "leaf")),
    )
    out_specs = P(("dp", "leaf"), None, None)
    return jax.shard_map(
        on_device, mesh=mesh, in_specs=in_specs, out_specs=out_specs, check_vma=False
    )
```

profile of v0, /device:TPU:24, one launch (start us, length us, event | category | flops | bytes accessed | tf_op | source)
XLA Modules:
  0.0 471.8 jit_solution(2272274287829747957)
XLA Ops:
  17.4 89.3 %all-gather.4.cloned.1.call-done = bf16[1,16,128,512]{3,2,0,1:T(8,128)(2,1)} async-done(((bf16[1,1,128,512]{3,2,0,1:T(8,128)(2,1)}), bf16[1,16,128,512]{3,2,0,1:T(8,128)(2,1)}) %all-gather.4.cloned.1.call-update) | async-done | bytes 2097168 | tf_op jit(solution)/shard_map/all_gather | solution.py:67
  106.7 86.2 %all-gather.6.cloned.1.call-done = bf16[1,16,128,512]{3,2,0,1:T(8,128)(2,1)} async-done(((bf16[1,1,128,512]{3,2,0,1:T(8,128)(2,1)}), bf16[1,16,128,512]{3,2,0,1:T(8,128)(2,1)}) %all-gather.6.cloned.1.call-update) | async-done | bytes 2097168 | tf_op jit(solution)/shard_map/all_gather | solution.py:68
  193.0 220.8 %while.18 = (s32[]{:T(128)}, f32[1,4,8,128]{3,2,1,0:T(8,128)}, f32[1,4,8,128]{3,2,1,0:T(8,128)}, f32[1,128,4,8,128]{1,4,3,2,0:T(8,128)}, pred[1,2048]{1,0:T(4,12...) while((s32[]{:T(128)}, f32[1,4,8,128]{3,2,1,0:T(8,128)}, ...), condition=%wide.region_3.4_spmd.clone, body=%wide.region_0.3_spmd.clone.sunk | while | flops 275800064 | bytes 13125011 | solution.py:86
  202.3 3.0 bitcast_add_fusion.7
  215.4 3.8 bitcast_add_fusion.7
  229.3 3.8 bitcast_add_fusion.7
  243.2 3.8 bitcast_add_fusion.7
  257.1 3.8 bitcast_add_fusion.7
  271.0 3.8 bitcast_add_fusion.7
  284.9 3.8 bitcast_add_fusion.7
  298.8 3.8 bitcast_add_fusion.7
  312.7 3.8 bitcast_add_fusion.7
  326.6 3.8 bitcast_add_fusion.7
  340.4 3.8 bitcast_add_fusion.7
  354.3 3.8 bitcast_add_fusion.7
  360.5 2.5 bitcast_reduce_fusion.2
  368.2 3.8 bitcast_add_fusion.7
  374.4 2.5 bitcast_reduce_fusion.2
  382.2 3.8 bitcast_add_fusion.7
  388.3 2.5 bitcast_reduce_fusion.2
  396.0 3.8 bitcast_add_fusion.7
  410.0 3.8 bitcast_add_fusion.7
  413.8 41.1 %all-gather.8.cloned.1.call-done = bf16[5120,1024]{1,0:T(8,128)(2,1)} async-done(((bf16[160,1024]{1,0:T(8,128)(2,1)}), bf16[5120,1024]{1,0:T(8,128)(2,1)}) %all-gather.8.cloned.1.call-update) | async-done | bytes 10485776 | tf_op jit(solution)/shard_map/all_gather | solution.py:90
  454.9 5.5 %fusion.18 = f32[128,1024]{1,0:T(8,128)S(1)} fusion(bf16[5120,1024]{1,0:T(8,128)(2,1)} %all-gather.8.cloned.1.call-done, bf16[1,128,5120]{2,1,0:T(8,128)(2,1)S(1)} %copy-done), kind=kOutput, calls=%fused_computation.32 | convolution fusion | flops 1342177280 | bytes 12320768 | tf_op jit(solution)/shard_map/dot_general | solution.py:88
  (292 shorter events, 167.5 us)
Async XLA Ops:
  6.5 448.3 %copy-start = (bf16[1,128,5120]{2,1,0:T(8,128)(2,1)S(1)}, bf16[1,128,5120]{2,1,0:T(8,128)(2,1)}, u32[]{:S(2)}) copy-start(bf16[1,128,5120]{2,1,0:T(8,128)(2,1)} %param.10) | copy-start | bytes 3932164
  6.5 100.2 %all-gather.4.cloned.1.call-start = ((), (), s32[]{:S(2)}) async-start(), calls=%async_computation | async-start | bytes 2228224 | tf_op jit(solution)/shard_map/all_gather | solution.py:67
  7.3 185.7 %all-gather.6.cloned.1.call-start = ((), (), s32[]{:S(2)}) async-start(), calls=%async_computation.1 | async-start | bytes 2228224 | tf_op jit(solution)/shard_map/all_gather | solution.py:68
  8.0 446.9 %all-gather.8.cloned.1.call-start = ((), (), s32[]{:S(2)}) async-start(), calls=%async_computation.2 | async-start | bytes 10813440 | tf_op jit(solution)/shard_map/all_gather | solution.py:90
  193.0 4.8 %copy-start.8 = (pred[128]{0:T(512)(128)(4,1)}, pred[128]{0:T(512)(128)(4,1)S(1)}, u32[]{:S(2)}) copy-start(pred[128]{0:T(512)(128)(4,1)S(1)} %dynamic-slice_bitcast_fusion.2) | copy-start | bytes 388 | tf_op jit(solution)/shard_map/while
  205.3 4.8 %copy-start.8 = (pred[128]{0:T(512)(128)(4,1)}, pred[128]{0:T(512)(128)(4,1)S(1)}, u32[]{:S(2)}) copy-start(pred[128]{0:T(512)(128)(4,1)S(1)} %dynamic-slice_bitcast_fusion.2) | copy-start | bytes 388 | tf_op jit(solution)/shard_map/while
  215.4 3.8 copy-start.11
  219.2 4.8 %copy-start.8 = (pred[128]{0:T(512)(128)(4,1)}, pred[128]{0:T(512)(128)(4,1)S(1)}, u32[]{:S(2)}) copy-start(pred[128]{0:T(512)(128)(4,1)S(1)} %dynamic-slice_bitcast_fusion.2) | copy-start | bytes 388 | tf_op jit(solution)/shard_map/while
  233.1 4.8 %copy-start.8 = (pred[128]{0:T(512)(128)(4,1)}, pred[128]{0:T(512)(128)(4,1)S(1)}, u32[]{:S(2)}) copy-start(pred[128]{0:T(512)(128)(4,1)S(1)} %dynamic-slice_bitcast_fusion.2) | copy-start | bytes 388 | tf_op jit(solution)/shard_map/while
  247.0 4.8 %copy-start.8 = (pred[128]{0:T(512)(128)(4,1)}, pred[128]{0:T(512)(128)(4,1)S(1)}, u32[]{:S(2)}) copy-start(pred[128]{0:T(512)(128)(4,1)S(1)} %dynamic-slice_bitcast_fusion.2) | copy-start | bytes 388 | tf_op jit(solution)/shard_map/while
  257.1 3.9 copy-start.11
  261.0 4.8 %copy-start.8 = (pred[128]{0:T(512)(128)(4,1)}, pred[128]{0:T(512)(128)(4,1)S(1)}, u32[]{:S(2)}) copy-start(pred[128]{0:T(512)(128)(4,1)S(1)} %dynamic-slice_bitcast_fusion.2) | copy-start | bytes 388 | tf_op jit(solution)/shard_map/while
  274.9 4.8 %copy-start.8 = (pred[128]{0:T(512)(128)(4,1)}, pred[128]{0:T(512)(128)(4,1)S(1)}, u32[]{:S(2)}) copy-start(pred[128]{0:T(512)(128)(4,1)S(1)} %dynamic-slice_bitcast_fusion.2) | copy-start | bytes 388 | tf_op jit(solution)/shard_map/while
  288.7 4.8 %copy-start.8 = (pred[128]{0:T(512)(128)(4,1)}, pred[128]{0:T(512)(128)(4,1)S(1)}, u32[]{:S(2)}) copy-start(pred[128]{0:T(512)(128)(4,1)S(1)} %dynamic-slice_bitcast_fusion.2) | copy-start | bytes 388 | tf_op jit(solution)/shard_map/while
  302.6 4.8 %copy-start.8 = (pred[128]{0:T(512)(128)(4,1)}, pred[128]{0:T(512)(128)(4,1)S(1)}, u32[]{:S(2)}) copy-start(pred[128]{0:T(512)(128)(4,1)S(1)} %dynamic-slice_bitcast_fusion.2) | copy-start | bytes 388 | tf_op jit(solution)/shard_map/while
  316.5 4.8 %copy-start.8 = (pred[128]{0:T(512)(128)(4,1)}, pred[128]{0:T(512)(128)(4,1)S(1)}, u32[]{:S(2)}) copy-start(pred[128]{0:T(512)(128)(4,1)S(1)} %dynamic-slice_bitcast_fusion.2) | copy-start | bytes 388 | tf_op jit(solution)/shard_map/while
  330.4 4.8 %copy-start.8 = (pred[128]{0:T(512)(128)(4,1)}, pred[128]{0:T(512)(128)(4,1)S(1)}, u32[]{:S(2)}) copy-start(pred[128]{0:T(512)(128)(4,1)S(1)} %dynamic-slice_bitcast_fusion.2) | copy-start | bytes 388 | tf_op jit(solution)/shard_map/while
  344.3 4.8 %copy-start.8 = (pred[128]{0:T(512)(128)(4,1)}, pred[128]{0:T(512)(128)(4,1)S(1)}, u32[]{:S(2)}) copy-start(pred[128]{0:T(512)(128)(4,1)S(1)} %dynamic-slice_bitcast_fusion.2) | copy-start | bytes 388 | tf_op jit(solution)/shard_map/while
  358.1 4.8 %copy-start.8 = (pred[128]{0:T(512)(128)(4,1)}, pred[128]{0:T(512)(128)(4,1)S(1)}, u32[]{:S(2)}) copy-start(pred[128]{0:T(512)(128)(4,1)S(1)} %dynamic-slice_bitcast_fusion.2) | copy-start | bytes 388 | tf_op jit(solution)/shard_map/while
  372.1 4.8 %copy-start.8 = (pred[128]{0:T(512)(128)(4,1)}, pred[128]{0:T(512)(128)(4,1)S(1)}, u32[]{:S(2)}) copy-start(pred[128]{0:T(512)(128)(4,1)S(1)} %dynamic-slice_bitcast_fusion.2) | copy-start | bytes 388 | tf_op jit(solution)/shard_map/while
  386.0 4.8 %copy-start.8 = (pred[128]{0:T(512)(128)(4,1)}, pred[128]{0:T(512)(128)(4,1)S(1)}, u32[]{:S(2)}) copy-start(pred[128]{0:T(512)(128)(4,1)S(1)} %dynamic-slice_bitcast_fusion.2) | copy-start | bytes 388 | tf_op jit(solution)/shard_map/while
  396.0 3.8 copy-start.11
  399.9 4.8 %copy-start.8 = (pred[128]{0:T(512)(128)(4,1)}, pred[128]{0:T(512)(128)(4,1)S(1)}, u32[]{:S(2)}) copy-start(pred[128]{0:T(512)(128)(4,1)S(1)} %dynamic-slice_bitcast_fusion.2) | copy-start | bytes 388 | tf_op jit(solution)/shard_map/while
  413.8 47.2 %copy-start.12 = (f32[128]{0:T(128)S(1)}, f32[128]{0:T(128)}, u32[]{:S(2)}) copy-start(f32[128]{0:T(128)} %param.13) | copy-start | bytes 1540
  (37 other events, 69.6 us)
Sparse Core Ops, SparseCore 0:
  10.6 96.0 all-gather.3
  110.0 82.9 all-gather.5
  195.0 259.7 all-gather.7
where the time goes:
time: 478 us; the launch traced here: 472 us
  waiting for transfers between devices  219 us (46%)
  matrix products  107 us (22%)
  other arithmetic  66.4 us (14%)
  local copies, waits for them, and re-layouts  65.6 us (14%)
  between operations  14 us (3%)
    all_gather x1, waiting for transfers between devices, on_device(): lax.all_gather(cached_ancestor_keys, 'leaf', axis=1, tiled=True)  89.3 us
    all_gather x1, waiting for transfers between devices, on_device(): lax.all_gather(cached_ancestor_values, 'leaf', axis=1, tiled=True)  86.2 us
    dot_general x17, matrix products, absorb(): jnp.einsum(form, weights.astype(jnp.bfloat16), segment_values, preferred_...  61.1 us
    all_gather x1, waiting for transfers between devices, on_device(): lax.all_gather(key_value_weight, 'dp', axis=0, tiled=True)  41.1 us
    dot_general x16, matrix products, one_block(): jnp.einsum('bsgjd,lgd->bgjsl', grouped_queries, keys_block, preferred_ele...  39.4 us
    dynamic_slice x32, local copies, waits for them, and re-layouts, one_block(): lax.dynamic_index_in_dim(values_piece[0], index, 0, keepdims=False)  27.8 us
    mul x17, other arithmetic, absorb(): summed = summed * jnp.transpose(factor, (0, 3, 1, 2))[..., None] + update  21.5 us
    add x16, other arithmetic, absorb(): total = total * factor + jnp.sum(weights, axis=-1)  21 us
  transfers between devices with their start and end apart: 3, of which 3 were waited for; matrix products, arithmetic and copies ran while one was open for 46% of the time, Pallas kernels for 0%

commit v1 on v0

v1 whole, which is shorter than its diff:
```python
import functools
import math

import jax
import jax.numpy as jnp
from jax import lax
from jax.experimental import pallas as pl
from jax.experimental.pallas import tpu as pltpu
from jax.sharding import PartitionSpec as P

EPS = 1e-06
THETA = 1000000.0
HEAD = 128
TOK = 128
FLOOR = -1e30
EXP_SCALE = HEAD ** (-0.5) * math.log2(math.e)
AXES = ("dp", "leaf")
NX, NZL, NY, NZH = 4, 8, 4, 2
NZ = NZL * NZH
BF = jnp.bfloat16
F32 = jnp.float32
VMEM = pl.BlockSpec(memory_space=pltpu.VMEM)
SMEM = pl.BlockSpec(memory_space=pltpu.SMEM)
HBM = pl.BlockSpec(memory_space=pltpu.HBM)
VMEM_LIMIT = 36 * 2**20
CORE, Y, ZH, X, ZL = range(5)
FIRST, SECOND = (0, 4, 2, 6), (1, 5, 3, 7)
ROUND_Y = (0, 2, 1, 3)


def place(x, y, z, core):
    return ((x % NX * NZL + z % NZL) * NY + y % NY) * 4 + (z // NZL % NZH) * 2 + core


def move(a, x=0, y=0, z=0, ways=(1, -1)):
    pairs = []
    for px in range(NX):
        for pz in range(NZ):
            for py in range(NY):
                for core, way in enumerate(ways):
                    to = place(px + way * x, py + way * y, (pz + way * z) % NZ, core)
                    pairs.append((place(px, py, pz, core), to))
    return lax.ppermute(a, AXES, pairs)


def swap_cores(a):
    pairs = [(n, n ^ 1) for n in range(NX * NY * NZ * 2)]
    return lax.ppermute(a, AXES, pairs)


def together(*arrays):
    return lax.optimization_barrier(arrays)


def dot_nt(a, b):
    return lax.dot_general(a, b, (((1,), (1,)), ((), ())), preferred_element_type=F32)


def run_copies(pairs, sems):
    copies = [pltpu.make_async_copy(a, b, sems.at[n]) for n, (a, b) in enumerate(pairs)]
    for copy in copies:
        copy.start()
    for copy in copies:
        copy.wait()


def columns(ref, start, size):
    return ref.at[:, pl.ds(pl.multiple_of(start, HEAD), size)]


def load_kernel(coord_ref, w_ref, k_ref, v_ref, load_ref):
    core = coord_ref[CORE]
    half = w_ref.shape[1] // 4
    shard = w_ref.shape[0]
    for n in range(2):
        start = pl.multiple_of((2 * n + core) * half, HEAD)
        load_ref[:shard, n * half : (n + 1) * half] = w_ref[:, pl.ds(start, half)]
    load_ref[shard : shard + TOK, :] = k_ref[...]
    load_ref[shard + TOK :, :] = v_ref[...]


def pick_load(coords, w, k, v):
    return pl.pallas_call(
        load_kernel,
        out_shape=jax.ShapeDtypeStruct((w.shape[0] + 2 * TOK, w.shape[1] // 2), BF),
        in_specs=[SMEM, VMEM, VMEM, VMEM],
        out_specs=VMEM,
        name="pick_load",
    )(coords, w, k, v)


def part_kernel(away, coord_ref, load_ref, hidden_ref, unit_ref, *part_refs):
    first = load_ref.shape[0] - 2 * TOK
    for n in range(2):
        unit_ref[n] = load_ref[first + n * TOK : first + (n + 1) * TOK, :]
    part = hidden_ref.shape[1] // NX
    for dx, ref in zip(away, part_refs):
        start = pl.multiple_of(lax.rem(coord_ref[X] + dx, NX) * part, HEAD)
        ref[...] = hidden_ref[:, pl.ds(start, part)]


def pick_parts(coords, load, hidden, away):
    part = jax.ShapeDtypeStruct((TOK, hidden.shape[1] // NX), BF)
    return pl.pallas_call(
        functools.partial(part_kernel, away),
        out_shape=(jax.ShapeDtypeStruct((2, TOK, load.shape[1]), BF),) + (part,) * len(away),
        in_specs=[SMEM, VMEM, VMEM],
        out_specs=(VMEM,) * (1 + len(away)),
        cost_estimate=pl.CostEstimate(flops=10**11, bytes_accessed=1000, transcendentals=0),
        name="pick_parts",
    )(coords, load, hidden)


def project_kernel(coord_ref, hidden_ref, *refs):
    peers, refs = refs[: NX - 1], refs[NX - 1 :]
    bundles, refs = refs[:4], refs[4:]
    own_ref, backs, (h_buf, w_buf, sems) = refs[0], refs[1:NX], refs[NX:]
    core, x, zl = coord_ref[CORE], coord_ref[X], coord_ref[ZL]
    part = h_buf.shape[1]
    pairs = [(columns(hidden_ref, x * part, part), h_buf.at[pl.ds(0, TOK)])]
    for n, ref in enumerate(peers):
        pairs.append((ref, h_buf.at[pl.ds((n + 1) * TOK, TOK)]))
    shard = part // NZL
    for ref, offsets, swapped in zip(bundles, (FIRST, SECOND) * 2, (0, 0, 1, 1)):
        from_core = 1 - core if swapped else core
        way = 1 - 2 * from_core
        for n, dz in enumerate(offsets):
            start = pl.multiple_of(lax.rem(zl - way * dz + NZL, NZL) * shard, 16)
            pairs.append((ref.at[pl.ds(n * shard, shard)], w_buf.at[from_core, pl.ds(start, shard)]))
    run_copies(pairs, sems)
    half = w_buf.shape[2] // 2
    keys = 2 * half
    for side in range(2):
        product = jnp.dot(h_buf[...], w_buf[side], preferred_element_type=F32)
        k, v = product[:, :half], product[:, half:]
        own_ref[:, side * half : (side + 1) * half] = k[:TOK]
        own_ref[:, keys + side * half : keys + (side + 1) * half] = v[:TOK]
        for n, ref in enumerate(backs):
            rows = slice((n + 1) * TOK, (n + 2) * TOK)
            high = k[rows].astype(BF)
            low = (k[rows] - high.astype(F32)).astype(BF)
            for i, value in enumerate((high, low, v[rows].astype(BF))):
                ref[:, i * keys + side * half : i * keys + (side + 1) * half] = value


def project(coords, hidden, peers, bundles):
    part = peers[0].shape[1]
    width = bundles[0].shape[1]
    back = jax.ShapeDtypeStruct((TOK, 3 * width), BF)
    return pl.pallas_call(
        project_kernel,
        out_shape=(jax.ShapeDtypeStruct((TOK, 2 * width), F32),) + (back,) * (NX - 1),
        in_specs=[SMEM] + [HBM] * (1 + len(peers) + len(bundles)),
        out_specs=(VMEM,) * NX,
        scratch_shapes=[
            pltpu.VMEM((NX * TOK, part), BF),
            pltpu.VMEM((2, part, width), BF),
            pltpu.SemaphoreType.DMA((NX + 2 * NZL,)),
        ],
        compiler_params=pltpu.CompilerParams(vmem_limit_bytes=VMEM_LIMIT),
        cost_estimate=pl.CostEstimate(flops=10**11, bytes_accessed=1000, transcendentals=0),
        name="project",
    )(coords, hidden, *peers, *bundles)


def pack_kernel(*refs):
    at = 0
    for ref in refs[:-1]:
        refs[-1][at : at + ref.shape[0]] = ref[...]
        at += ref.shape[0]


def pack(blocks, rank):
    return pl.pallas_call(
        pack_kernel,
        out_shape=jax.ShapeDtypeStruct((sum(a.shape[0] for a in blocks), *blocks[0].shape[1:]), BF),
        in_specs=[VMEM] * len(blocks),
        out_specs=VMEM,
        cost_estimate=pl.CostEstimate(flops=rank, bytes_accessed=1000, transcendentals=0),
        name="pack",
    )(*blocks)


def seen_tokens(mask_ref, fork_ref, block):
    count = jnp.clip(fork_ref[0] + 1 - block * TOK, 0, TOK)
    return jnp.where(mask_ref[0, block] == 1, count, 0)


def attention_kernel(stage, together_heads, coord_ref, mask_ref, fork_ref, q_ref, *refs):
    segment, carried = stage == 2, stage > 0
    if segment:
        (cos_ref, sin_ref, gain_ref, own_ref), refs = refs[:4], refs[4:]
        backs, refs = refs[: NX - 1], refs[NX - 1 :]
    elif stage == 0:
        blocks, refs = [*(refs[0].at[n] for n in range(NY)), *refs[1 : NY + 1]], refs[NY + 1 :]
    else:
        blocks, refs = [refs[0].at[n] for n in range(2 * NY)], refs[1:]
    if carried:
        (acc_in, top_in, total_in), refs = refs[:3], refs[3:]
    if segment:
        out_ref, refs = refs[0], refs[1:]
    else:
        (acc_ref, top_ref, total_ref), refs = refs[:3], refs[3:]
    k_buf, v_buf = refs
    groups = k_buf.shape[0]
    heads = q_ref.shape[1] // HEAD
    per_group = heads // groups

    def lanes_of(h):
        return slice(h * HEAD, (h + 1) * HEAD)

    for g in range(groups):
        v_buf[g, :, HEAD:] = jnp.ones((k_buf.shape[1], HEAD), BF)
        if segment:
            k, v = own_ref[:, lanes_of(g)], own_ref[:, lanes_of(groups + g)]
            for ref in backs:
                high, low = ref[:, lanes_of(g)], ref[:, lanes_of(groups + g)]
                k = k + (high.astype(F32) + low.astype(F32))
                v = v + ref[:, lanes_of(2 * groups + g)].astype(F32)
            k = k * lax.rsqrt(jnp.mean(k * k, axis=1, keepdims=True) + EPS) * gain_ref[...]
            k = k * cos_ref[...] + pltpu.roll(k, HEAD // 2, 1) * sin_ref[...]
            k_buf[g] = k.astype(BF)
            v_buf[g, :, :HEAD] = v.astype(BF)
        else:
            for i, ref in enumerate(blocks):
                rows = slice(i * TOK, (i + 1) * TOK)
                k_buf[g, rows, :] = ref[0, :, lanes_of(g)]
                v_buf[g, rows, :HEAD] = ref[1, :, lanes_of(g)]
    if segment:
        row = lax.broadcasted_iota(jnp.int32, (TOK, TOK), 0)
        column = lax.broadcasted_iota(jnp.int32, (TOK, TOK), 1)
        bias = jnp.where(row >= column, 0.0, FLOOR)
        bias = jnp.concatenate([bias] * together_heads, axis=0)
    else:
        core, y, zh = coord_ref[CORE], coord_ref[Y], coord_ref[ZH]
        from_core = core if stage == 0 else 1 - core
        lane = lax.broadcasted_iota(jnp.int32, (1, TOK), 1)
        bias = []
        for side in (zh, 1 - zh):
            for away in ROUND_Y:
                block = lax.rem(y - away + NY, NY) * 4 + side * 2 + from_core
                bias.append(jnp.where(lane < seen_tokens(mask_ref, fork_ref, block), 0.0, FLOOR))
        bias = jnp.concatenate(bias, axis=1)
    units = [range(h, h + together_heads) for h in range(0, heads, together_heads)]

    def score(unit):
        q = jnp.concatenate([q_ref[:, lanes_of(h)] for h in unit], axis=0)
        return dot_nt(q, k_buf[unit[0] // per_group])

    ahead = score(units[0])
    for n, unit in enumerate(units):
        scores = ahead + bias
        if n + 1 < len(units):
            ahead = score(units[n + 1])
        top = jnp.max(scores, axis=1, keepdims=True)
        if carried:
            old = jnp.concatenate([top_in[:, lanes_of(h)] for h in unit], axis=0)
            wide = jnp.maximum(old, top)
            factor = jnp.exp2((old - wide) * EXP_SCALE)
            top = jnp.concatenate([wide] * (scores.shape[1] // HEAD), axis=1)
        else:
            wide = jnp.broadcast_to(top, (top.shape[0], HEAD))
        weights = jnp.exp2((scores - top) * EXP_SCALE).astype(BF)
        summed = jnp.dot(weights, v_buf[unit[0] // per_group], preferred_element_type=F32)
        for i, h in enumerate(unit):
            rows = slice(i * TOK, (i + 1) * TOK)
            value, total = summed[rows, :HEAD], summed[rows, HEAD:]
            if carried:
                value = value + acc_in[:, lanes_of(h)] * factor[rows]
                total = total + total_in[:, lanes_of(h)] * factor[rows]
            if segment:
                out_ref[:, lanes_of(h)] = (value / total).astype(BF)
            else:
                acc_ref[:, lanes_of(h)] = value
                top_ref[:, lanes_of(h)] = wide[rows]
                total_ref[:, lanes_of(h)] = total


def attention(stage, coords, mask, fork, queries, groups, operands):
    width = queries.shape[1]
    heads = width // HEAD
    length = TOK if stage == 2 else 2 * NY * TOK
    if stage == 2:
        out_shape = jax.ShapeDtypeStruct((TOK, width), BF)
    else:
        out_shape = (jax.ShapeDtypeStruct((TOK, width), F32),) * 3
    return pl.pallas_call(
        functools.partial(attention_kernel, stage, 4 if stage == 2 else 2),
        out_shape=out_shape,
        in_specs=[SMEM] * 3 + [VMEM] * (1 + len(operands)),
        out_specs=VMEM if stage == 2 else (VMEM,) * 3,
        scratch_shapes=[
            pltpu.VMEM((groups, length, HEAD), BF),
            pltpu.VMEM((groups, length, 2 * HEAD), BF),
        ],
        compiler_params=pltpu.CompilerParams(vmem_limit_bytes=VMEM_LIMIT),
        cost_estimate=pl.CostEstimate(flops=10**9, bytes_accessed=1000, transcendentals=0),
        name=("own_blocks", "other_blocks", "segment_block")[stage],
    )(coords, mask, fork, queries, *operands)


def on_device(
    hidden,
    queries,
    key_value_weight,
    k_gain,
    cached_ancestor_keys,
    cached_ancestor_values,
    ancestor_mask,
    fork_offset,
):
    dp, leaf = lax.axis_index("dp"), lax.axis_index("leaf")
    coords = jnp.stack([leaf % 2, leaf // 4, (leaf // 2) % 2, dp // NZL, dp % NZL]).astype(jnp.int32)
    groups = cached_ancestor_keys.shape[3] // HEAD
    keys, values = cached_ancestor_keys[0, 0], cached_ancestor_values[0, 0]
    load = pick_load(coords, key_value_weight, keys, values)
    unit, *sent = pick_parts(coords, load, hidden[0], (1,))

    block_start = jnp.arange(ancestor_mask.shape[1], dtype=jnp.int32) * TOK
    seen = jnp.clip(fork_offset[:, None] + 1 - block_start[None, :], 0, TOK)
    start = jnp.sum(jnp.where(ancestor_mask == 1, seen, 0))
    positions = (start + jnp.arange(TOK, dtype=jnp.int32)).astype(F32)
    freq = THETA ** (-jnp.arange(HEAD // 2, dtype=F32) * 2.0 / HEAD)
    angle = positions[:, None] * freq
    cosine, sine = jnp.cos(angle), jnp.sin(angle)
    cosine = jnp.concatenate([cosine, cosine], axis=-1)
    sine = jnp.concatenate([-sine, sine], axis=-1)

    def direct(a, **by):
        return move(a, ways=(1, 1), **by)

    def to_y_peers(a):
        return [direct(a, y=n) for n in ROUND_Y[1:]]

    shard = key_value_weight.shape[0]
    got = move(load, z=4)
    fours = jnp.concatenate([load[:shard], got[:shard]], axis=0)
    fours, far, part_one, *near = together(
        fours, got[shard:].reshape(unit.shape), direct(sent[0], x=1), *to_y_peers(unit)
    )
    _, *sent = pick_parts(coords, got, hidden[0], (2, 3))
    far, two, part_two, part_three, cosine, sine = together(
        move(far, z=4), move(fours, z=2), direct(sent[0], x=2), direct(sent[1], x=3), cosine, sine
    )
    first = jnp.concatenate([fours, two], axis=0)
    second, other_first = together(move(first, z=1), swap_cores(first))
    other_second = swap_cores(second)
    peers = [part_one, part_two, part_three]
    partial, *backs = project(coords, hidden[0], peers, [first, second, other_first, other_second])
    backs = [direct(backs[n - 1], x=-n) for n in (2, 3, 1)]
    near = pack([unit, *near], 10**13)
    far = [far, *to_y_peers(far)]
    other = swap_cores(pack([near, *far], 10**6)).reshape(2 * NY, *unit.shape)
    blocks = [near.reshape(NY, *unit.shape), *far]

    given = (coords, ancestor_mask, fork_offset, queries[0], groups)
    state = attention(0, *given, blocks)
    state = attention(1, *given, [other, *state])
    result = attention(2, *given, [cosine, sine, k_gain[None, :], partial, *backs, *state])
    return result[None]


def solution(mesh):
    in_specs = (
        P(("dp", "leaf"), None, None),
        P(("dp", "leaf"), None, None),
        P("dp", None),
        P(),
        P("dp", "leaf", None, None),
        P("dp", "leaf", None, None),
        P(("dp", "leaf"), None),
        P(("dp", "leaf")),
    )
    out_specs = P(("dp", "leaf"), None, None)
    return jax.shard_map(
        on_device, mesh=mesh, in_specs=in_specs, out_specs=out_specs, check_vma=False
    )
```

time: 478 us -> 135 us (0.28); the launches traced: 472 us -> 134 us
  waiting for transfers between devices: 219 us -> 22.7 us
  matrix products: 107 us -> 0 us
  starting transfers between devices: 0.08 us -> 67.9 us
  other arithmetic: 66.4 us -> 1.74 us
  local copies, waits for them, and re-layouts: 65.6 us -> 5.06 us
  Pallas kernels: 0 us -> 35.5 us
  between operations: 14 us -> 1.16 us
    all_gather x3 -> x0, waiting for transfers between devices: 217 us -> none  [the longest x1 89.3 us: on_device(): lax.all_gather(cached_ancestor_keys, 'leaf', axis=1, tiled=True)]
    dot_general x35 -> x0, matrix products: 107 us -> none  [the longest x17 61.1 us: absorb(): jnp.einsum(form, weights.astype(jnp.bfloat16), segment_values, preferred_...]
    ppermute x0 -> x19, starting transfers between devices: none -> 67.9 us  [the longest x16 61.7 us: move(): return lax.ppermute(a, AXES, pairs)]
    dynamic_slice x48 -> x0, local copies, waits for them, and re-layouts: 39.8 us -> none  [the longest x32 27.8 us: one_block(): lax.dynamic_index_in_dim(values_piece[0], index, 0, keepdims=False)]
    pallas_call x0 -> x9, Pallas kernels: none -> 35.5 us  [the longest x3 17.9 us: attention(): pl.pallas_call(functools.partial(attention_kernel, stage, 4 if stage == 2...]
    ppermute x0 -> x19, waiting for transfers between devices: none -> 22.7 us  [the longest x16 22.7 us: move(): return lax.ppermute(a, AXES, pairs)]
    mul x18 -> x0, other arithmetic: 21.7 us -> none  [the longest x17 21.5 us: absorb(): summed = summed * jnp.transpose(factor, (0, 3, 1, 2))[..., None] + update]
    add x16 -> x0, other arithmetic: 21 us -> none  [absorb(): total = total * factor + jnp.sum(weights, axis=-1)]
  transfers between devices with their start and end apart: 3 -> 19, of which waited for: 3 -> 7; matrix products, arithmetic and copies ran while one was open for 46% -> 2% of each run, Pallas kernels for 0% -> 22%
where the time goes in v1:
time: 135 us; the launch traced here: 134 us
  starting transfers between devices  67.9 us (50%)
  Pallas kernels  35.5 us (26%)
  waiting for transfers between devices  22.7 us (17%)
  local copies, waits for them, and re-layouts  5.06 us (4%)
  other arithmetic  1.74 us (1%)
    ppermute x16, starting transfers between devices, move(): return lax.ppermute(a, AXES, pairs)  61.7 us
    ppermute x16, waiting for transfers between devices, move(): return lax.ppermute(a, AXES, pairs)  22.7 us
    pallas_call x3, Pallas kernels, attention(): pl.pallas_call(functools.partial(attention_kernel, stage, 4 if stage == 2...  17.9 us
    ppermute x3, starting transfers between devices, swap_cores(): return lax.ppermute(a, AXES, pairs)  6.2 us
    pallas_call x1, Pallas kernels, project(): pl.pallas_call(project_kernel, out_shape=(jax.ShapeDtypeStruct((TOK, 2 *...  5.67 us
    pallas_call x2, Pallas kernels, pack(): pl.pallas_call(pack_kernel, out_shape=jax.ShapeDtypeStruct((sum((a.shape[...  5.22 us
    pallas_call x2, Pallas kernels, pick_parts(): pl.pallas_call(functools.partial(part_kernel, away), out_shape=(jax.Shape...  4.83 us
    unnamed x43, local copies, waits for them, and re-layouts  3.49 us
  transfers between devices with their start and end apart: 19, of which 7 were waited for; matrix products, arithmetic and copies ran while one was open for 2% of the time, Pallas kernels for 22%

profile of v1, /device:TPU:24, one launch (start us, length us, event | category | flops | bytes accessed | tf_op | source)
XLA Modules:
  0.0 134.0 jit_solution(9786702316470952528)
XLA Ops:
  2.5 9.1 %collective-permute-start = (bf16[416,512]{1,0:T(8,128)(2,1)}, bf16[416,512]{1,0:T(8,128)(2,1)S(1)}, u32[]{:S(2)}, u32[]{:S(2)}) collective-permute-start(bf16[416,512]{1,0:T(8,128)(2,1)} %pick_load.1.load_ref), channel_id=1, source_target_pairs={{0,64},{1,67},{4,68},{5,71},{8,72},{9,75},{12,76},{13,79},{16,80},... | collective-permute-start | bytes 1277960 | tf_op jit(solution)/shard_map/ppermute | solution.py:43
  13.9 3.1 %collective-permute-start.2 = (bf16[2,128,512]{2,1,0:T(8,128)(2,1)}, bf16[2,128,512]{2,1,0:T(8,128)(2,1)S(1)}, u32[]{:S(2)}, u32[]{:S(2)}) collective-permute-start(bf16[2,128,512]{2,1,0:T(8,128)(2,1)} %get-tuple-element.34.refs_0_), channel_id=1, source_target_pairs={{0,8},{1,9},{4,12},{5,13},{8,0},{9,1},{12,4},{13,5},{16,24},{17,25... | collective-permute-start | bytes 786440 | tf_op jit(solution)/shard_map/ppermute | solution.py:43
  17.0 4.1 %collective-permute-start.3 = (bf16[2,128,512]{2,1,0:T(8,128)(2,1)}, bf16[2,128,512]{2,1,0:T(8,128)(2,1)S(1)}, u32[]{:S(2)}, u32[]{:S(2)}) collective-permute-start(bf16[2,128,512]{2,1,0:T(8,128)(2,1)} %get-tuple-element.34.refs_0_), channel_id=1, source_target_pairs={{0,4},{1,5},{4,8},{5,9},{8,12},{9,13},{12,0},{13,1},{16,20},{17,21... | collective-permute-start | bytes 786440 | tf_op jit(solution)/shard_map/ppermute | solution.py:43
  23.1 3.4 %collective-permute-start.1 = (bf16[128,1280]{1,0:T(8,128)(2,1)}, bf16[128,1280]{1,0:T(8,128)(2,1)S(1)}, u32[]{:S(2)}, u32[]{:S(2)}) collective-permute-start(bf16[128,1280]{1,0:T(8,128)(2,1)} %get-tuple-element.33), channel_id=1, source_target_pairs={{0,128},{1,129},{4,132},{5,133},{8,136},{9,137},{12,140},{13,141},... | collective-permute-start | bytes 983048 | tf_op jit(solution)/shard_map/ppermute | solution.py:43
  29.5 2.4 %collective-permute-done.4.refs_3_ = bf16[2,128,512]{2,1,0:T(8,128)(2,1)S(1)} collective-permute-done((bf16[2,128,512]{2,1,0:T(8,128)(2,1)}, bf16[2,128,512]{2,1,0:T(8,128)(2,1)S(1)}, u32[]{:S(2)}, u32[]{:S(2)}) %collective-permute-start.4) | collective-permute-done | bytes 262176 | tf_op jit(solution)/shard_map/ppermute | solution.py:43
  31.9 3.3 %collective-permute-done.1.refs_0_ = bf16[128,1280]{1,0:T(8,128)(2,1)S(1)} collective-permute-done((bf16[128,1280]{1,0:T(8,128)(2,1)}, bf16[128,1280]{1,0:T(8,128)(2,1)S(1)}, u32[]{:S(2)}, u32[]{:S(2)}) %collective-permute-start.1) | collective-permute-done | bytes 327712 | tf_op jit(solution)/shard_map/ppermute | solution.py:43
  36.0 6.8 %collective-permute-start.6 = (bf16[320,512]{1,0:T(8,128)(2,1)S(1)}, bf16[320,512]{1,0:T(8,128)(2,1)S(1)}, u32[]{:S(2)}, u32[]{:S(2)}) collective-permute-start(bf16[320,512]{1,0:T(8,128)(2,1)S(1)} %pad_maximum_fusion), channel_id=1, source_target_pairs={{0,32},{1,99},{4,36},{5,103},{8,40},{9,107},{12,44},{13,111},{16,4... | collective-permute-start | bytes 983048 | tf_op jit(solution)/shard_map/ppermute | solution.py:43
  42.7 3.9 %collective-permute-start.5 = (bf16[2,128,512]{2,1,0:T(8,128)(2,1)S(1)}, bf16[2,128,512]{2,1,0:T(8,128)(2,1)}, u32[]{:S(2)}, u32[]{:S(2)}) collective-permute-start(bf16[2,128,512]{2,1,0:T(8,128)(2,1)S(1)} %bitcast.24), channel_id=1, source_target_pairs={{0,64},{1,67},{4,68},{5,71},{8,72},{9,75},{12,76},{13,79},{16,80},... | collective-permute-start | bytes 786440 | tf_op jit(solution)/shard_map/ppermute | solution.py:43
  46.7 2.5 %pick_parts.3 = (bf16[2,128,512]{2,1,0:T(8,128)(2,1)}, bf16[128,1280]{1,0:T(8,128)(2,1)}, bf16[128,1280]{1,0:T(8,128)(2,1)}) custom-call(s32[5]{0:T(128)} %stack.23.coord_ref, bf16[416,512]{1,0:T(8,128)(2,1)} %copy-done.17, bf16[128,5120]{1,0:T(8,128)(2,1)} %bitcast.22), custom_call_target="tpu_custom_call" | custom-call | flops 99999997952 | bytes 1000 | tf_op jit(solution)/shard_map/pick_parts/pallas_call | solution.py:104
  49.2 3.7 %collective-permute-start.7 = (bf16[128,1280]{1,0:T(8,128)(2,1)}, bf16[128,1280]{1,0:T(8,128)(2,1)S(1)}, u32[]{:S(2)}, u32[]{:S(2)}) collective-permute-start(bf16[128,1280]{1,0:T(8,128)(2,1)} %get-tuple-element.37), channel_id=1, source_target_pairs={{0,256},{1,257},{4,260},{5,261},{8,264},{9,265},{12,268},{13,269},... | collective-permute-start | bytes 983048 | tf_op jit(solution)/shard_map/ppermute | solution.py:43
  52.9 3.0 %collective-permute-start.8 = (bf16[128,1280]{1,0:T(8,128)(2,1)}, bf16[128,1280]{1,0:T(8,128)(2,1)S(1)}, u32[]{:S(2)}, u32[]{:S(2)}) collective-permute-start(bf16[128,1280]{1,0:T(8,128)(2,1)} %get-tuple-element.38), channel_id=1, source_target_pairs={{0,384},{1,385},{4,388},{5,389},{8,392},{9,393},{12,396},{13,397},... | collective-permute-start | bytes 983048 | tf_op jit(solution)/shard_map/ppermute | solution.py:43
  56.4 4.9 %collective-permute-done.5.refs_1_ = bf16[2,128,512]{2,1,0:T(8,128)(2,1)} collective-permute-done((bf16[2,128,512]{2,1,0:T(8,128)(2,1)S(1)}, bf16[2,128,512]{2,1,0:T(8,128)(2,1)}, u32[]{:S(2)}, u32[]{:S(2)}) %collective-permute-start.5) | collective-permute-done | bytes 262176 | tf_op jit(solution)/shard_map/ppermute | solution.py:43
  61.3 6.9 %collective-permute-done.8.refs_2_ = bf16[128,1280]{1,0:T(8,128)(2,1)S(1)} collective-permute-done((bf16[128,1280]{1,0:T(8,128)(2,1)}, bf16[128,1280]{1,0:T(8,128)(2,1)S(1)}, u32[]{:S(2)}, u32[]{:S(2)}) %collective-permute-start.8) | collective-permute-done | bytes 327712 | tf_op jit(solution)/shard_map/ppermute | solution.py:43
  73.3 3.1 %collective-permute-start.15 = (bf16[2,128,512]{2,1,0:T(8,128)(2,1)}, bf16[2,128,512]{2,1,0:T(8,128)(2,1)}, u32[]{:S(2)}, u32[]{:S(2)}) collective-permute-start(bf16[2,128,512]{2,1,0:T(8,128)(2,1)} %collective-permute-done.5.refs_1_), channel_id=1, source_target_pairs={{0,8},{1,9},{4,12},{5,13},{8,0},{9,1},{12,4},{13,5},{16,24},{17,25... | collective-permute-start | bytes 786440 | tf_op jit(solution)/shard_map/ppermute | solution.py:43
  76.4 4.1 %collective-permute-start.16 = (bf16[2,128,512]{2,1,0:T(8,128)(2,1)}, bf16[2,128,512]{2,1,0:T(8,128)(2,1)}, u32[]{:S(2)}, u32[]{:S(2)}) collective-permute-start(bf16[2,128,512]{2,1,0:T(8,128)(2,1)} %collective-permute-done.5.refs_1_), channel_id=1, source_target_pairs={{0,4},{1,5},{4,8},{5,9},{8,12},{9,13},{12,0},{13,1},{16,20},{17,21... | collective-permute-start | bytes 786440 | tf_op jit(solution)/shard_map/ppermute | solution.py:43
  89.8 3.2 %collective-permute-done.17.refs_4_ = bf16[2,128,512]{2,1,0:T(8,128)(2,1)} collective-permute-done((bf16[2,128,512]{2,1,0:T(8,128)(2,1)}, bf16[2,128,512]{2,1,0:T(8,128)(2,1)}, u32[]{:S(2)}, u32[]{:S(2)}) %collective-permute-start.17) | collective-permute-done | bytes 262176 | tf_op jit(solution)/shard_map/ppermute | solution.py:43
  93.1 3.0 %pack.3 = bf16[16,128,512]{2,1,0:T(8,128)(2,1)} custom-call(bf16[8,128,512]{2,1,0:T(8,128)(2,1)} %pack.2.refs_0_, bf16[2,128,512]{2,1,0:T(8,128)(2,1)} %collective-permute-done.5.refs_1_, bf16[2,128,512]{2,1,0:T(8,128)(2,1)} %collective-permute-done.15.refs_2_, bf16[2,128,512]{2,1,0:T(8,128)(2,1)} %collective-permute-done.16.refs_3_, ...), custom_call_target="tpu_custom_call" | custom-call | flops 1000000 | bytes 1000 | tf_op jit(solution)/shard_map/pack/pallas_call | solution.py:174
  99.2 5.7 %project.1 = (f32[128,1024]{1,0:T(8,128)S(1)}, bf16[128,1536]{1,0:T(8,128)(2,1)S(1)}, bf16[128,1536]{1,0:T(8,128)(2,1)S(1)}, bf16[128,1536]{1,0:T(8,128)(2,1)S(1)}) custom-call(s32[5]{0:T(128)S(1)} %copy-done.4, bf16[128,5120]{1,0:T(8,128)(2,1)S(1)} %bitcast.23, bf16[128,1280]{1,0:T(8,128)(2,1)S(1)} %copy-done.12, bf16[128,1280]{1,0:T(8,128)(2,1)S(1)} %copy-done.14, ...), custom_call_target="tpu_custom_call" | custom-call | flops 99999997952 | bytes 1000 | tf_op jit(solution)/shard_map/project/pallas_call | solution.py:150
  104.8 3.9 %collective-permute-start.12 = (bf16[128,1536]{1,0:T(8,128)(2,1)S(1)}, bf16[128,1536]{1,0:T(8,128)(2,1)S(1)}, u32[]{:S(2)}, u32[]{:S(2)}) collective-permute-start(bf16[128,1536]{1,0:T(8,128)(2,1)S(1)} %get-tuple-element.48), channel_id=1, source_target_pairs={{0,256},{1,257},{4,260},{5,261},{8,264},{9,265},{12,268},{13,269},... | collective-permute-start | bytes 1179656 | tf_op jit(solution)/shard_map/ppermute | solution.py:43
  108.8 3.4 %collective-permute-start.13 = (bf16[128,1536]{1,0:T(8,128)(2,1)S(1)}, bf16[128,1536]{1,0:T(8,128)(2,1)S(1)}, u32[]{:S(2)}, u32[]{:S(2)}) collective-permute-start(bf16[128,1536]{1,0:T(8,128)(2,1)S(1)} %get-tuple-element.49), channel_id=1, source_target_pairs={{0,128},{1,129},{4,132},{5,133},{8,136},{9,137},{12,140},{13,141},... | collective-permute-start | bytes 1179656 | tf_op jit(solution)/shard_map/ppermute | solution.py:43
  112.2 3.9 %collective-permute-start.14 = (bf16[128,1536]{1,0:T(8,128)(2,1)S(1)}, bf16[128,1536]{1,0:T(8,128)(2,1)S(1)}, u32[]{:S(2)}, u32[]{:S(2)}) collective-permute-start(bf16[128,1536]{1,0:T(8,128)(2,1)S(1)} %get-tuple-element.50), channel_id=1, source_target_pairs={{0,384},{1,385},{4,388},{5,389},{8,392},{9,393},{12,396},{13,397},... | collective-permute-start | bytes 1179656 | tf_op jit(solution)/shard_map/ppermute | solution.py:43
  116.1 7.1 %own_blocks.1 = (f32[128,4096]{1,0:T(8,128)S(1)}, f32[128,4096]{1,0:T(8,128)S(1)}, f32[128,4096]{1,0:T(8,128)S(1)}) custom-call(s32[5]{0:T(128)S(1)} %copy-done.4, s32[1,16]{1,0:T(1,128)S(1)} %copy-done.6, s32[1]{0:T(128)S(6)} %copy.10.fork_ref, bf16[128,4096]{1,0:T(8,128)(2,1)S(1)} %bitcast.15, bf16[4,2,128,512]{3,2,1,0:T(8,128)(2,1)S(1)} %bitcast.19, ...), custom_call_target="tpu_custom_call" | custom-call | flops 1000000000 | bytes 1000 | tf_op jit(solution)/shard_map/own_blocks/pallas_call | solution.py:287
  123.2 6.9 %other_blocks.1 = (f32[128,4096]{1,0:T(8,128)S(1)}, f32[128,4096]{1,0:T(8,128)S(1)}, f32[128,4096]{1,0:T(8,128)S(1)}) custom-call(s32[5]{0:T(128)S(1)} %copy-done.4, s32[1,16]{1,0:T(1,128)S(1)} %copy-done.6, s32[1]{0:T(128)S(6)} %copy.10.fork_ref, bf16[128,4096]{1,0:T(8,128)(2,1)S(1)} %bitcast.16, bf16[8,2,128,512]{3,2,1,0:T(8,128)(2,1)S(1)} %bitcast.18, ...), custom_call_target="tpu_custom_call" | custom-call | flops 1000000000 | bytes 1000 | tf_op jit(solution)/shard_map/other_blocks/pallas_call | solution.py:287
  130.1 4.0 %segment_block.1 = bf16[128,4096]{1,0:T(8,128)(2,1)} custom-call(s32[5]{0:T(128)S(1)} %copy-done.4, s32[1,16]{1,0:T(1,128)S(1)} %copy-done.6, s32[1]{0:T(128)S(6)} %copy.10.fork_ref, bf16[128,4096]{1,0:T(8,128)(2,1)S(1)} %bitcast.17, f32[128,128]{1,0:T(8,128)S(1)} %get-tuple-element.39.refs_0_, f32[128,128]{1,0:T(8,128)S(1)} %get-tuple-element.40.refs_1_, ...), custom_call_target="tpu_custom_call" | custom-call | flops 1000000000 | bytes 1000 | tf_op jit(solution)/shard_map/segment_block/pallas_call | solution.py:287
  (77 shorter events, 27.6 us)
Async XLA Ops:
  2.5 26.9 %collective-permute-start = (bf16[416,512]{1,0:T(8,128)(2,1)}, bf16[416,512]{1,0:T(8,128)(2,1)S(1)}, u32[]{:S(2)}, u32[]{:S(2)}) collective-permute-start(bf16[416,512]{1,0:T(8,128)(2,1)} %pick_load.1.load_ref), channel_id=1, source_target_pairs={{0,64},{1,67},{4,68},{5,71},{8,72},{9,75},{12,76},{13,79},{16,80},... | collective-permute-start | bytes 1277960 | tf_op jit(solution)/shard_map/ppermute | solution.py:43
  13.9 15.6 %collective-permute-start.2 = (bf16[2,128,512]{2,1,0:T(8,128)(2,1)}, bf16[2,128,512]{2,1,0:T(8,128)(2,1)S(1)}, u32[]{:S(2)}, u32[]{:S(2)}) collective-permute-start(bf16[2,128,512]{2,1,0:T(8,128)(2,1)} %get-tuple-element.34.refs_0_), channel_id=1, source_target_pairs={{0,8},{1,9},{4,12},{5,13},{8,0},{9,1},{12,4},{13,5},{16,24},{17,25... | collective-permute-start | bytes 786440 | tf_op jit(solution)/shard_map/ppermute | solution.py:43
  17.0 12.5 %collective-permute-start.3 = (bf16[2,128,512]{2,1,0:T(8,128)(2,1)}, bf16[2,128,512]{2,1,0:T(8,128)(2,1)S(1)}, u32[]{:S(2)}, u32[]{:S(2)}) collective-permute-start(bf16[2,128,512]{2,1,0:T(8,128)(2,1)} %get-tuple-element.34.refs_0_), channel_id=1, source_target_pairs={{0,4},{1,5},{4,8},{5,9},{8,12},{9,13},{12,0},{13,1},{16,20},{17,21... | collective-permute-start | bytes 786440 | tf_op jit(solution)/shard_map/ppermute | solution.py:43
  21.1 10.8 %collective-permute-start.4 = (bf16[2,128,512]{2,1,0:T(8,128)(2,1)}, bf16[2,128,512]{2,1,0:T(8,128)(2,1)S(1)}, u32[]{:S(2)}, u32[]{:S(2)}) collective-permute-start(bf16[2,128,512]{2,1,0:T(8,128)(2,1)} %get-tuple-element.34.refs_0_), channel_id=1, source_target_pairs={{0,12},{1,13},{4,0},{5,1},{8,4},{9,5},{12,8},{13,9},{16,28},{17,29... | collective-permute-start | bytes 786440 | tf_op jit(solution)/shard_map/ppermute | solution.py:43
  23.1 12.2 %collective-permute-start.1 = (bf16[128,1280]{1,0:T(8,128)(2,1)}, bf16[128,1280]{1,0:T(8,128)(2,1)S(1)}, u32[]{:S(2)}, u32[]{:S(2)}) collective-permute-start(bf16[128,1280]{1,0:T(8,128)(2,1)} %get-tuple-element.33), channel_id=1, source_target_pairs={{0,128},{1,129},{4,132},{5,133},{8,136},{9,137},{12,140},{13,141},... | collective-permute-start | bytes 983048 | tf_op jit(solution)/shard_map/ppermute | solution.py:43
  29.5 19.7 %copy-start.18 = (bf16[2,128,512]{2,1,0:T(8,128)(2,1)}, bf16[2,128,512]{2,1,0:T(8,128)(2,1)S(1)}, u32[]{:S(2)}) copy-start(bf16[2,128,512]{2,1,0:T(8,128)(2,1)S(1)} %collective-permute-done.2.refs_1_) | copy-start | bytes 786436
  36.0 25.3 %collective-permute-start.6 = (bf16[320,512]{1,0:T(8,128)(2,1)S(1)}, bf16[320,512]{1,0:T(8,128)(2,1)S(1)}, u32[]{:S(2)}, u32[]{:S(2)}) collective-permute-start(bf16[320,512]{1,0:T(8,128)(2,1)S(1)} %pad_maximum_fusion), channel_id=1, source_target_pairs={{0,32},{1,99},{4,36},{5,103},{8,40},{9,107},{12,44},{13,111},{16,4... | collective-permute-start | bytes 983048 | tf_op jit(solution)/shard_map/ppermute | solution.py:43
  42.7 18.5 %collective-permute-start.5 = (bf16[2,128,512]{2,1,0:T(8,128)(2,1)S(1)}, bf16[2,128,512]{2,1,0:T(8,128)(2,1)}, u32[]{:S(2)}, u32[]{:S(2)}) collective-permute-start(bf16[2,128,512]{2,1,0:T(8,128)(2,1)S(1)} %bitcast.24), channel_id=1, source_target_pairs={{0,64},{1,67},{4,68},{5,71},{8,72},{9,75},{12,76},{13,79},{16,80},... | collective-permute-start | bytes 786440 | tf_op jit(solution)/shard_map/ppermute | solution.py:43
  49.2 12.1 %collective-permute-start.7 = (bf16[128,1280]{1,0:T(8,128)(2,1)}, bf16[128,1280]{1,0:T(8,128)(2,1)S(1)}, u32[]{:S(2)}, u32[]{:S(2)}) collective-permute-start(bf16[128,1280]{1,0:T(8,128)(2,1)} %get-tuple-element.37), channel_id=1, source_target_pairs={{0,256},{1,257},{4,260},{5,261},{8,264},{9,265},{12,268},{13,269},... | collective-permute-start | bytes 983048 | tf_op jit(solution)/shard_map/ppermute | solution.py:43
  52.9 15.2 %collective-permute-start.8 = (bf16[128,1280]{1,0:T(8,128)(2,1)}, bf16[128,1280]{1,0:T(8,128)(2,1)S(1)}, u32[]{:S(2)}, u32[]{:S(2)}) collective-permute-start(bf16[128,1280]{1,0:T(8,128)(2,1)} %get-tuple-element.38), channel_id=1, source_target_pairs={{0,384},{1,385},{4,388},{5,389},{8,392},{9,393},{12,396},{13,397},... | collective-permute-start | bytes 983048 | tf_op jit(solution)/shard_map/ppermute | solution.py:43
  61.3 22.6 %copy-start.13 = (bf16[128,1280]{1,0:T(8,128)(2,1)}, bf16[128,1280]{1,0:T(8,128)(2,1)S(1)}, u32[]{:S(2)}) copy-start(bf16[128,1280]{1,0:T(8,128)(2,1)S(1)} %collective-permute-done.7.refs_1_) | copy-start | bytes 983044
  68.2 14.3 %collective-permute-start.10 = (bf16[640,512]{1,0:T(8,128)(2,1)S(1)}, bf16[640,512]{1,0:T(8,128)(2,1)S(1)}, u32[]{:S(2)}, u32[]{:S(2)}) collective-permute-start(bf16[640,512]{1,0:T(8,128)(2,1)S(1)} %constant_dynamic-update-slice_fusion.refs_3_), channel_id=1, source_target_pairs={{0,1},{1,0},{2,3},{3,2},{4,5},{5,4},{6,7},{7,6},{8,9},{9,8},{10,11... | collective-permute-start | bytes 1966088 | tf_op jit(solution)/shard_map/ppermute | solution.py:48
  70.1 13.8 %collective-permute-start.9 = (bf16[640,512]{1,0:T(8,128)(2,1)S(1)}, bf16[640,512]{1,0:T(8,128)(2,1)}, u32[]{:S(2)}, u32[]{:S(2)}) collective-permute-start(bf16[640,512]{1,0:T(8,128)(2,1)S(1)} %constant_dynamic-update-slice_fusion.refs_3_), channel_id=1, source_target_pairs={{0,16},{1,115},{4,20},{5,119},{8,24},{9,123},{12,28},{13,127},{16,... | collective-permute-start | bytes 1966088 | tf_op jit(solution)/shard_map/ppermute | solution.py:43
  73.3 15.1 %collective-permute-start.15 = (bf16[2,128,512]{2,1,0:T(8,128)(2,1)}, bf16[2,128,512]{2,1,0:T(8,128)(2,1)}, u32[]{:S(2)}, u32[]{:S(2)}) collective-permute-start(bf16[2,128,512]{2,1,0:T(8,128)(2,1)} %collective-permute-done.5.refs_1_), channel_id=1, source_target_pairs={{0,8},{1,9},{4,12},{5,13},{8,0},{9,1},{12,4},{13,5},{16,24},{17,25... | collective-permute-start | bytes 786440 | tf_op jit(solution)/shard_map/ppermute | solution.py:43
  76.4 13.4 %collective-permute-start.16 = (bf16[2,128,512]{2,1,0:T(8,128)(2,1)}, bf16[2,128,512]{2,1,0:T(8,128)(2,1)}, u32[]{:S(2)}, u32[]{:S(2)}) collective-permute-start(bf16[2,128,512]{2,1,0:T(8,128)(2,1)} %collective-permute-done.5.refs_1_), channel_id=1, source_target_pairs={{0,4},{1,5},{4,8},{5,9},{8,12},{9,13},{12,0},{13,1},{16,20},{17,21... | collective-permute-start | bytes 786440 | tf_op jit(solution)/shard_map/ppermute | solution.py:43
  80.5 12.5 %collective-permute-start.17 = (bf16[2,128,512]{2,1,0:T(8,128)(2,1)}, bf16[2,128,512]{2,1,0:T(8,128)(2,1)}, u32[]{:S(2)}, u32[]{:S(2)}) collective-permute-start(bf16[2,128,512]{2,1,0:T(8,128)(2,1)} %collective-permute-done.5.refs_1_), channel_id=1, source_target_pairs={{0,12},{1,13},{4,0},{5,1},{8,4},{9,5},{12,8},{13,9},{16,28},{17,29... | collective-permute-start | bytes 786440 | tf_op jit(solution)/shard_map/ppermute | solution.py:43
  83.9 14.2 %collective-permute-start.11 = (bf16[640,512]{1,0:T(8,128)(2,1)}, bf16[640,512]{1,0:T(8,128)(2,1)}, u32[]{:S(2)}, u32[]{:S(2)}) collective-permute-start(bf16[640,512]{1,0:T(8,128)(2,1)} %collective-permute-done.9.refs_4_), channel_id=1, source_target_pairs={{0,1},{1,0},{2,3},{3,2},{4,5},{5,4},{6,7},{7,6},{8,9},{9,8},{10,11... | collective-permute-start | bytes 1966088 | tf_op jit(solution)/shard_map/ppermute | solution.py:48
  96.1 20.0 %copy-start = (bf16[1,128,4096]{2,1,0:T(8,128)(2,1)S(1)}, bf16[1,128,4096]{2,1,0:T(8,128)(2,1)}, u32[]{:S(2)}) copy-start(bf16[1,128,4096]{2,1,0:T(8,128)(2,1)} %param.9) | copy-start | bytes 3145732
  96.1 20.0 %copy-start.1 = (bf16[8,128,512]{2,1,0:T(8,128)(2,1)S(1)}, bf16[8,128,512]{2,1,0:T(8,128)(2,1)}, u32[]{:S(2)}) copy-start(bf16[8,128,512]{2,1,0:T(8,128)(2,1)} %pack.2.refs_0_) | copy-start | bytes 3145732
  96.1 20.0 %copy-start.6 = (s32[1,16]{1,0:T(1,128)S(1)}, s32[1,16]{1,0:T(1,128)}, u32[]{:S(2)}) copy-start(s32[1,16]{1,0:T(1,128)} %mask_ref.5) | copy-start | bytes 196
  96.1 27.1 %collective-permute-start.18 = (bf16[16,128,512]{2,1,0:T(8,128)(2,1)}, bf16[16,128,512]{2,1,0:T(8,128)(2,1)S(1)}, u32[]{:S(2)}, u32[]{:S(2)}) collective-permute-start(bf16[16,128,512]{2,1,0:T(8,128)(2,1)} %pack.3), channel_id=1, source_target_pairs={{0,1},{1,0},{2,3},{3,2},{4,5},{5,4},{6,7},{7,6},{8,9},{9,8},{10,11... | collective-permute-start | bytes 6291464 | tf_op jit(solution)/shard_map/ppermute | solution.py:48
  104.8 25.2 %collective-permute-start.12 = (bf16[128,1536]{1,0:T(8,128)(2,1)S(1)}, bf16[128,1536]{1,0:T(8,128)(2,1)S(1)}, u32[]{:S(2)}, u32[]{:S(2)}) collective-permute-start(bf16[128,1536]{1,0:T(8,128)(2,1)S(1)} %get-tuple-element.48), channel_id=1, source_target_pairs={{0,256},{1,257},{4,260},{5,261},{8,264},{9,265},{12,268},{13,269},... | collective-permute-start | bytes 1179656 | tf_op jit(solution)/shard_map/ppermute | solution.py:43
  108.8 21.3 %collective-permute-start.13 = (bf16[128,1536]{1,0:T(8,128)(2,1)S(1)}, bf16[128,1536]{1,0:T(8,128)(2,1)S(1)}, u32[]{:S(2)}, u32[]{:S(2)}) collective-permute-start(bf16[128,1536]{1,0:T(8,128)(2,1)S(1)} %get-tuple-element.49), channel_id=1, source_target_pairs={{0,128},{1,129},{4,132},{5,133},{8,136},{9,137},{12,140},{13,141},... | collective-permute-start | bytes 1179656 | tf_op jit(solution)/shard_map/ppermute | solution.py:43
  112.2 17.9 %collective-permute-start.14 = (bf16[128,1536]{1,0:T(8,128)(2,1)S(1)}, bf16[128,1536]{1,0:T(8,128)(2,1)S(1)}, u32[]{:S(2)}, u32[]{:S(2)}) collective-permute-start(bf16[128,1536]{1,0:T(8,128)(2,1)S(1)} %get-tuple-element.50), channel_id=1, source_target_pairs={{0,384},{1,385},{4,388},{5,389},{8,392},{9,393},{12,396},{13,397},... | collective-permute-start | bytes 1179656 | tf_op jit(solution)/shard_map/ppermute | solution.py:43
  (16 other events, 154.6 us)

commit v2 on v1

--- a/solution.py
+++ b/solution.py
@@ -23,6 +23,7 @@
 SMEM = pl.BlockSpec(memory_space=pltpu.SMEM)
 HBM = pl.BlockSpec(memory_space=pltpu.HBM)
 VMEM_LIMIT = 36 * 2**20
+SMALL_LIMIT = 24 * 2**20
 CORE, Y, ZH, X, ZL = range(5)
 FIRST, SECOND = (0, 4, 2, 6), (1, 5, 3, 7)
 ROUND_Y = (0, 2, 1, 3)
@@ -157,7 +158,6 @@
             pltpu.VMEM((2, part, width), BF),
             pltpu.SemaphoreType.DMA((NX + 2 * NZL,)),
         ],
-        compiler_params=pltpu.CompilerParams(vmem_limit_bytes=VMEM_LIMIT),
         cost_estimate=pl.CostEstimate(flops=10**11, bytes_accessed=1000, transcendentals=0),
         name="project",
     )(coords, hidden, *peers, *bundles)
@@ -176,6 +176,7 @@
         out_shape=jax.ShapeDtypeStruct((sum(a.shape[0] for a in blocks), *blocks[0].shape[1:]), BF),
         in_specs=[VMEM] * len(blocks),
         out_specs=VMEM,
+        compiler_params=pltpu.CompilerParams(vmem_limit_bytes=SMALL_LIMIT),
         cost_estimate=pl.CostEstimate(flops=rank, bytes_accessed=1000, transcendentals=0),
         name="pack",
     )(*blocks)

time: 135 us -> 134 us (level)
  waiting for transfers between devices: 22.7 us -> 25.8 us
  Pallas kernels: 35.5 us -> 32.8 us
  local copies, waits for them, and re-layouts: 5.06 us -> 3.69 us
    ppermute x16, waiting for transfers between devices: 22.7 us -> 25.8 us  [move(): return lax.ppermute(a, AXES, pairs)]
    pallas_call x2, Pallas kernels: 5.22 us -> 2.76 us  [pack(): pl.pallas_call(pack_kernel, out_shape=jax.ShapeDtypeStruct((sum((a.shape[...]
    unnamed x43 -> x31, local copies, waits for them, and re-layouts: 3.49 us -> 2.04 us
  transfers between devices with their start and end apart: 19 -> 19, of which waited for: 7 -> 7; matrix products, arithmetic and copies ran while one was open for 2% -> 2% of each run, Pallas kernels for 22% -> 20%
where the time goes in v2:
time: 134 us; the launch traced here: 133 us
  starting transfers between devices  67.7 us (51%)
  Pallas kernels  32.8 us (24%)
  waiting for transfers between devices  25.8 us (19%)
  local copies, waits for them, and re-layouts  3.69 us (3%)
  other arithmetic  1.82 us (1%)
    ppermute x16, starting transfers between devices, move(): return lax.ppermute(a, AXES, pairs)  61.8 us
    ppermute x16, waiting for transfers between devices, move(): return lax.ppermute(a, AXES, pairs)  25.8 us
    pallas_call x3, Pallas kernels, attention(): pl.pallas_call(functools.partial(attention_kernel, stage, 4 if stage == 2...  17.8 us
    ppermute x3, starting transfers between devices, swap_cores(): return lax.ppermute(a, AXES, pairs)  5.9 us
    pallas_call x1, Pallas kernels, project(): pl.pallas_call(project_kernel, out_shape=(jax.ShapeDtypeStruct((TOK, 2 *...  5.57 us
    pallas_call x2, Pallas kernels, pick_parts(): pl.pallas_call(functools.partial(part_kernel, away), out_shape=(jax.Shape...  4.83 us
    pallas_call x2, Pallas kernels, pack(): pl.pallas_call(pack_kernel, out_shape=jax.ShapeDtypeStruct((sum((a.shape[...  2.76 us
  transfers between devices with their start and end apart: 19, of which 7 were waited for; matrix products, arithmetic and copies ran while one was open for 2% of the time, Pallas kernels for 20%

profile of v2, /device:TPU:24, one launch (start us, length us, event | category | flops | bytes accessed | tf_op | source)
XLA Modules:
  0.0 132.9 jit_solution(8431343881637754206)
XLA Ops:
  2.5 9.1 %collective-permute-start = (bf16[416,512]{1,0:T(8,128)(2,1)}, bf16[416,512]{1,0:T(8,128)(2,1)S(1)}, u32[]{:S(2)}, u32[]{:S(2)}) collective-permute-start(bf16[416,512]{1,0:T(8,128)(2,1)} %pick_load.1.load_ref), channel_id=1, source_target_pairs={{0,64},{1,67},{4,68},{5,71},{8,72},{9,75},{12,76},{13,79},{16,80},... | collective-permute-start | bytes 1277960 | tf_op jit(solution)/shard_map/ppermute | solution.py:44
  14.0 3.1 %collective-permute-start.2 = (bf16[2,128,512]{2,1,0:T(8,128)(2,1)}, bf16[2,128,512]{2,1,0:T(8,128)(2,1)S(1)}, u32[]{:S(2)}, u32[]{:S(2)}) collective-permute-start(bf16[2,128,512]{2,1,0:T(8,128)(2,1)} %get-tuple-element.34.refs_0_), channel_id=1, source_target_pairs={{0,8},{1,9},{4,12},{5,13},{8,0},{9,1},{12,4},{13,5},{16,24},{17,25... | collective-permute-start | bytes 786440 | tf_op jit(solution)/shard_map/ppermute | solution.py:44
  17.1 4.1 %collective-permute-start.3 = (bf16[2,128,512]{2,1,0:T(8,128)(2,1)}, bf16[2,128,512]{2,1,0:T(8,128)(2,1)S(1)}, u32[]{:S(2)}, u32[]{:S(2)}) collective-permute-start(bf16[2,128,512]{2,1,0:T(8,128)(2,1)} %get-tuple-element.34.refs_0_), channel_id=1, source_target_pairs={{0,4},{1,5},{4,8},{5,9},{8,12},{9,13},{12,0},{13,1},{16,20},{17,21... | collective-permute-start | bytes 786440 | tf_op jit(solution)/shard_map/ppermute | solution.py:44
  23.1 3.4 %collective-permute-start.1 = (bf16[128,1280]{1,0:T(8,128)(2,1)}, bf16[128,1280]{1,0:T(8,128)(2,1)S(1)}, u32[]{:S(2)}, u32[]{:S(2)}) collective-permute-start(bf16[128,1280]{1,0:T(8,128)(2,1)} %get-tuple-element.33), channel_id=1, source_target_pairs={{0,128},{1,129},{4,132},{5,133},{8,136},{9,137},{12,140},{13,141},... | collective-permute-start | bytes 983048 | tf_op jit(solution)/shard_map/ppermute | solution.py:44
  32.0 3.3 %collective-permute-done.1.refs_0_ = bf16[128,1280]{1,0:T(8,128)(2,1)S(1)} collective-permute-done((bf16[128,1280]{1,0:T(8,128)(2,1)}, bf16[128,1280]{1,0:T(8,128)(2,1)S(1)}, u32[]{:S(2)}, u32[]{:S(2)}) %collective-permute-start.1) | collective-permute-done | bytes 327712 | tf_op jit(solution)/shard_map/ppermute | solution.py:44
  36.0 6.9 %collective-permute-start.6 = (bf16[320,512]{1,0:T(8,128)(2,1)S(1)}, bf16[320,512]{1,0:T(8,128)(2,1)S(1)}, u32[]{:S(2)}, u32[]{:S(2)}) collective-permute-start(bf16[320,512]{1,0:T(8,128)(2,1)S(1)} %pad_maximum_fusion), channel_id=1, source_target_pairs={{0,32},{1,99},{4,36},{5,103},{8,40},{9,107},{12,44},{13,111},{16,4... | collective-permute-start | bytes 983048 | tf_op jit(solution)/shard_map/ppermute | solution.py:44
  42.9 3.9 %collective-permute-start.5 = (bf16[2,128,512]{2,1,0:T(8,128)(2,1)S(1)}, bf16[2,128,512]{2,1,0:T(8,128)(2,1)}, u32[]{:S(2)}, u32[]{:S(2)}) collective-permute-start(bf16[2,128,512]{2,1,0:T(8,128)(2,1)S(1)} %bitcast.21), channel_id=1, source_target_pairs={{0,64},{1,67},{4,68},{5,71},{8,72},{9,75},{12,76},{13,79},{16,80},... | collective-permute-start | bytes 786440 | tf_op jit(solution)/shard_map/ppermute | solution.py:44
  46.9 2.5 %pick_parts.3 = (bf16[2,128,512]{2,1,0:T(8,128)(2,1)}, bf16[128,1280]{1,0:T(8,128)(2,1)}, bf16[128,1280]{1,0:T(8,128)(2,1)}) custom-call(s32[5]{0:T(128)} %stack.23.coord_ref, bf16[416,512]{1,0:T(8,128)(2,1)} %copy-done.9, bf16[128,5120]{1,0:T(8,128)(2,1)} %bitcast.25), custom_call_target="tpu_custom_call" | custom-call | flops 99999997952 | bytes 1000 | tf_op jit(solution)/shard_map/pick_parts/pallas_call | solution.py:105
  49.4 3.7 %collective-permute-start.7 = (bf16[128,1280]{1,0:T(8,128)(2,1)}, bf16[128,1280]{1,0:T(8,128)(2,1)S(1)}, u32[]{:S(2)}, u32[]{:S(2)}) collective-permute-start(bf16[128,1280]{1,0:T(8,128)(2,1)} %get-tuple-element.37), channel_id=1, source_target_pairs={{0,256},{1,257},{4,260},{5,261},{8,264},{9,265},{12,268},{13,269},... | collective-permute-start | bytes 983048 | tf_op jit(solution)/shard_map/ppermute | solution.py:44
  53.1 3.0 %collective-permute-start.8 = (bf16[128,1280]{1,0:T(8,128)(2,1)}, bf16[128,1280]{1,0:T(8,128)(2,1)S(1)}, u32[]{:S(2)}, u32[]{:S(2)}) collective-permute-start(bf16[128,1280]{1,0:T(8,128)(2,1)} %get-tuple-element.38), channel_id=1, source_target_pairs={{0,384},{1,385},{4,388},{5,389},{8,392},{9,393},{12,396},{13,397},... | collective-permute-start | bytes 983048 | tf_op jit(solution)/shard_map/ppermute | solution.py:44
  56.6 4.9 %collective-permute-done.5.refs_1_ = bf16[2,128,512]{2,1,0:T(8,128)(2,1)} collective-permute-done((bf16[2,128,512]{2,1,0:T(8,128)(2,1)S(1)}, bf16[2,128,512]{2,1,0:T(8,128)(2,1)}, u32[]{:S(2)}, u32[]{:S(2)}) %collective-permute-start.5) | collective-permute-done | bytes 262176 | tf_op jit(solution)/shard_map/ppermute | solution.py:44
  61.5 6.7 %collective-permute-done.8.refs_2_ = bf16[128,1280]{1,0:T(8,128)(2,1)S(1)} collective-permute-done((bf16[128,1280]{1,0:T(8,128)(2,1)}, bf16[128,1280]{1,0:T(8,128)(2,1)S(1)}, u32[]{:S(2)}, u32[]{:S(2)}) %collective-permute-start.8) | collective-permute-done | bytes 327712 | tf_op jit(solution)/shard_map/ppermute | solution.py:44
  72.5 3.1 %collective-permute-start.15 = (bf16[2,128,512]{2,1,0:T(8,128)(2,1)}, bf16[2,128,512]{2,1,0:T(8,128)(2,1)}, u32[]{:S(2)}, u32[]{:S(2)}) collective-permute-start(bf16[2,128,512]{2,1,0:T(8,128)(2,1)} %collective-permute-done.5.refs_1_), channel_id=1, source_target_pairs={{0,8},{1,9},{4,12},{5,13},{8,0},{9,1},{12,4},{13,5},{16,24},{17,25... | collective-permute-start | bytes 786440 | tf_op jit(solution)/shard_map/ppermute | solution.py:44
  75.6 4.1 %collective-permute-start.16 = (bf16[2,128,512]{2,1,0:T(8,128)(2,1)}, bf16[2,128,512]{2,1,0:T(8,128)(2,1)}, u32[]{:S(2)}, u32[]{:S(2)}) collective-permute-start(bf16[2,128,512]{2,1,0:T(8,128)(2,1)} %collective-permute-done.5.refs_1_), channel_id=1, source_target_pairs={{0,4},{1,5},{4,8},{5,9},{8,12},{9,13},{12,0},{13,1},{16,20},{17,21... | collective-permute-start | bytes 786440 | tf_op jit(solution)/shard_map/ppermute | solution.py:44
  86.0 3.0 %collective-permute-done.16.refs_3_ = bf16[2,128,512]{2,1,0:T(8,128)(2,1)} collective-permute-done((bf16[2,128,512]{2,1,0:T(8,128)(2,1)}, bf16[2,128,512]{2,1,0:T(8,128)(2,1)}, u32[]{:S(2)}, u32[]{:S(2)}) %collective-permute-start.16) | collective-permute-done | bytes 262176 | tf_op jit(solution)/shard_map/ppermute | solution.py:44
  89.0 3.2 %collective-permute-done.17.refs_4_ = bf16[2,128,512]{2,1,0:T(8,128)(2,1)} collective-permute-done((bf16[2,128,512]{2,1,0:T(8,128)(2,1)}, bf16[2,128,512]{2,1,0:T(8,128)(2,1)}, u32[]{:S(2)}, u32[]{:S(2)}) %collective-permute-start.17) | collective-permute-done | bytes 262176 | tf_op jit(solution)/shard_map/ppermute | solution.py:44
  92.3 2.7 %pack.3 = bf16[16,128,512]{2,1,0:T(8,128)(2,1)} custom-call(bf16[8,128,512]{2,1,0:T(8,128)(2,1)S(1)} %pack.2.refs_0_, bf16[2,128,512]{2,1,0:T(8,128)(2,1)} %collective-permute-done.5.refs_1_, bf16[2,128,512]{2,1,0:T(8,128)(2,1)} %collective-permute-done.15.refs_2_, bf16[2,128,512]{2,1,0:T(8,128)(2,1)} %collective-permute-done.16.refs_3_, ...), custom_call_target="tpu_custom_call" | custom-call | flops 1000000 | bytes 1000 | tf_op jit(solution)/shard_map/pack/pallas_call | solution.py:174
  97.1 5.6 %project.1 = (f32[128,1024]{1,0:T(8,128)}, bf16[128,1536]{1,0:T(8,128)(2,1)}, bf16[128,1536]{1,0:T(8,128)(2,1)}, bf16[128,1536]{1,0:T(8,128)(2,1)}) custom-call(s32[5]{0:T(128)} %stack.23.coord_ref, bf16[128,5120]{1,0:T(8,128)(2,1)} %bitcast.26, bf16[128,1280]{1,0:T(8,128)(2,1)} %copy-done.12, bf16[128,1280]{1,0:T(8,128)(2,1)} %copy-done.13, ...), custom_call_target="tpu_custom_call" | custom-call | flops 99999997952 | bytes 1000 | tf_op jit(solution)/shard_map/project/pallas_call | solution.py:151
  102.6 3.9 %collective-permute-start.12 = (bf16[128,1536]{1,0:T(8,128)(2,1)}, bf16[128,1536]{1,0:T(8,128)(2,1)S(1)}, u32[]{:S(2)}, u32[]{:S(2)}) collective-permute-start(bf16[128,1536]{1,0:T(8,128)(2,1)} %get-tuple-element.48), channel_id=1, source_target_pairs={{0,256},{1,257},{4,260},{5,261},{8,264},{9,265},{12,268},{13,269},... | collective-permute-start | bytes 1179656 | tf_op jit(solution)/shard_map/ppermute | solution.py:44
  106.6 3.4 %collective-permute-start.13 = (bf16[128,1536]{1,0:T(8,128)(2,1)}, bf16[128,1536]{1,0:T(8,128)(2,1)S(1)}, u32[]{:S(2)}, u32[]{:S(2)}) collective-permute-start(bf16[128,1536]{1,0:T(8,128)(2,1)} %get-tuple-element.49), channel_id=1, source_target_pairs={{0,128},{1,129},{4,132},{5,133},{8,136},{9,137},{12,140},{13,141},... | collective-permute-start | bytes 1179656 | tf_op jit(solution)/shard_map/ppermute | solution.py:44
  110.0 3.9 %collective-permute-start.14 = (bf16[128,1536]{1,0:T(8,128)(2,1)}, bf16[128,1536]{1,0:T(8,128)(2,1)S(1)}, u32[]{:S(2)}, u32[]{:S(2)}) collective-permute-start(bf16[128,1536]{1,0:T(8,128)(2,1)} %get-tuple-element.50), channel_id=1, source_target_pairs={{0,384},{1,385},{4,388},{5,389},{8,392},{9,393},{12,396},{13,397},... | collective-permute-start | bytes 1179656 | tf_op jit(solution)/shard_map/ppermute | solution.py:44
  115.1 7.1 %own_blocks.1 = (f32[128,4096]{1,0:T(8,128)S(1)}, f32[128,4096]{1,0:T(8,128)S(1)}, f32[128,4096]{1,0:T(8,128)S(1)}) custom-call(s32[5]{0:T(128)S(1)} %copy-done.4, s32[1,16]{1,0:T(1,128)S(1)} %copy-done.6, s32[1]{0:T(128)S(6)} %copy.10.fork_ref, bf16[128,4096]{1,0:T(8,128)(2,1)S(1)} %bitcast.15, bf16[4,2,128,512]{3,2,1,0:T(8,128)(2,1)S(1)} %bitcast.19, ...), custom_call_target="tpu_custom_call" | custom-call | flops 1000000000 | bytes 1000 | tf_op jit(solution)/shard_map/own_blocks/pallas_call | solution.py:288
  122.2 6.7 %other_blocks.1 = (f32[128,4096]{1,0:T(8,128)S(1)}, f32[128,4096]{1,0:T(8,128)S(1)}, f32[128,4096]{1,0:T(8,128)S(1)}) custom-call(s32[5]{0:T(128)S(1)} %copy-done.4, s32[1,16]{1,0:T(1,128)S(1)} %copy-done.6, s32[1]{0:T(128)S(6)} %copy.10.fork_ref, bf16[128,4096]{1,0:T(8,128)(2,1)S(1)} %bitcast.16, bf16[8,2,128,512]{3,2,1,0:T(8,128)(2,1)S(1)} %bitcast.18, ...), custom_call_target="tpu_custom_call" | custom-call | flops 1000000000 | bytes 1000 | tf_op jit(solution)/shard_map/other_blocks/pallas_call | solution.py:288
  129.0 4.0 %segment_block.1 = bf16[128,4096]{1,0:T(8,128)(2,1)} custom-call(s32[5]{0:T(128)S(1)} %copy-done.4, s32[1,16]{1,0:T(1,128)S(1)} %copy-done.6, s32[1]{0:T(128)S(6)} %copy.10.fork_ref, bf16[128,4096]{1,0:T(8,128)(2,1)S(1)} %bitcast.17, f32[128,128]{1,0:T(8,128)S(1)} %get-tuple-element.39.refs_0_, f32[128,128]{1,0:T(8,128)S(1)} %get-tuple-element.40.refs_1_, ...), custom_call_target="tpu_custom_call" | custom-call | flops 1000000000 | bytes 1000 | tf_op jit(solution)/shard_map/segment_block/pallas_call | solution.py:288
  (65 shorter events, 26.5 us)
Async XLA Ops:
  2.5 27.0 %collective-permute-start = (bf16[416,512]{1,0:T(8,128)(2,1)}, bf16[416,512]{1,0:T(8,128)(2,1)S(1)}, u32[]{:S(2)}, u32[]{:S(2)}) collective-permute-start(bf16[416,512]{1,0:T(8,128)(2,1)} %pick_load.1.load_ref), channel_id=1, source_target_pairs={{0,64},{1,67},{4,68},{5,71},{8,72},{9,75},{12,76},{13,79},{16,80},... | collective-permute-start | bytes 1277960 | tf_op jit(solution)/shard_map/ppermute | solution.py:44
  14.0 15.7 %collective-permute-start.2 = (bf16[2,128,512]{2,1,0:T(8,128)(2,1)}, bf16[2,128,512]{2,1,0:T(8,128)(2,1)S(1)}, u32[]{:S(2)}, u32[]{:S(2)}) collective-permute-start(bf16[2,128,512]{2,1,0:T(8,128)(2,1)} %get-tuple-element.34.refs_0_), channel_id=1, source_target_pairs={{0,8},{1,9},{4,12},{5,13},{8,0},{9,1},{12,4},{13,5},{16,24},{17,25... | collective-permute-start | bytes 786440 | tf_op jit(solution)/shard_map/ppermute | solution.py:44
  17.1 12.5 %collective-permute-start.3 = (bf16[2,128,512]{2,1,0:T(8,128)(2,1)}, bf16[2,128,512]{2,1,0:T(8,128)(2,1)S(1)}, u32[]{:S(2)}, u32[]{:S(2)}) collective-permute-start(bf16[2,128,512]{2,1,0:T(8,128)(2,1)} %get-tuple-element.34.refs_0_), channel_id=1, source_target_pairs={{0,4},{1,5},{4,8},{5,9},{8,12},{9,13},{12,0},{13,1},{16,20},{17,21... | collective-permute-start | bytes 786440 | tf_op jit(solution)/shard_map/ppermute | solution.py:44
  21.2 10.8 %collective-permute-start.4 = (bf16[2,128,512]{2,1,0:T(8,128)(2,1)}, bf16[2,128,512]{2,1,0:T(8,128)(2,1)S(1)}, u32[]{:S(2)}, u32[]{:S(2)}) collective-permute-start(bf16[2,128,512]{2,1,0:T(8,128)(2,1)} %get-tuple-element.34.refs_0_), channel_id=1, source_target_pairs={{0,12},{1,13},{4,0},{5,1},{8,4},{9,5},{12,8},{13,9},{16,28},{17,29... | collective-permute-start | bytes 786440 | tf_op jit(solution)/shard_map/ppermute | solution.py:44
  23.1 12.2 %collective-permute-start.1 = (bf16[128,1280]{1,0:T(8,128)(2,1)}, bf16[128,1280]{1,0:T(8,128)(2,1)S(1)}, u32[]{:S(2)}, u32[]{:S(2)}) collective-permute-start(bf16[128,1280]{1,0:T(8,128)(2,1)} %get-tuple-element.33), channel_id=1, source_target_pairs={{0,128},{1,129},{4,132},{5,133},{8,136},{9,137},{12,140},{13,141},... | collective-permute-start | bytes 983048 | tf_op jit(solution)/shard_map/ppermute | solution.py:44
  36.0 49.9 %copy-start.8 = (bf16[2,128,512]{2,1,0:T(8,128)(2,1)S(1)}, bf16[2,128,512]{2,1,0:T(8,128)(2,1)}, u32[]{:S(2)}) copy-start(bf16[2,128,512]{2,1,0:T(8,128)(2,1)} %get-tuple-element.34.refs_0_) | copy-start | bytes 786436
  36.0 25.5 %collective-permute-start.6 = (bf16[320,512]{1,0:T(8,128)(2,1)S(1)}, bf16[320,512]{1,0:T(8,128)(2,1)S(1)}, u32[]{:S(2)}, u32[]{:S(2)}) collective-permute-start(bf16[320,512]{1,0:T(8,128)(2,1)S(1)} %pad_maximum_fusion), channel_id=1, source_target_pairs={{0,32},{1,99},{4,36},{5,103},{8,40},{9,107},{12,44},{13,111},{16,4... | collective-permute-start | bytes 983048 | tf_op jit(solution)/shard_map/ppermute | solution.py:44
  42.9 18.5 %collective-permute-start.5 = (bf16[2,128,512]{2,1,0:T(8,128)(2,1)S(1)}, bf16[2,128,512]{2,1,0:T(8,128)(2,1)}, u32[]{:S(2)}, u32[]{:S(2)}) collective-permute-start(bf16[2,128,512]{2,1,0:T(8,128)(2,1)S(1)} %bitcast.21), channel_id=1, source_target_pairs={{0,64},{1,67},{4,68},{5,71},{8,72},{9,75},{12,76},{13,79},{16,80},... | collective-permute-start | bytes 786440 | tf_op jit(solution)/shard_map/ppermute | solution.py:44
  49.4 12.1 %collective-permute-start.7 = (bf16[128,1280]{1,0:T(8,128)(2,1)}, bf16[128,1280]{1,0:T(8,128)(2,1)S(1)}, u32[]{:S(2)}, u32[]{:S(2)}) collective-permute-start(bf16[128,1280]{1,0:T(8,128)(2,1)} %get-tuple-element.37), channel_id=1, source_target_pairs={{0,256},{1,257},{4,260},{5,261},{8,264},{9,265},{12,268},{13,269},... | collective-permute-start | bytes 983048 | tf_op jit(solution)/shard_map/ppermute | solution.py:44
  53.1 15.1 %collective-permute-start.8 = (bf16[128,1280]{1,0:T(8,128)(2,1)}, bf16[128,1280]{1,0:T(8,128)(2,1)S(1)}, u32[]{:S(2)}, u32[]{:S(2)}) collective-permute-start(bf16[128,1280]{1,0:T(8,128)(2,1)} %get-tuple-element.38), channel_id=1, source_target_pairs={{0,384},{1,385},{4,388},{5,389},{8,392},{9,393},{12,396},{13,397},... | collective-permute-start | bytes 983048 | tf_op jit(solution)/shard_map/ppermute | solution.py:44
  61.5 22.5 %copy-start.13 = (bf16[128,1280]{1,0:T(8,128)(2,1)}, bf16[128,1280]{1,0:T(8,128)(2,1)S(1)}, u32[]{:S(2)}) copy-start(bf16[128,1280]{1,0:T(8,128)(2,1)S(1)} %collective-permute-done.7.refs_1_) | copy-start | bytes 983044
  68.2 13.4 %collective-permute-start.10 = (bf16[640,512]{1,0:T(8,128)(2,1)S(1)}, bf16[640,512]{1,0:T(8,128)(2,1)S(1)}, u32[]{:S(2)}, u32[]{:S(2)}) collective-permute-start(bf16[640,512]{1,0:T(8,128)(2,1)S(1)} %constant_dynamic-update-slice_fusion.refs_3_), channel_id=1, source_target_pairs={{0,1},{1,0},{2,3},{3,2},{4,5},{5,4},{6,7},{7,6},{8,9},{9,8},{10,11... | collective-permute-start | bytes 1966088 | tf_op jit(solution)/shard_map/ppermute | solution.py:49
  70.2 13.8 %collective-permute-start.9 = (bf16[640,512]{1,0:T(8,128)(2,1)S(1)}, bf16[640,512]{1,0:T(8,128)(2,1)}, u32[]{:S(2)}, u32[]{:S(2)}) collective-permute-start(bf16[640,512]{1,0:T(8,128)(2,1)S(1)} %constant_dynamic-update-slice_fusion.refs_3_), channel_id=1, source_target_pairs={{0,16},{1,115},{4,20},{5,119},{8,24},{9,123},{12,28},{13,127},{16,... | collective-permute-start | bytes 1966088 | tf_op jit(solution)/shard_map/ppermute | solution.py:44
  72.5 13.5 %collective-permute-start.15 = (bf16[2,128,512]{2,1,0:T(8,128)(2,1)}, bf16[2,128,512]{2,1,0:T(8,128)(2,1)}, u32[]{:S(2)}, u32[]{:S(2)}) collective-permute-start(bf16[2,128,512]{2,1,0:T(8,128)(2,1)} %collective-permute-done.5.refs_1_), channel_id=1, source_target_pairs={{0,8},{1,9},{4,12},{5,13},{8,0},{9,1},{12,4},{13,5},{16,24},{17,25... | collective-permute-start | bytes 786440 | tf_op jit(solution)/shard_map/ppermute | solution.py:44
  75.6 13.4 %collective-permute-start.16 = (bf16[2,128,512]{2,1,0:T(8,128)(2,1)}, bf16[2,128,512]{2,1,0:T(8,128)(2,1)}, u32[]{:S(2)}, u32[]{:S(2)}) collective-permute-start(bf16[2,128,512]{2,1,0:T(8,128)(2,1)} %collective-permute-done.5.refs_1_), channel_id=1, source_target_pairs={{0,4},{1,5},{4,8},{5,9},{8,12},{9,13},{12,0},{13,1},{16,20},{17,21... | collective-permute-start | bytes 786440 | tf_op jit(solution)/shard_map/ppermute | solution.py:44
  79.8 12.5 %collective-permute-start.17 = (bf16[2,128,512]{2,1,0:T(8,128)(2,1)}, bf16[2,128,512]{2,1,0:T(8,128)(2,1)}, u32[]{:S(2)}, u32[]{:S(2)}) collective-permute-start(bf16[2,128,512]{2,1,0:T(8,128)(2,1)} %collective-permute-done.5.refs_1_), channel_id=1, source_target_pairs={{0,12},{1,13},{4,0},{5,1},{8,4},{9,5},{12,8},{13,9},{16,28},{17,29... | collective-permute-start | bytes 786440 | tf_op jit(solution)/shard_map/ppermute | solution.py:44
  84.0 13.1 %collective-permute-start.11 = (bf16[640,512]{1,0:T(8,128)(2,1)}, bf16[640,512]{1,0:T(8,128)(2,1)}, u32[]{:S(2)}, u32[]{:S(2)}) collective-permute-start(bf16[640,512]{1,0:T(8,128)(2,1)} %collective-permute-done.9.refs_4_), channel_id=1, source_target_pairs={{0,1},{1,0},{2,3},{3,2},{4,5},{5,4},{6,7},{7,6},{8,9},{9,8},{10,11... | collective-permute-start | bytes 1966088 | tf_op jit(solution)/shard_map/ppermute | solution.py:49
  95.0 18.9 %copy-start = (bf16[1,128,4096]{2,1,0:T(8,128)(2,1)S(1)}, bf16[1,128,4096]{2,1,0:T(8,128)(2,1)}, u32[]{:S(2)}) copy-start(bf16[1,128,4096]{2,1,0:T(8,128)(2,1)} %param.9) | copy-start | bytes 3145732
  95.0 18.9 %copy-start.4 = (s32[5]{0:T(128)S(1)}, s32[5]{0:T(128)}, u32[]{:S(2)}) copy-start(s32[5]{0:T(128)} %stack.23.coord_ref) | copy-start | bytes 64
  95.0 18.9 %copy-start.6 = (s32[1,16]{1,0:T(1,128)S(1)}, s32[1,16]{1,0:T(1,128)}, u32[]{:S(2)}) copy-start(s32[1,16]{1,0:T(1,128)} %mask_ref.5) | copy-start | bytes 196
  95.0 27.2 %collective-permute-start.18 = (bf16[16,128,512]{2,1,0:T(8,128)(2,1)}, bf16[16,128,512]{2,1,0:T(8,128)(2,1)S(1)}, u32[]{:S(2)}, u32[]{:S(2)}) collective-permute-start(bf16[16,128,512]{2,1,0:T(8,128)(2,1)} %pack.3), channel_id=1, source_target_pairs={{0,1},{1,0},{2,3},{3,2},{4,5},{5,4},{6,7},{7,6},{8,9},{9,8},{10,11... | collective-permute-start | bytes 6291464 | tf_op jit(solution)/shard_map/ppermute | solution.py:49
  102.6 26.3 %collective-permute-start.12 = (bf16[128,1536]{1,0:T(8,128)(2,1)}, bf16[128,1536]{1,0:T(8,128)(2,1)S(1)}, u32[]{:S(2)}, u32[]{:S(2)}) collective-permute-start(bf16[128,1536]{1,0:T(8,128)(2,1)} %get-tuple-element.48), channel_id=1, source_target_pairs={{0,256},{1,257},{4,260},{5,261},{8,264},{9,265},{12,268},{13,269},... | collective-permute-start | bytes 1179656 | tf_op jit(solution)/shard_map/ppermute | solution.py:44
  106.6 22.3 %collective-permute-start.13 = (bf16[128,1536]{1,0:T(8,128)(2,1)}, bf16[128,1536]{1,0:T(8,128)(2,1)S(1)}, u32[]{:S(2)}, u32[]{:S(2)}) collective-permute-start(bf16[128,1536]{1,0:T(8,128)(2,1)} %get-tuple-element.49), channel_id=1, source_target_pairs={{0,128},{1,129},{4,132},{5,133},{8,136},{9,137},{12,140},{13,141},... | collective-permute-start | bytes 1179656 | tf_op jit(solution)/shard_map/ppermute | solution.py:44
  110.0 19.0 %collective-permute-start.14 = (bf16[128,1536]{1,0:T(8,128)(2,1)}, bf16[128,1536]{1,0:T(8,128)(2,1)S(1)}, u32[]{:S(2)}, u32[]{:S(2)}) collective-permute-start(bf16[128,1536]{1,0:T(8,128)(2,1)} %get-tuple-element.50), channel_id=1, source_target_pairs={{0,384},{1,385},{4,388},{5,389},{8,392},{9,393},{12,396},{13,397},... | collective-permute-start | bytes 1179656 | tf_op jit(solution)/shard_map/ppermute | solution.py:44
  (10 other events, 95.2 us)

commit v3 on v2

--- a/solution.py
+++ b/solution.py
@@ -315,7 +315,7 @@
     groups = cached_ancestor_keys.shape[3] // HEAD
     keys, values = cached_ancestor_keys[0, 0], cached_ancestor_values[0, 0]
     load = pick_load(coords, key_value_weight, keys, values)
-    unit, *sent = pick_parts(coords, load, hidden[0], (1,))
+    unit, *_ = pick_parts(coords, load, hidden[0], ())
 
     block_start = jnp.arange(ancestor_mask.shape[1], dtype=jnp.int32) * TOK
     seen = jnp.clip(fork_offset[:, None] + 1 - block_start[None, :], 0, TOK)
@@ -336,12 +336,10 @@
     shard = key_value_weight.shape[0]
     got = move(load, z=4)
     fours = jnp.concatenate([load[:shard], got[:shard]], axis=0)
-    fours, far, part_one, *near = together(
-        fours, got[shard:].reshape(unit.shape), direct(sent[0], x=1), *to_y_peers(unit)
-    )
-    _, *sent = pick_parts(coords, got, hidden[0], (2, 3))
-    far, two, part_two, part_three, cosine, sine = together(
-        move(far, z=4), move(fours, z=2), direct(sent[0], x=2), direct(sent[1], x=3), cosine, sine
+    fours, far, *near = together(fours, got[shard:].reshape(unit.shape), *to_y_peers(unit))
+    _, *sent = pick_parts(coords, got, hidden[0], (1, 2, 3))
+    far, two, part_two, part_one, part_three, cosine, sine = together(
+        move(far, z=4), move(fours, z=2), *(direct(sent[n - 1], x=n) for n in (2, 1, 3)), cosine, sine
     )
     first = jnp.concatenate([fours, two], axis=0)
     second, other_first = together(move(first, z=1), swap_cores(first))

time: 134 us -> 133 us (level)
  waiting for transfers between devices: 25.8 us -> 21.9 us
  starting transfers between devices: 67.7 us -> 71.5 us
    ppermute x16, waiting for transfers between devices: 25.8 us -> 21.9 us  [move(): return lax.ppermute(a, AXES, pairs)]
    ppermute x16, starting transfers between devices: 61.8 us -> 65.5 us  [move(): return lax.ppermute(a, AXES, pairs)]
where the time goes in v3:
time: 133 us; the launch traced here: 131 us
  starting transfers between devices  71.5 us (54%)
  Pallas kernels  31.9 us (24%)
  waiting for transfers between devices  21.9 us (16%)
  local copies, waits for them, and re-layouts  2.86 us (2%)
  other arithmetic  1.64 us (1%)
    ppermute x16, starting transfers between devices, move(): return lax.ppermute(a, AXES, pairs)  65.5 us
    ppermute x16, waiting for transfers between devices, move(): return lax.ppermute(a, AXES, pairs)  21.9 us
    pallas_call x3, Pallas kernels, attention(): pl.pallas_call(functools.partial(attention_kernel, stage, 4 if stage == 2...  16.9 us
    ppermute x3, starting transfers between devices, swap_cores(): return lax.ppermute(a, AXES, pairs)  6 us
    pallas_call x1, Pallas kernels, project(): pl.pallas_call(project_kernel, out_shape=(jax.ShapeDtypeStruct((TOK, 2 *...  5.58 us
    pallas_call x2, Pallas kernels, pick_parts(): pl.pallas_call(functools.partial(part_kernel, away), out_shape=(jax.Shape...  4.72 us
    pallas_call x2, Pallas kernels, pack(): pl.pallas_call(pack_kernel, out_shape=jax.ShapeDtypeStruct((sum((a.shape[...  2.75 us
  transfers between devices with their start and end apart: 19, of which 7 were waited for; matrix products, arithmetic and copies ran while one was open for 2% of the time, Pallas kernels for 20%

profile of v3, /device:TPU:24, one launch (start us, length us, event | category | flops | bytes accessed | tf_op | source)
XLA Modules:
  0.0 131.0 jit_solution(8432862299037866949)
XLA Ops:
  2.4 9.1 %collective-permute-start = (bf16[416,512]{1,0:T(8,128)(2,1)}, bf16[416,512]{1,0:T(8,128)(2,1)S(1)}, u32[]{:S(2)}, u32[]{:S(2)}) collective-permute-start(bf16[416,512]{1,0:T(8,128)(2,1)} %pick_load.1.load_ref), channel_id=1, source_target_pairs={{0,64},{1,67},{4,68},{5,71},{8,72},{9,75},{12,76},{13,79},{16,80},... | collective-permute-start | bytes 1277960 | tf_op jit(solution)/shard_map/ppermute | solution.py:44
  13.7 3.1 %collective-permute-start.1 = (bf16[2,128,512]{2,1,0:T(8,128)(2,1)}, bf16[2,128,512]{2,1,0:T(8,128)(2,1)S(1)}, u32[]{:S(2)}, u32[]{:S(2)}) collective-permute-start(bf16[2,128,512]{2,1,0:T(8,128)(2,1)} %pick_parts.2.refs_0_), channel_id=1, source_target_pairs={{0,8},{1,9},{4,12},{5,13},{8,0},{9,1},{12,4},{13,5},{16,24},{17,25... | collective-permute-start | bytes 786440 | tf_op jit(solution)/shard_map/ppermute | solution.py:44
  16.9 4.1 %collective-permute-start.2 = (bf16[2,128,512]{2,1,0:T(8,128)(2,1)}, bf16[2,128,512]{2,1,0:T(8,128)(2,1)S(1)}, u32[]{:S(2)}, u32[]{:S(2)}) collective-permute-start(bf16[2,128,512]{2,1,0:T(8,128)(2,1)} %pick_parts.2.refs_0_), channel_id=1, source_target_pairs={{0,4},{1,5},{4,8},{5,9},{8,12},{9,13},{12,0},{13,1},{16,20},{17,21... | collective-permute-start | bytes 786440 | tf_op jit(solution)/shard_map/ppermute | solution.py:44
  28.2 3.5 %collective-permute-done.3.refs_3_ = bf16[2,128,512]{2,1,0:T(8,128)(2,1)S(1)} collective-permute-done((bf16[2,128,512]{2,1,0:T(8,128)(2,1)}, bf16[2,128,512]{2,1,0:T(8,128)(2,1)S(1)}, u32[]{:S(2)}, u32[]{:S(2)}) %collective-permute-start.3) | collective-permute-done | bytes 262176 | tf_op jit(solution)/shard_map/ppermute | solution.py:44
  31.7 6.9 %collective-permute-start.5 = (bf16[320,512]{1,0:T(8,128)(2,1)S(1)}, bf16[320,512]{1,0:T(8,128)(2,1)S(1)}, u32[]{:S(2)}, u32[]{:S(2)}) collective-permute-start(bf16[320,512]{1,0:T(8,128)(2,1)S(1)} %pad_maximum_fusion), channel_id=1, source_target_pairs={{0,32},{1,99},{4,36},{5,103},{8,40},{9,107},{12,44},{13,111},{16,4... | collective-permute-start | bytes 983048 | tf_op jit(solution)/shard_map/ppermute | solution.py:44
  38.6 4.6 %collective-permute-start.4 = (bf16[2,128,512]{2,1,0:T(8,128)(2,1)S(1)}, bf16[2,128,512]{2,1,0:T(8,128)(2,1)}, u32[]{:S(2)}, u32[]{:S(2)}) collective-permute-start(bf16[2,128,512]{2,1,0:T(8,128)(2,1)S(1)} %bitcast.21), channel_id=1, source_target_pairs={{0,64},{1,67},{4,68},{5,71},{8,72},{9,75},{12,76},{13,79},{16,80},... | collective-permute-start | bytes 786440 | tf_op jit(solution)/shard_map/ppermute | solution.py:44
  43.3 2.5 %pick_parts.3 = (bf16[2,128,512]{2,1,0:T(8,128)(2,1)}, bf16[128,1280]{1,0:T(8,128)(2,1)}, bf16[128,1280]{1,0:T(8,128)(2,1)}, bf16[128,1280]{1,0:T(8,128)(2,1)}) custom-call(s32[5]{0:T(128)} %stack.23.coord_ref, bf16[416,512]{1,0:T(8,128)(2,1)} %copy-done.9, bf16[128,5120]{1,0:T(8,128)(2,1)} %bitcast.25), custom_call_target="tpu_custom_call" | custom-call | flops 99999997952 | bytes 1000 | tf_op jit(solution)/shard_map/pick_parts/pallas_call | solution.py:105
  45.8 4.9 %collective-permute-start.6 = (bf16[128,1280]{1,0:T(8,128)(2,1)}, bf16[128,1280]{1,0:T(8,128)(2,1)S(1)}, u32[]{:S(2)}, u32[]{:S(2)}) collective-permute-start(bf16[128,1280]{1,0:T(8,128)(2,1)} %get-tuple-element.34), channel_id=1, source_target_pairs={{0,256},{1,257},{4,260},{5,261},{8,264},{9,265},{12,268},{13,269},... | collective-permute-start | bytes 983048 | tf_op jit(solution)/shard_map/ppermute | solution.py:44
  53.2 4.6 %collective-permute-start.8 = (bf16[128,1280]{1,0:T(8,128)(2,1)}, bf16[128,1280]{1,0:T(8,128)(2,1)S(1)}, u32[]{:S(2)}, u32[]{:S(2)}) collective-permute-start(bf16[128,1280]{1,0:T(8,128)(2,1)} %get-tuple-element.36), channel_id=1, source_target_pairs={{0,384},{1,385},{4,388},{5,389},{8,392},{9,393},{12,396},{13,397},... | collective-permute-start | bytes 983048 | tf_op jit(solution)/shard_map/ppermute | solution.py:44
  58.3 3.5 %collective-permute-done.4.refs_1_ = bf16[2,128,512]{2,1,0:T(8,128)(2,1)} collective-permute-done((bf16[2,128,512]{2,1,0:T(8,128)(2,1)S(1)}, bf16[2,128,512]{2,1,0:T(8,128)(2,1)}, u32[]{:S(2)}, u32[]{:S(2)}) %collective-permute-start.4) | collective-permute-done | bytes 262176 | tf_op jit(solution)/shard_map/ppermute | solution.py:44
  61.7 5.3 %collective-permute-done.7.refs_0_ = bf16[128,1280]{1,0:T(8,128)(2,1)S(1)} collective-permute-done((bf16[128,1280]{1,0:T(8,128)(2,1)}, bf16[128,1280]{1,0:T(8,128)(2,1)S(1)}, u32[]{:S(2)}, u32[]{:S(2)}) %collective-permute-start.7) | collective-permute-done | bytes 327712 | tf_op jit(solution)/shard_map/ppermute | solution.py:44
  69.1 2.6 %collective-permute-start.9 = (bf16[640,512]{1,0:T(8,128)(2,1)S(1)}, bf16[640,512]{1,0:T(8,128)(2,1)}, u32[]{:S(2)}, u32[]{:S(2)}) collective-permute-start(bf16[640,512]{1,0:T(8,128)(2,1)S(1)} %constant_dynamic-update-slice_fusion.refs_3_), channel_id=1, source_target_pairs={{0,16},{1,115},{4,20},{5,119},{8,24},{9,123},{12,28},{13,127},{16,... | collective-permute-start | bytes 1966088 | tf_op jit(solution)/shard_map/ppermute | solution.py:44
  71.7 3.1 %collective-permute-start.15 = (bf16[2,128,512]{2,1,0:T(8,128)(2,1)}, bf16[2,128,512]{2,1,0:T(8,128)(2,1)}, u32[]{:S(2)}, u32[]{:S(2)}) collective-permute-start(bf16[2,128,512]{2,1,0:T(8,128)(2,1)} %collective-permute-done.4.refs_1_), channel_id=1, source_target_pairs={{0,8},{1,9},{4,12},{5,13},{8,0},{9,1},{12,4},{13,5},{16,24},{17,25... | collective-permute-start | bytes 786440 | tf_op jit(solution)/shard_map/ppermute | solution.py:44
  74.8 4.1 %collective-permute-start.16 = (bf16[2,128,512]{2,1,0:T(8,128)(2,1)}, bf16[2,128,512]{2,1,0:T(8,128)(2,1)}, u32[]{:S(2)}, u32[]{:S(2)}) collective-permute-start(bf16[2,128,512]{2,1,0:T(8,128)(2,1)} %collective-permute-done.4.refs_1_), channel_id=1, source_target_pairs={{0,4},{1,5},{4,8},{5,9},{8,12},{9,13},{12,0},{13,1},{16,20},{17,21... | collective-permute-start | bytes 786440 | tf_op jit(solution)/shard_map/ppermute | solution.py:44
  85.0 2.7 %collective-permute-done.16.refs_3_ = bf16[2,128,512]{2,1,0:T(8,128)(2,1)} collective-permute-done((bf16[2,128,512]{2,1,0:T(8,128)(2,1)}, bf16[2,128,512]{2,1,0:T(8,128)(2,1)}, u32[]{:S(2)}, u32[]{:S(2)}) %collective-permute-start.16) | collective-permute-done | bytes 262176 | tf_op jit(solution)/shard_map/ppermute | solution.py:44
  87.6 2.5 %collective-permute-done.17.refs_4_ = bf16[2,128,512]{2,1,0:T(8,128)(2,1)} collective-permute-done((bf16[2,128,512]{2,1,0:T(8,128)(2,1)}, bf16[2,128,512]{2,1,0:T(8,128)(2,1)}, u32[]{:S(2)}, u32[]{:S(2)}) %collective-permute-start.17) | collective-permute-done | bytes 262176 | tf_op jit(solution)/shard_map/ppermute | solution.py:44
  90.2 2.7 %pack.3 = bf16[16,128,512]{2,1,0:T(8,128)(2,1)} custom-call(bf16[8,128,512]{2,1,0:T(8,128)(2,1)S(1)} %pack.2.refs_0_, bf16[2,128,512]{2,1,0:T(8,128)(2,1)} %collective-permute-done.4.refs_1_, bf16[2,128,512]{2,1,0:T(8,128)(2,1)} %collective-permute-done.15.refs_2_, bf16[2,128,512]{2,1,0:T(8,128)(2,1)} %collective-permute-done.16.refs_3_, ...), custom_call_target="tpu_custom_call" | custom-call | flops 1000000 | bytes 1000 | tf_op jit(solution)/shard_map/pack/pallas_call | solution.py:174
  94.9 5.6 %project.1 = (f32[128,1024]{1,0:T(8,128)}, bf16[128,1536]{1,0:T(8,128)(2,1)}, bf16[128,1536]{1,0:T(8,128)(2,1)}, bf16[128,1536]{1,0:T(8,128)(2,1)}) custom-call(s32[5]{0:T(128)} %stack.23.coord_ref, bf16[128,5120]{1,0:T(8,128)(2,1)} %bitcast.26, bf16[128,1280]{1,0:T(8,128)(2,1)} %copy-done.13, bf16[128,1280]{1,0:T(8,128)(2,1)} %copy-done.12, ...), custom_call_target="tpu_custom_call" | custom-call | flops 99999997952 | bytes 1000 | tf_op jit(solution)/shard_map/project/pallas_call | solution.py:151
  100.5 4.9 %collective-permute-start.12 = (bf16[128,1536]{1,0:T(8,128)(2,1)}, bf16[128,1536]{1,0:T(8,128)(2,1)S(1)}, u32[]{:S(2)}, u32[]{:S(2)}) collective-permute-start(bf16[128,1536]{1,0:T(8,128)(2,1)} %get-tuple-element.46), channel_id=1, source_target_pairs={{0,256},{1,257},{4,260},{5,261},{8,264},{9,265},{12,268},{13,269},... | collective-permute-start | bytes 1179656 | tf_op jit(solution)/shard_map/ppermute | solution.py:44
  105.4 3.0 %collective-permute-start.13 = (bf16[128,1536]{1,0:T(8,128)(2,1)}, bf16[128,1536]{1,0:T(8,128)(2,1)S(1)}, u32[]{:S(2)}, u32[]{:S(2)}) collective-permute-start(bf16[128,1536]{1,0:T(8,128)(2,1)} %get-tuple-element.47), channel_id=1, source_target_pairs={{0,128},{1,129},{4,132},{5,133},{8,136},{9,137},{12,140},{13,141},... | collective-permute-start | bytes 1179656 | tf_op jit(solution)/shard_map/ppermute | solution.py:44
  108.4 4.3 %collective-permute-start.14 = (bf16[128,1536]{1,0:T(8,128)(2,1)}, bf16[128,1536]{1,0:T(8,128)(2,1)S(1)}, u32[]{:S(2)}, u32[]{:S(2)}) collective-permute-start(bf16[128,1536]{1,0:T(8,128)(2,1)} %get-tuple-element.48), channel_id=1, source_target_pairs={{0,384},{1,385},{4,388},{5,389},{8,392},{9,393},{12,396},{13,397},... | collective-permute-start | bytes 1179656 | tf_op jit(solution)/shard_map/ppermute | solution.py:44
  113.9 6.8 %own_blocks.1 = (f32[128,4096]{1,0:T(8,128)S(1)}, f32[128,4096]{1,0:T(8,128)S(1)}, f32[128,4096]{1,0:T(8,128)S(1)}) custom-call(s32[5]{0:T(128)S(1)} %copy-done.4, s32[1,16]{1,0:T(1,128)S(1)} %copy-done.6, s32[1]{0:T(128)S(6)} %copy.10.fork_ref, bf16[128,4096]{1,0:T(8,128)(2,1)S(1)} %bitcast.15, bf16[4,2,128,512]{3,2,1,0:T(8,128)(2,1)S(1)} %bitcast.19, ...), custom_call_target="tpu_custom_call" | custom-call | flops 1000000000 | bytes 1000 | tf_op jit(solution)/shard_map/own_blocks/pallas_call | solution.py:288
  120.7 6.3 %other_blocks.1 = (f32[128,4096]{1,0:T(8,128)S(1)}, f32[128,4096]{1,0:T(8,128)S(1)}, f32[128,4096]{1,0:T(8,128)S(1)}) custom-call(s32[5]{0:T(128)S(1)} %copy-done.4, s32[1,16]{1,0:T(1,128)S(1)} %copy-done.6, s32[1]{0:T(128)S(6)} %copy.10.fork_ref, bf16[128,4096]{1,0:T(8,128)(2,1)S(1)} %bitcast.16, bf16[8,2,128,512]{3,2,1,0:T(8,128)(2,1)S(1)} %bitcast.18, ...), custom_call_target="tpu_custom_call" | custom-call | flops 1000000000 | bytes 1000 | tf_op jit(solution)/shard_map/other_blocks/pallas_call | solution.py:288
  127.1 3.8 %segment_block.1 = bf16[128,4096]{1,0:T(8,128)(2,1)} custom-call(s32[5]{0:T(128)S(1)} %copy-done.4, s32[1,16]{1,0:T(1,128)S(1)} %copy-done.6, s32[1]{0:T(128)S(6)} %copy.10.fork_ref, bf16[128,4096]{1,0:T(8,128)(2,1)S(1)} %bitcast.17, f32[128,128]{1,0:T(8,128)S(1)} %get-tuple-element.37.refs_0_, f32[128,128]{1,0:T(8,128)S(1)} %get-tuple-element.38.refs_1_, ...), custom_call_target="tpu_custom_call" | custom-call | flops 1000000000 | bytes 1000 | tf_op jit(solution)/shard_map/segment_block/pallas_call | solution.py:288
  (65 shorter events, 25.4 us)
Async XLA Ops:
  2.4 23.3 %collective-permute-start = (bf16[416,512]{1,0:T(8,128)(2,1)}, bf16[416,512]{1,0:T(8,128)(2,1)S(1)}, u32[]{:S(2)}, u32[]{:S(2)}) collective-permute-start(bf16[416,512]{1,0:T(8,128)(2,1)} %pick_load.1.load_ref), channel_id=1, source_target_pairs={{0,64},{1,67},{4,68},{5,71},{8,72},{9,75},{12,76},{13,79},{16,80},... | collective-permute-start | bytes 1277960 | tf_op jit(solution)/shard_map/ppermute | solution.py:44
  13.7 12.1 %collective-permute-start.1 = (bf16[2,128,512]{2,1,0:T(8,128)(2,1)}, bf16[2,128,512]{2,1,0:T(8,128)(2,1)S(1)}, u32[]{:S(2)}, u32[]{:S(2)}) collective-permute-start(bf16[2,128,512]{2,1,0:T(8,128)(2,1)} %pick_parts.2.refs_0_), channel_id=1, source_target_pairs={{0,8},{1,9},{4,12},{5,13},{8,0},{9,1},{12,4},{13,5},{16,24},{17,25... | collective-permute-start | bytes 786440 | tf_op jit(solution)/shard_map/ppermute | solution.py:44
  16.9 11.3 %collective-permute-start.2 = (bf16[2,128,512]{2,1,0:T(8,128)(2,1)}, bf16[2,128,512]{2,1,0:T(8,128)(2,1)S(1)}, u32[]{:S(2)}, u32[]{:S(2)}) collective-permute-start(bf16[2,128,512]{2,1,0:T(8,128)(2,1)} %pick_parts.2.refs_0_), channel_id=1, source_target_pairs={{0,4},{1,5},{4,8},{5,9},{8,12},{9,13},{12,0},{13,1},{16,20},{17,21... | collective-permute-start | bytes 786440 | tf_op jit(solution)/shard_map/ppermute | solution.py:44
  21.0 10.8 %collective-permute-start.3 = (bf16[2,128,512]{2,1,0:T(8,128)(2,1)}, bf16[2,128,512]{2,1,0:T(8,128)(2,1)S(1)}, u32[]{:S(2)}, u32[]{:S(2)}) collective-permute-start(bf16[2,128,512]{2,1,0:T(8,128)(2,1)} %pick_parts.2.refs_0_), channel_id=1, source_target_pairs={{0,12},{1,13},{4,0},{5,1},{8,4},{9,5},{12,8},{13,9},{16,28},{17,29... | collective-permute-start | bytes 786440 | tf_op jit(solution)/shard_map/ppermute | solution.py:44
  31.7 53.1 %copy-start.8 = (bf16[2,128,512]{2,1,0:T(8,128)(2,1)S(1)}, bf16[2,128,512]{2,1,0:T(8,128)(2,1)}, u32[]{:S(2)}) copy-start(bf16[2,128,512]{2,1,0:T(8,128)(2,1)} %pick_parts.2.refs_0_) | copy-start | bytes 786436
  31.7 30.0 %collective-permute-start.5 = (bf16[320,512]{1,0:T(8,128)(2,1)S(1)}, bf16[320,512]{1,0:T(8,128)(2,1)S(1)}, u32[]{:S(2)}, u32[]{:S(2)}) collective-permute-start(bf16[320,512]{1,0:T(8,128)(2,1)S(1)} %pad_maximum_fusion), channel_id=1, source_target_pairs={{0,32},{1,99},{4,36},{5,103},{8,40},{9,107},{12,44},{13,111},{16,4... | collective-permute-start | bytes 983048 | tf_op jit(solution)/shard_map/ppermute | solution.py:44
  38.6 23.1 %collective-permute-start.4 = (bf16[2,128,512]{2,1,0:T(8,128)(2,1)S(1)}, bf16[2,128,512]{2,1,0:T(8,128)(2,1)}, u32[]{:S(2)}, u32[]{:S(2)}) collective-permute-start(bf16[2,128,512]{2,1,0:T(8,128)(2,1)S(1)} %bitcast.21), channel_id=1, source_target_pairs={{0,64},{1,67},{4,68},{5,71},{8,72},{9,75},{12,76},{13,79},{16,80},... | collective-permute-start | bytes 786440 | tf_op jit(solution)/shard_map/ppermute | solution.py:44
  45.8 15.9 %collective-permute-start.6 = (bf16[128,1280]{1,0:T(8,128)(2,1)}, bf16[128,1280]{1,0:T(8,128)(2,1)S(1)}, u32[]{:S(2)}, u32[]{:S(2)}) collective-permute-start(bf16[128,1280]{1,0:T(8,128)(2,1)} %get-tuple-element.34), channel_id=1, source_target_pairs={{0,256},{1,257},{4,260},{5,261},{8,264},{9,265},{12,268},{13,269},... | collective-permute-start | bytes 983048 | tf_op jit(solution)/shard_map/ppermute | solution.py:44
  50.7 16.3 %collective-permute-start.7 = (bf16[128,1280]{1,0:T(8,128)(2,1)}, bf16[128,1280]{1,0:T(8,128)(2,1)S(1)}, u32[]{:S(2)}, u32[]{:S(2)}) collective-permute-start(bf16[128,1280]{1,0:T(8,128)(2,1)} %get-tuple-element.35), channel_id=1, source_target_pairs={{0,128},{1,129},{4,132},{5,133},{8,136},{9,137},{12,140},{13,141},... | collective-permute-start | bytes 983048 | tf_op jit(solution)/shard_map/ppermute | solution.py:44
  53.2 13.8 %collective-permute-start.8 = (bf16[128,1280]{1,0:T(8,128)(2,1)}, bf16[128,1280]{1,0:T(8,128)(2,1)S(1)}, u32[]{:S(2)}, u32[]{:S(2)}) collective-permute-start(bf16[128,1280]{1,0:T(8,128)(2,1)} %get-tuple-element.36), channel_id=1, source_target_pairs={{0,384},{1,385},{4,388},{5,389},{8,392},{9,393},{12,396},{13,397},... | collective-permute-start | bytes 983048 | tf_op jit(solution)/shard_map/ppermute | solution.py:44
  61.7 21.2 %copy-start.12 = (bf16[128,1280]{1,0:T(8,128)(2,1)}, bf16[128,1280]{1,0:T(8,128)(2,1)S(1)}, u32[]{:S(2)}) copy-start(bf16[128,1280]{1,0:T(8,128)(2,1)S(1)} %collective-permute-done.6.refs_1_) | copy-start | bytes 983044
  67.1 13.8 %collective-permute-start.10 = (bf16[640,512]{1,0:T(8,128)(2,1)S(1)}, bf16[640,512]{1,0:T(8,128)(2,1)S(1)}, u32[]{:S(2)}, u32[]{:S(2)}) collective-permute-start(bf16[640,512]{1,0:T(8,128)(2,1)S(1)} %constant_dynamic-update-slice_fusion.refs_3_), channel_id=1, source_target_pairs={{0,1},{1,0},{2,3},{3,2},{4,5},{5,4},{6,7},{7,6},{8,9},{9,8},{10,11... | collective-permute-start | bytes 1966088 | tf_op jit(solution)/shard_map/ppermute | solution.py:49
  69.1 13.8 %collective-permute-start.9 = (bf16[640,512]{1,0:T(8,128)(2,1)S(1)}, bf16[640,512]{1,0:T(8,128)(2,1)}, u32[]{:S(2)}, u32[]{:S(2)}) collective-permute-start(bf16[640,512]{1,0:T(8,128)(2,1)S(1)} %constant_dynamic-update-slice_fusion.refs_3_), channel_id=1, source_target_pairs={{0,16},{1,115},{4,20},{5,119},{8,24},{9,123},{12,28},{13,127},{16,... | collective-permute-start | bytes 1966088 | tf_op jit(solution)/shard_map/ppermute | solution.py:44
  71.7 13.3 %collective-permute-start.15 = (bf16[2,128,512]{2,1,0:T(8,128)(2,1)}, bf16[2,128,512]{2,1,0:T(8,128)(2,1)}, u32[]{:S(2)}, u32[]{:S(2)}) collective-permute-start(bf16[2,128,512]{2,1,0:T(8,128)(2,1)} %collective-permute-done.4.refs_1_), channel_id=1, source_target_pairs={{0,8},{1,9},{4,12},{5,13},{8,0},{9,1},{12,4},{13,5},{16,24},{17,25... | collective-permute-start | bytes 786440 | tf_op jit(solution)/shard_map/ppermute | solution.py:44
  74.8 12.8 %collective-permute-start.16 = (bf16[2,128,512]{2,1,0:T(8,128)(2,1)}, bf16[2,128,512]{2,1,0:T(8,128)(2,1)}, u32[]{:S(2)}, u32[]{:S(2)}) collective-permute-start(bf16[2,128,512]{2,1,0:T(8,128)(2,1)} %collective-permute-done.4.refs_1_), channel_id=1, source_target_pairs={{0,4},{1,5},{4,8},{5,9},{8,12},{9,13},{12,0},{13,1},{16,20},{17,21... | collective-permute-start | bytes 786440 | tf_op jit(solution)/shard_map/ppermute | solution.py:44
  78.9 11.3 %collective-permute-start.17 = (bf16[2,128,512]{2,1,0:T(8,128)(2,1)}, bf16[2,128,512]{2,1,0:T(8,128)(2,1)}, u32[]{:S(2)}, u32[]{:S(2)}) collective-permute-start(bf16[2,128,512]{2,1,0:T(8,128)(2,1)} %collective-permute-done.4.refs_1_), channel_id=1, source_target_pairs={{0,12},{1,13},{4,0},{5,1},{8,4},{9,5},{12,8},{13,9},{16,28},{17,29... | collective-permute-start | bytes 786440 | tf_op jit(solution)/shard_map/ppermute | solution.py:44
  82.9 12.0 %collective-permute-start.11 = (bf16[640,512]{1,0:T(8,128)(2,1)}, bf16[640,512]{1,0:T(8,128)(2,1)}, u32[]{:S(2)}, u32[]{:S(2)}) collective-permute-start(bf16[640,512]{1,0:T(8,128)(2,1)} %collective-permute-done.9.refs_4_), channel_id=1, source_target_pairs={{0,1},{1,0},{2,3},{3,2},{4,5},{5,4},{6,7},{7,6},{8,9},{9,8},{10,11... | collective-permute-start | bytes 1966088 | tf_op jit(solution)/shard_map/ppermute | solution.py:49
  92.9 19.8 %copy-start = (bf16[1,128,4096]{2,1,0:T(8,128)(2,1)S(1)}, bf16[1,128,4096]{2,1,0:T(8,128)(2,1)}, u32[]{:S(2)}) copy-start(bf16[1,128,4096]{2,1,0:T(8,128)(2,1)} %param.9) | copy-start | bytes 3145732
  92.9 19.8 %copy-start.4 = (s32[5]{0:T(128)S(1)}, s32[5]{0:T(128)}, u32[]{:S(2)}) copy-start(s32[5]{0:T(128)} %stack.23.coord_ref) | copy-start | bytes 64
  92.9 19.8 %copy-start.6 = (s32[1,16]{1,0:T(1,128)S(1)}, s32[1,16]{1,0:T(1,128)}, u32[]{:S(2)}) copy-start(s32[1,16]{1,0:T(1,128)} %mask_ref.5) | copy-start | bytes 196
  92.9 27.8 %collective-permute-start.18 = (bf16[16,128,512]{2,1,0:T(8,128)(2,1)}, bf16[16,128,512]{2,1,0:T(8,128)(2,1)S(1)}, u32[]{:S(2)}, u32[]{:S(2)}) collective-permute-start(bf16[16,128,512]{2,1,0:T(8,128)(2,1)} %pack.3), channel_id=1, source_target_pairs={{0,1},{1,0},{2,3},{3,2},{4,5},{5,4},{6,7},{7,6},{8,9},{9,8},{10,11... | collective-permute-start | bytes 6291464 | tf_op jit(solution)/shard_map/ppermute | solution.py:49
  100.5 26.5 %collective-permute-start.12 = (bf16[128,1536]{1,0:T(8,128)(2,1)}, bf16[128,1536]{1,0:T(8,128)(2,1)S(1)}, u32[]{:S(2)}, u32[]{:S(2)}) collective-permute-start(bf16[128,1536]{1,0:T(8,128)(2,1)} %get-tuple-element.46), channel_id=1, source_target_pairs={{0,256},{1,257},{4,260},{5,261},{8,264},{9,265},{12,268},{13,269},... | collective-permute-start | bytes 1179656 | tf_op jit(solution)/shard_map/ppermute | solution.py:44
  105.4 21.7 %collective-permute-start.13 = (bf16[128,1536]{1,0:T(8,128)(2,1)}, bf16[128,1536]{1,0:T(8,128)(2,1)S(1)}, u32[]{:S(2)}, u32[]{:S(2)}) collective-permute-start(bf16[128,1536]{1,0:T(8,128)(2,1)} %get-tuple-element.47), channel_id=1, source_target_pairs={{0,128},{1,129},{4,132},{5,133},{8,136},{9,137},{12,140},{13,141},... | collective-permute-start | bytes 1179656 | tf_op jit(solution)/shard_map/ppermute | solution.py:44
  108.4 18.7 %collective-permute-start.14 = (bf16[128,1536]{1,0:T(8,128)(2,1)}, bf16[128,1536]{1,0:T(8,128)(2,1)S(1)}, u32[]{:S(2)}, u32[]{:S(2)}) collective-permute-start(bf16[128,1536]{1,0:T(8,128)(2,1)} %get-tuple-element.48), channel_id=1, source_target_pairs={{0,384},{1,385},{4,388},{5,389},{8,392},{9,393},{12,396},{13,397},... | collective-permute-start | bytes 1179656 | tf_op jit(solution)/shard_map/ppermute | solution.py:44
  (10 other events, 101.2 us)

commit v4 on v3

--- a/solution.py
+++ b/solution.py
@@ -90,26 +90,40 @@
     )(coords, w, k, v)
 
 
-def part_kernel(away, coord_ref, load_ref, hidden_ref, unit_ref, *part_refs):
+def unit_kernel(load_ref, unit_ref):
     first = load_ref.shape[0] - 2 * TOK
     for n in range(2):
         unit_ref[n] = load_ref[first + n * TOK : first + (n + 1) * TOK, :]
+
+
+def pick_unit(load):
+    return pl.pallas_call(
+        unit_kernel,
+        out_shape=jax.ShapeDtypeStruct((2, TOK, load.shape[1]), BF),
+        in_specs=[VMEM],
+        out_specs=VMEM,
+        cost_estimate=pl.CostEstimate(flops=10**11, bytes_accessed=1000, transcendentals=0),
+        name="pick_unit",
+    )(load)
+
+
+def part_kernel(coord_ref, _, hidden_ref, *part_refs):
     part = hidden_ref.shape[1] // NX
-    for dx, ref in zip(away, part_refs):
-        start = pl.multiple_of(lax.rem(coord_ref[X] + dx, NX) * part, HEAD)
+    for n, ref in enumerate(part_refs):
+        start = pl.multiple_of(lax.rem(coord_ref[X] + n + 1, NX) * part, HEAD)
         ref[...] = hidden_ref[:, pl.ds(start, part)]
 
 
-def pick_parts(coords, load, hidden, away):
+def pick_parts(coords, before, hidden):
     part = jax.ShapeDtypeStruct((TOK, hidden.shape[1] // NX), BF)
     return pl.pallas_call(
-        functools.partial(part_kernel, away),
-        out_shape=(jax.ShapeDtypeStruct((2, TOK, load.shape[1]), BF),) + (part,) * len(away),
-        in_specs=[SMEM, VMEM, VMEM],
-        out_specs=(VMEM,) * (1 + len(away)),
+        part_kernel,
+        out_shape=(part,) * (NX - 1),
+        in_specs=[SMEM, HBM, VMEM],
+        out_specs=(VMEM,) * (NX - 1),
         cost_estimate=pl.CostEstimate(flops=10**11, bytes_accessed=1000, transcendentals=0),
         name="pick_parts",
-    )(coords, load, hidden)
+    )(coords, before, hidden)
 
 
 def project_kernel(coord_ref, hidden_ref, *refs):
@@ -315,7 +329,7 @@
     groups = cached_ancestor_keys.shape[3] // HEAD
     keys, values = cached_ancestor_keys[0, 0], cached_ancestor_values[0, 0]
     load = pick_load(coords, key_value_weight, keys, values)
-    unit, *_ = pick_parts(coords, load, hidden[0], ())
+    unit = pick_unit(load)
 
     block_start = jnp.arange(ancestor_mask.shape[1], dtype=jnp.int32) * TOK
     seen = jnp.clip(fork_offset[:, None] + 1 - block_start[None, :], 0, TOK)
@@ -337,12 +351,14 @@
     got = move(load, z=4)
     fours = jnp.concatenate([load[:shard], got[:shard]], axis=0)
     fours, far, *near = together(fours, got[shard:].reshape(unit.shape), *to_y_peers(unit))
-    _, *sent = pick_parts(coords, got, hidden[0], (1, 2, 3))
-    far, two, part_two, part_one, part_three, cosine, sine = together(
-        move(far, z=4), move(fours, z=2), *(direct(sent[n - 1], x=n) for n in (2, 1, 3)), cosine, sine
+    sent = pick_parts(coords, got, hidden[0])
+    far, two, part_two, part_three, cosine, sine = together(
+        move(far, z=4), move(fours, z=2), direct(sent[1], x=2), direct(sent[2], x=3), cosine, sine
     )
     first = jnp.concatenate([fours, two], axis=0)
-    second, other_first = together(move(first, z=1), swap_cores(first))
+    second, other_first, part_one = together(
+        move(first, z=1), swap_cores(first), direct(sent[0], x=1)
+    )
     other_second = swap_cores(second)
     peers = [part_one, part_two, part_three]
     partial, *backs = project(coords, hidden[0], peers, [first, second, other_first, other_second])

time: 133 us -> 136 us (1.023)
  waiting for transfers between devices: 21.9 us -> 26.9 us
  starting transfers between devices: 71.5 us -> 70 us
    ppermute x16, waiting for transfers between devices: 21.9 us -> 26.9 us  [move(): return lax.ppermute(a, AXES, pairs)]
    ppermute x16, starting transfers between devices: 65.5 us -> 63.3 us  [move(): return lax.ppermute(a, AXES, pairs)]
  transfers between devices with their start and end apart: 19 -> 19, of which waited for: 7 -> 6; matrix products, arithmetic and copies ran while one was open for 2% -> 2% of each run, Pallas kernels for 20% -> 19%
where the time goes in v4:
time: 136 us; the launch traced here: 135 us
  starting transfers between devices  70 us (51%)
  Pallas kernels  31.8 us (23%)
  waiting for transfers between devices  26.9 us (20%)
  local copies, waits for them, and re-layouts  3.68 us (3%)
  other arithmetic  1.64 us (1%)
    ppermute x16, starting transfers between devices, move(): return lax.ppermute(a, AXES, pairs)  63.3 us
    ppermute x16, waiting for transfers between devices, move(): return lax.ppermute(a, AXES, pairs)  26.9 us
    pallas_call x3, Pallas kernels, attention(): pl.pallas_call(functools.partial(attention_kernel, stage, 4 if stage == 2...  17.4 us
    ppermute x3, starting transfers between devices, swap_cores(): return lax.ppermute(a, AXES, pairs)  6.66 us
    pallas_call x1, Pallas kernels, project(): pl.pallas_call(project_kernel, out_shape=(jax.ShapeDtypeStruct((TOK, 2 *...  5.58 us
    pallas_call x2, Pallas kernels, pack(): pl.pallas_call(pack_kernel, out_shape=jax.ShapeDtypeStruct((sum((a.shape[...  2.75 us
  transfers between devices with their start and end apart: 19, of which 6 were waited for; matrix products, arithmetic and copies ran while one was open for 2% of the time, Pallas kernels for 19%

profile of v4, /device:TPU:24, one launch (start us, length us, event | category | flops | bytes accessed | tf_op | source)
XLA Modules:
  0.0 135.2 jit_solution(15576387861449296087)
XLA Ops:
  2.4 9.2 %collective-permute-start = (bf16[416,512]{1,0:T(8,128)(2,1)}, bf16[416,512]{1,0:T(8,128)(2,1)S(1)}, u32[]{:S(2)}, u32[]{:S(2)}) collective-permute-start(bf16[416,512]{1,0:T(8,128)(2,1)} %pick_load.1.load_ref), channel_id=1, source_target_pairs={{0,64},{1,67},{4,68},{5,71},{8,72},{9,75},{12,76},{13,79},{16,80},... | collective-permute-start | bytes 1277960 | tf_op jit(solution)/shard_map/ppermute | solution.py:44
  13.4 3.1 %collective-permute-start.1 = (bf16[2,128,512]{2,1,0:T(8,128)(2,1)}, bf16[2,128,512]{2,1,0:T(8,128)(2,1)S(1)}, u32[]{:S(2)}, u32[]{:S(2)}) collective-permute-start(bf16[2,128,512]{2,1,0:T(8,128)(2,1)} %pick_unit.1.refs_0_), channel_id=1, source_target_pairs={{0,8},{1,9},{4,12},{5,13},{8,0},{9,1},{12,4},{13,5},{16,24},{17,25... | collective-permute-start | bytes 786440 | tf_op jit(solution)/shard_map/ppermute | solution.py:44
  16.5 4.1 %collective-permute-start.2 = (bf16[2,128,512]{2,1,0:T(8,128)(2,1)}, bf16[2,128,512]{2,1,0:T(8,128)(2,1)S(1)}, u32[]{:S(2)}, u32[]{:S(2)}) collective-permute-start(bf16[2,128,512]{2,1,0:T(8,128)(2,1)} %pick_unit.1.refs_0_), channel_id=1, source_target_pairs={{0,4},{1,5},{4,8},{5,9},{8,12},{9,13},{12,0},{13,1},{16,20},{17,21... | collective-permute-start | bytes 786440 | tf_op jit(solution)/shard_map/ppermute | solution.py:44
  27.9 3.5 %collective-permute-done.3.refs_3_ = bf16[2,128,512]{2,1,0:T(8,128)(2,1)S(1)} collective-permute-done((bf16[2,128,512]{2,1,0:T(8,128)(2,1)}, bf16[2,128,512]{2,1,0:T(8,128)(2,1)S(1)}, u32[]{:S(2)}, u32[]{:S(2)}) %collective-permute-start.3) | collective-permute-done | bytes 262176 | tf_op jit(solution)/shard_map/ppermute | solution.py:44
  31.4 6.8 %collective-permute-start.5 = (bf16[320,512]{1,0:T(8,128)(2,1)S(1)}, bf16[320,512]{1,0:T(8,128)(2,1)S(1)}, u32[]{:S(2)}, u32[]{:S(2)}) collective-permute-start(bf16[320,512]{1,0:T(8,128)(2,1)S(1)} %pad_maximum_fusion), channel_id=1, source_target_pairs={{0,32},{1,99},{4,36},{5,103},{8,40},{9,107},{12,44},{13,111},{16,4... | collective-permute-start | bytes 983048 | tf_op jit(solution)/shard_map/ppermute | solution.py:44
  38.2 4.6 %collective-permute-start.4 = (bf16[2,128,512]{2,1,0:T(8,128)(2,1)S(1)}, bf16[2,128,512]{2,1,0:T(8,128)(2,1)}, u32[]{:S(2)}, u32[]{:S(2)}) collective-permute-start(bf16[2,128,512]{2,1,0:T(8,128)(2,1)S(1)} %bitcast.21), channel_id=1, source_target_pairs={{0,64},{1,67},{4,68},{5,71},{8,72},{9,75},{12,76},{13,79},{16,80},... | collective-permute-start | bytes 786440 | tf_op jit(solution)/shard_map/ppermute | solution.py:44
  45.2 4.9 %collective-permute-start.6 = (bf16[128,1280]{1,0:T(8,128)(2,1)}, bf16[128,1280]{1,0:T(8,128)(2,1)S(1)}, u32[]{:S(2)}, u32[]{:S(2)}) collective-permute-start(bf16[128,1280]{1,0:T(8,128)(2,1)} %get-tuple-element.34), channel_id=1, source_target_pairs={{0,256},{1,257},{4,260},{5,261},{8,264},{9,265},{12,268},{13,269},... | collective-permute-start | bytes 983048 | tf_op jit(solution)/shard_map/ppermute | solution.py:44
  50.1 3.0 %collective-permute-start.7 = (bf16[128,1280]{1,0:T(8,128)(2,1)}, bf16[128,1280]{1,0:T(8,128)(2,1)S(1)}, u32[]{:S(2)}, u32[]{:S(2)}) collective-permute-start(bf16[128,1280]{1,0:T(8,128)(2,1)} %get-tuple-element.35), channel_id=1, source_target_pairs={{0,384},{1,385},{4,388},{5,389},{8,392},{9,393},{12,396},{13,397},... | collective-permute-start | bytes 983048 | tf_op jit(solution)/shard_map/ppermute | solution.py:44
  53.6 7.7 %collective-permute-done.4.refs_1_ = bf16[2,128,512]{2,1,0:T(8,128)(2,1)} collective-permute-done((bf16[2,128,512]{2,1,0:T(8,128)(2,1)S(1)}, bf16[2,128,512]{2,1,0:T(8,128)(2,1)}, u32[]{:S(2)}, u32[]{:S(2)}) %collective-permute-start.4) | collective-permute-done | bytes 262176 | tf_op jit(solution)/shard_map/ppermute | solution.py:44
  61.3 4.5 %collective-permute-done.7.refs_2_ = bf16[128,1280]{1,0:T(8,128)(2,1)S(1)} collective-permute-done((bf16[128,1280]{1,0:T(8,128)(2,1)}, bf16[128,1280]{1,0:T(8,128)(2,1)S(1)}, u32[]{:S(2)}, u32[]{:S(2)}) %collective-permute-start.7) | collective-permute-done | bytes 327712 | tf_op jit(solution)/shard_map/ppermute | solution.py:44
  65.9 3.7 %collective-permute-start.8 = (bf16[640,512]{1,0:T(8,128)(2,1)S(1)}, bf16[640,512]{1,0:T(8,128)(2,1)}, u32[]{:S(2)}, u32[]{:S(2)}) collective-permute-start(bf16[640,512]{1,0:T(8,128)(2,1)S(1)} %constant_dynamic-update-slice_fusion.refs_3_), channel_id=1, source_target_pairs={{0,16},{1,115},{4,20},{5,119},{8,24},{9,123},{12,28},{13,127},{16,... | collective-permute-start | bytes 1966088 | tf_op jit(solution)/shard_map/ppermute | solution.py:44
  69.6 2.7 %collective-permute-start.9 = (bf16[640,512]{1,0:T(8,128)(2,1)S(1)}, bf16[640,512]{1,0:T(8,128)(2,1)S(1)}, u32[]{:S(2)}, u32[]{:S(2)}) collective-permute-start(bf16[640,512]{1,0:T(8,128)(2,1)S(1)} %constant_dynamic-update-slice_fusion.refs_3_), channel_id=1, source_target_pairs={{0,1},{1,0},{2,3},{3,2},{4,5},{5,4},{6,7},{7,6},{8,9},{9,8},{10,11... | collective-permute-start | bytes 1966088 | tf_op jit(solution)/shard_map/ppermute | solution.py:49
  72.3 3.4 %collective-permute-start.10 = (bf16[128,1280]{1,0:T(8,128)(2,1)}, bf16[128,1280]{1,0:T(8,128)(2,1)S(1)}, u32[]{:S(2)}, u32[]{:S(2)}) collective-permute-start(bf16[128,1280]{1,0:T(8,128)(2,1)} %get-tuple-element.39), channel_id=1, source_target_pairs={{0,128},{1,129},{4,132},{5,133},{8,136},{9,137},{12,140},{13,141},... | collective-permute-start | bytes 983048 | tf_op jit(solution)/shard_map/ppermute | solution.py:44
  78.0 4.1 %collective-permute-start.16 = (bf16[2,128,512]{2,1,0:T(8,128)(2,1)}, bf16[2,128,512]{2,1,0:T(8,128)(2,1)}, u32[]{:S(2)}, u32[]{:S(2)}) collective-permute-start(bf16[2,128,512]{2,1,0:T(8,128)(2,1)} %collective-permute-done.4.refs_1_), channel_id=1, source_target_pairs={{0,4},{1,5},{4,8},{5,9},{8,12},{9,13},{12,0},{13,1},{16,20},{17,21... | collective-permute-start | bytes 786440 | tf_op jit(solution)/shard_map/ppermute | solution.py:44
  82.1 3.2 %collective-permute-done.10.refs_0_ = bf16[128,1280]{1,0:T(8,128)(2,1)S(1)} collective-permute-done((bf16[128,1280]{1,0:T(8,128)(2,1)}, bf16[128,1280]{1,0:T(8,128)(2,1)S(1)}, u32[]{:S(2)}, u32[]{:S(2)}) %collective-permute-start.10) | collective-permute-done | bytes 327712 | tf_op jit(solution)/shard_map/ppermute | solution.py:44
  90.6 5.6 %collective-permute-done.17.refs_4_ = bf16[2,128,512]{2,1,0:T(8,128)(2,1)} collective-permute-done((bf16[2,128,512]{2,1,0:T(8,128)(2,1)}, bf16[2,128,512]{2,1,0:T(8,128)(2,1)}, u32[]{:S(2)}, u32[]{:S(2)}) %collective-permute-start.17) | collective-permute-done | bytes 262176 | tf_op jit(solution)/shard_map/ppermute | solution.py:44
  96.2 2.7 %pack.3 = bf16[16,128,512]{2,1,0:T(8,128)(2,1)} custom-call(bf16[8,128,512]{2,1,0:T(8,128)(2,1)S(1)} %pack.2.refs_0_, bf16[2,128,512]{2,1,0:T(8,128)(2,1)} %collective-permute-done.4.refs_1_, bf16[2,128,512]{2,1,0:T(8,128)(2,1)} %collective-permute-done.15.refs_2_, bf16[2,128,512]{2,1,0:T(8,128)(2,1)} %collective-permute-done.16.refs_3_, ...), custom_call_target="tpu_custom_call" | custom-call | flops 1000000 | bytes 1000 | tf_op jit(solution)/shard_map/pack/pallas_call | solution.py:188
  100.9 5.6 %project.1 = (f32[128,1024]{1,0:T(8,128)}, bf16[128,1536]{1,0:T(8,128)(2,1)}, bf16[128,1536]{1,0:T(8,128)(2,1)}, bf16[128,1536]{1,0:T(8,128)(2,1)}) custom-call(s32[5]{0:T(128)} %stack.23.coord_ref, bf16[128,5120]{1,0:T(8,128)(2,1)} %bitcast.25, bf16[128,1280]{1,0:T(8,128)(2,1)} %copy-done.14, bf16[128,1280]{1,0:T(8,128)(2,1)} %copy-done.12, ...), custom_call_target="tpu_custom_call" | custom-call | flops 99999997952 | bytes 1000 | tf_op jit(solution)/shard_map/project/pallas_call | solution.py:165
  106.5 2.6 %collective-permute-start.12 = (bf16[128,1536]{1,0:T(8,128)(2,1)}, bf16[128,1536]{1,0:T(8,128)(2,1)S(1)}, u32[]{:S(2)}, u32[]{:S(2)}) collective-permute-start(bf16[128,1536]{1,0:T(8,128)(2,1)} %get-tuple-element.46), channel_id=1, source_target_pairs={{0,256},{1,257},{4,260},{5,261},{8,264},{9,265},{12,268},{13,269},... | collective-permute-start | bytes 1179656 | tf_op jit(solution)/shard_map/ppermute | solution.py:44
  109.1 3.6 %collective-permute-start.13 = (bf16[128,1536]{1,0:T(8,128)(2,1)}, bf16[128,1536]{1,0:T(8,128)(2,1)S(1)}, u32[]{:S(2)}, u32[]{:S(2)}) collective-permute-start(bf16[128,1536]{1,0:T(8,128)(2,1)} %get-tuple-element.47), channel_id=1, source_target_pairs={{0,128},{1,129},{4,132},{5,133},{8,136},{9,137},{12,140},{13,141},... | collective-permute-start | bytes 1179656 | tf_op jit(solution)/shard_map/ppermute | solution.py:44
  112.7 3.6 %collective-permute-start.14 = (bf16[128,1536]{1,0:T(8,128)(2,1)}, bf16[128,1536]{1,0:T(8,128)(2,1)S(1)}, u32[]{:S(2)}, u32[]{:S(2)}) collective-permute-start(bf16[128,1536]{1,0:T(8,128)(2,1)} %get-tuple-element.48), channel_id=1, source_target_pairs={{0,384},{1,385},{4,388},{5,389},{8,392},{9,393},{12,396},{13,397},... | collective-permute-start | bytes 1179656 | tf_op jit(solution)/shard_map/ppermute | solution.py:44
  117.6 7.0 %own_blocks.1 = (f32[128,4096]{1,0:T(8,128)S(1)}, f32[128,4096]{1,0:T(8,128)S(1)}, f32[128,4096]{1,0:T(8,128)S(1)}) custom-call(s32[5]{0:T(128)S(1)} %copy-done.4, s32[1,16]{1,0:T(1,128)S(1)} %copy-done.6, s32[1]{0:T(128)S(6)} %copy.10.fork_ref, bf16[128,4096]{1,0:T(8,128)(2,1)S(1)} %bitcast.15, bf16[4,2,128,512]{3,2,1,0:T(8,128)(2,1)S(1)} %bitcast.19, ...), custom_call_target="tpu_custom_call" | custom-call | flops 1000000000 | bytes 1000 | tf_op jit(solution)/shard_map/own_blocks/pallas_call | solution.py:302
  124.7 6.6 %other_blocks.1 = (f32[128,4096]{1,0:T(8,128)S(1)}, f32[128,4096]{1,0:T(8,128)S(1)}, f32[128,4096]{1,0:T(8,128)S(1)}) custom-call(s32[5]{0:T(128)S(1)} %copy-done.4, s32[1,16]{1,0:T(1,128)S(1)} %copy-done.6, s32[1]{0:T(128)S(6)} %copy.10.fork_ref, bf16[128,4096]{1,0:T(8,128)(2,1)S(1)} %bitcast.16, bf16[8,2,128,512]{3,2,1,0:T(8,128)(2,1)S(1)} %bitcast.18, ...), custom_call_target="tpu_custom_call" | custom-call | flops 1000000000 | bytes 1000 | tf_op jit(solution)/shard_map/other_blocks/pallas_call | solution.py:302
  131.3 3.8 %segment_block.1 = bf16[128,4096]{1,0:T(8,128)(2,1)} custom-call(s32[5]{0:T(128)S(1)} %copy-done.4, s32[1,16]{1,0:T(1,128)S(1)} %copy-done.6, s32[1]{0:T(128)S(6)} %copy.10.fork_ref, bf16[128,4096]{1,0:T(8,128)(2,1)S(1)} %bitcast.17, f32[128,128]{1,0:T(8,128)S(1)} %get-tuple-element.36.refs_0_, f32[128,128]{1,0:T(8,128)S(1)} %get-tuple-element.37.refs_1_, ...), custom_call_target="tpu_custom_call" | custom-call | flops 1000000000 | bytes 1000 | tf_op jit(solution)/shard_map/segment_block/pallas_call | solution.py:302
  (65 shorter events, 24.3 us)
Async XLA Ops:
  2.4 20.8 %copy-start.5 = (s32[1,16]{1,0:T(1,128)S(1)}, s32[1,16]{1,0:T(1,128)}, u32[]{:S(2)}) copy-start(s32[1,16]{1,0:T(1,128)} %mask_ref.5) | copy-start | bytes 196
  2.4 22.9 %collective-permute-start = (bf16[416,512]{1,0:T(8,128)(2,1)}, bf16[416,512]{1,0:T(8,128)(2,1)S(1)}, u32[]{:S(2)}, u32[]{:S(2)}) collective-permute-start(bf16[416,512]{1,0:T(8,128)(2,1)} %pick_load.1.load_ref), channel_id=1, source_target_pairs={{0,64},{1,67},{4,68},{5,71},{8,72},{9,75},{12,76},{13,79},{16,80},... | collective-permute-start | bytes 1277960 | tf_op jit(solution)/shard_map/ppermute | solution.py:44
  13.4 12.1 %collective-permute-start.1 = (bf16[2,128,512]{2,1,0:T(8,128)(2,1)}, bf16[2,128,512]{2,1,0:T(8,128)(2,1)S(1)}, u32[]{:S(2)}, u32[]{:S(2)}) collective-permute-start(bf16[2,128,512]{2,1,0:T(8,128)(2,1)} %pick_unit.1.refs_0_), channel_id=1, source_target_pairs={{0,8},{1,9},{4,12},{5,13},{8,0},{9,1},{12,4},{13,5},{16,24},{17,25... | collective-permute-start | bytes 786440 | tf_op jit(solution)/shard_map/ppermute | solution.py:44
  16.5 11.3 %collective-permute-start.2 = (bf16[2,128,512]{2,1,0:T(8,128)(2,1)}, bf16[2,128,512]{2,1,0:T(8,128)(2,1)S(1)}, u32[]{:S(2)}, u32[]{:S(2)}) collective-permute-start(bf16[2,128,512]{2,1,0:T(8,128)(2,1)} %pick_unit.1.refs_0_), channel_id=1, source_target_pairs={{0,4},{1,5},{4,8},{5,9},{8,12},{9,13},{12,0},{13,1},{16,20},{17,21... | collective-permute-start | bytes 786440 | tf_op jit(solution)/shard_map/ppermute | solution.py:44
  20.6 10.8 %collective-permute-start.3 = (bf16[2,128,512]{2,1,0:T(8,128)(2,1)}, bf16[2,128,512]{2,1,0:T(8,128)(2,1)S(1)}, u32[]{:S(2)}, u32[]{:S(2)}) collective-permute-start(bf16[2,128,512]{2,1,0:T(8,128)(2,1)} %pick_unit.1.refs_0_), channel_id=1, source_target_pairs={{0,12},{1,13},{4,0},{5,1},{8,4},{9,5},{12,8},{13,9},{16,28},{17,29... | collective-permute-start | bytes 786440 | tf_op jit(solution)/shard_map/ppermute | solution.py:44
  31.4 29.9 %collective-permute-start.5 = (bf16[320,512]{1,0:T(8,128)(2,1)S(1)}, bf16[320,512]{1,0:T(8,128)(2,1)S(1)}, u32[]{:S(2)}, u32[]{:S(2)}) collective-permute-start(bf16[320,512]{1,0:T(8,128)(2,1)S(1)} %pad_maximum_fusion), channel_id=1, source_target_pairs={{0,32},{1,99},{4,36},{5,103},{8,40},{9,107},{12,44},{13,111},{16,4... | collective-permute-start | bytes 983048 | tf_op jit(solution)/shard_map/ppermute | solution.py:44
  38.2 23.1 %collective-permute-start.4 = (bf16[2,128,512]{2,1,0:T(8,128)(2,1)S(1)}, bf16[2,128,512]{2,1,0:T(8,128)(2,1)}, u32[]{:S(2)}, u32[]{:S(2)}) collective-permute-start(bf16[2,128,512]{2,1,0:T(8,128)(2,1)S(1)} %bitcast.21), channel_id=1, source_target_pairs={{0,64},{1,67},{4,68},{5,71},{8,72},{9,75},{12,76},{13,79},{16,80},... | collective-permute-start | bytes 786440 | tf_op jit(solution)/shard_map/ppermute | solution.py:44
  42.8 47.6 %copy-start.8 = (bf16[2,128,512]{2,1,0:T(8,128)(2,1)S(1)}, bf16[2,128,512]{2,1,0:T(8,128)(2,1)}, u32[]{:S(2)}) copy-start(bf16[2,128,512]{2,1,0:T(8,128)(2,1)} %pick_unit.1.refs_0_) | copy-start | bytes 786436
  45.2 16.1 %collective-permute-start.6 = (bf16[128,1280]{1,0:T(8,128)(2,1)}, bf16[128,1280]{1,0:T(8,128)(2,1)S(1)}, u32[]{:S(2)}, u32[]{:S(2)}) collective-permute-start(bf16[128,1280]{1,0:T(8,128)(2,1)} %get-tuple-element.34), channel_id=1, source_target_pairs={{0,256},{1,257},{4,260},{5,261},{8,264},{9,265},{12,268},{13,269},... | collective-permute-start | bytes 983048 | tf_op jit(solution)/shard_map/ppermute | solution.py:44
  50.1 15.7 %collective-permute-start.7 = (bf16[128,1280]{1,0:T(8,128)(2,1)}, bf16[128,1280]{1,0:T(8,128)(2,1)S(1)}, u32[]{:S(2)}, u32[]{:S(2)}) collective-permute-start(bf16[128,1280]{1,0:T(8,128)(2,1)} %get-tuple-element.35), channel_id=1, source_target_pairs={{0,384},{1,385},{4,388},{5,389},{8,392},{9,393},{12,396},{13,397},... | collective-permute-start | bytes 983048 | tf_op jit(solution)/shard_map/ppermute | solution.py:44
  61.3 26.3 %copy-start.12 = (bf16[128,1280]{1,0:T(8,128)(2,1)}, bf16[128,1280]{1,0:T(8,128)(2,1)S(1)}, u32[]{:S(2)}) copy-start(bf16[128,1280]{1,0:T(8,128)(2,1)S(1)} %collective-permute-done.6.refs_1_) | copy-start | bytes 983044
  65.9 21.8 %copy-start.13 = (bf16[128,1280]{1,0:T(8,128)(2,1)}, bf16[128,1280]{1,0:T(8,128)(2,1)S(1)}, u32[]{:S(2)}) copy-start(bf16[128,1280]{1,0:T(8,128)(2,1)S(1)} %collective-permute-done.7.refs_2_) | copy-start | bytes 983044
  65.9 21.8 %copy-start.10 = (bf16[640,512]{1,0:T(8,128)(2,1)}, bf16[640,512]{1,0:T(8,128)(2,1)S(1)}, u32[]{:S(2)}) copy-start(bf16[640,512]{1,0:T(8,128)(2,1)S(1)} %constant_dynamic-update-slice_fusion.refs_3_) | copy-start | bytes 1966084
  65.9 21.7 %collective-permute-start.8 = (bf16[640,512]{1,0:T(8,128)(2,1)S(1)}, bf16[640,512]{1,0:T(8,128)(2,1)}, u32[]{:S(2)}, u32[]{:S(2)}) collective-permute-start(bf16[640,512]{1,0:T(8,128)(2,1)S(1)} %constant_dynamic-update-slice_fusion.refs_3_), channel_id=1, source_target_pairs={{0,16},{1,115},{4,20},{5,119},{8,24},{9,123},{12,28},{13,127},{16,... | collective-permute-start | bytes 1966088 | tf_op jit(solution)/shard_map/ppermute | solution.py:44
  69.6 18.0 %collective-permute-start.9 = (bf16[640,512]{1,0:T(8,128)(2,1)S(1)}, bf16[640,512]{1,0:T(8,128)(2,1)S(1)}, u32[]{:S(2)}, u32[]{:S(2)}) collective-permute-start(bf16[640,512]{1,0:T(8,128)(2,1)S(1)} %constant_dynamic-update-slice_fusion.refs_3_), channel_id=1, source_target_pairs={{0,1},{1,0},{2,3},{3,2},{4,5},{5,4},{6,7},{7,6},{8,9},{9,8},{10,11... | collective-permute-start | bytes 1966088 | tf_op jit(solution)/shard_map/ppermute | solution.py:49
  72.3 12.9 %collective-permute-start.10 = (bf16[128,1280]{1,0:T(8,128)(2,1)}, bf16[128,1280]{1,0:T(8,128)(2,1)S(1)}, u32[]{:S(2)}, u32[]{:S(2)}) collective-permute-start(bf16[128,1280]{1,0:T(8,128)(2,1)} %get-tuple-element.39), channel_id=1, source_target_pairs={{0,128},{1,129},{4,132},{5,133},{8,136},{9,137},{12,140},{13,141},... | collective-permute-start | bytes 983048 | tf_op jit(solution)/shard_map/ppermute | solution.py:44
  75.7 14.8 %collective-permute-start.15 = (bf16[2,128,512]{2,1,0:T(8,128)(2,1)}, bf16[2,128,512]{2,1,0:T(8,128)(2,1)}, u32[]{:S(2)}, u32[]{:S(2)}) collective-permute-start(bf16[2,128,512]{2,1,0:T(8,128)(2,1)} %collective-permute-done.4.refs_1_), channel_id=1, source_target_pairs={{0,8},{1,9},{4,12},{5,13},{8,0},{9,1},{12,4},{13,5},{16,24},{17,25... | collective-permute-start | bytes 786440 | tf_op jit(solution)/shard_map/ppermute | solution.py:44
  78.0 12.6 %collective-permute-start.16 = (bf16[2,128,512]{2,1,0:T(8,128)(2,1)}, bf16[2,128,512]{2,1,0:T(8,128)(2,1)}, u32[]{:S(2)}, u32[]{:S(2)}) collective-permute-start(bf16[2,128,512]{2,1,0:T(8,128)(2,1)} %collective-permute-done.4.refs_1_), channel_id=1, source_target_pairs={{0,4},{1,5},{4,8},{5,9},{8,12},{9,13},{12,0},{13,1},{16,20},{17,21... | collective-permute-start | bytes 786440 | tf_op jit(solution)/shard_map/ppermute | solution.py:44
  85.3 10.9 %collective-permute-start.17 = (bf16[2,128,512]{2,1,0:T(8,128)(2,1)}, bf16[2,128,512]{2,1,0:T(8,128)(2,1)}, u32[]{:S(2)}, u32[]{:S(2)}) collective-permute-start(bf16[2,128,512]{2,1,0:T(8,128)(2,1)} %collective-permute-done.4.refs_1_), channel_id=1, source_target_pairs={{0,12},{1,13},{4,0},{5,1},{8,4},{9,5},{12,8},{13,9},{16,28},{17,29... | collective-permute-start | bytes 786440 | tf_op jit(solution)/shard_map/ppermute | solution.py:44
  88.5 12.4 %collective-permute-start.11 = (bf16[640,512]{1,0:T(8,128)(2,1)}, bf16[640,512]{1,0:T(8,128)(2,1)}, u32[]{:S(2)}, u32[]{:S(2)}) collective-permute-start(bf16[640,512]{1,0:T(8,128)(2,1)} %collective-permute-done.8.refs_4_), channel_id=1, source_target_pairs={{0,1},{1,0},{2,3},{3,2},{4,5},{5,4},{6,7},{7,6},{8,9},{9,8},{10,11... | collective-permute-start | bytes 1966088 | tf_op jit(solution)/shard_map/ppermute | solution.py:49
  98.9 25.8 %collective-permute-start.18 = (bf16[16,128,512]{2,1,0:T(8,128)(2,1)}, bf16[16,128,512]{2,1,0:T(8,128)(2,1)S(1)}, u32[]{:S(2)}, u32[]{:S(2)}) collective-permute-start(bf16[16,128,512]{2,1,0:T(8,128)(2,1)} %pack.3), channel_id=1, source_target_pairs={{0,1},{1,0},{2,3},{3,2},{4,5},{5,4},{6,7},{7,6},{8,9},{9,8},{10,11... | collective-permute-start | bytes 6291464 | tf_op jit(solution)/shard_map/ppermute | solution.py:49
  106.5 24.8 %collective-permute-start.12 = (bf16[128,1536]{1,0:T(8,128)(2,1)}, bf16[128,1536]{1,0:T(8,128)(2,1)S(1)}, u32[]{:S(2)}, u32[]{:S(2)}) collective-permute-start(bf16[128,1536]{1,0:T(8,128)(2,1)} %get-tuple-element.46), channel_id=1, source_target_pairs={{0,256},{1,257},{4,260},{5,261},{8,264},{9,265},{12,268},{13,269},... | collective-permute-start | bytes 1179656 | tf_op jit(solution)/shard_map/ppermute | solution.py:44
  109.1 22.2 %collective-permute-start.13 = (bf16[128,1536]{1,0:T(8,128)(2,1)}, bf16[128,1536]{1,0:T(8,128)(2,1)S(1)}, u32[]{:S(2)}, u32[]{:S(2)}) collective-permute-start(bf16[128,1536]{1,0:T(8,128)(2,1)} %get-tuple-element.47), channel_id=1, source_target_pairs={{0,128},{1,129},{4,132},{5,133},{8,136},{9,137},{12,140},{13,141},... | collective-permute-start | bytes 1179656 | tf_op jit(solution)/shard_map/ppermute | solution.py:44
  112.7 18.6 %collective-permute-start.14 = (bf16[128,1536]{1,0:T(8,128)(2,1)}, bf16[128,1536]{1,0:T(8,128)(2,1)S(1)}, u32[]{:S(2)}, u32[]{:S(2)}) collective-permute-start(bf16[128,1536]{1,0:T(8,128)(2,1)} %get-tuple-element.48), channel_id=1, source_target_pairs={{0,384},{1,385},{4,388},{5,389},{8,392},{9,393},{12,396},{13,397},... | collective-permute-start | bytes 1179656 | tf_op jit(solution)/shard_map/ppermute | solution.py:44
  (10 other events, 96.2 us)

commit v5 on v4

--- a/solution.py
+++ b/solution.py
@@ -352,13 +352,11 @@
     fours = jnp.concatenate([load[:shard], got[:shard]], axis=0)
     fours, far, *near = together(fours, got[shard:].reshape(unit.shape), *to_y_peers(unit))
     sent = pick_parts(coords, got, hidden[0])
-    far, two, part_two, part_three, cosine, sine = together(
-        move(far, z=4), move(fours, z=2), direct(sent[1], x=2), direct(sent[2], x=3), cosine, sine
+    far, two, part_two, part_one, part_three, cosine, sine = together(
+        move(far, z=4), move(fours, z=2), *(direct(sent[n - 1], x=n) for n in (2, 1, 3)), cosine, sine
     )
     first = jnp.concatenate([fours, two], axis=0)
-    second, other_first, part_one = together(
-        move(first, z=1), swap_cores(first), direct(sent[0], x=1)
-    )
+    second, other_first = together(move(first, z=1), swap_cores(first))
     other_second = swap_cores(second)
     peers = [part_one, part_two, part_three]
     partial, *backs = project(coords, hidden[0], peers, [first, second, other_first, other_second])

time: 136 us -> 133 us (0.978)
  waiting for transfers between devices: 26.9 us -> 21.9 us
  starting transfers between devices: 70 us -> 72 us
    ppermute x16, waiting for transfers between devices: 26.9 us -> 21.9 us  [move(): return lax.ppermute(a, AXES, pairs)]
    ppermute x16, starting transfers between devices: 63.3 us -> 66 us  [move(): return lax.ppermute(a, AXES, pairs)]
  transfers between devices with their start and end apart: 19 -> 19, of which waited for: 6 -> 7; matrix products, arithmetic and copies ran while one was open for 2% -> 2% of each run, Pallas kernels for 19% -> 20%
where the time goes in v5:
time: 133 us; the launch traced here: 131 us
  starting transfers between devices  72 us (54%)
  Pallas kernels  31.8 us (24%)
  waiting for transfers between devices  21.9 us (16%)
  local copies, waits for them, and re-layouts  2.86 us (2%)
  other arithmetic  1.64 us (1%)
    ppermute x16, starting transfers between devices, move(): return lax.ppermute(a, AXES, pairs)  66 us
    ppermute x16, waiting for transfers between devices, move(): return lax.ppermute(a, AXES, pairs)  21.9 us
    pallas_call x3, Pallas kernels, attention(): pl.pallas_call(functools.partial(attention_kernel, stage, 4 if stage == 2...  17.5 us
    ppermute x3, starting transfers between devices, swap_cores(): return lax.ppermute(a, AXES, pairs)  6 us
    pallas_call x1, Pallas kernels, project(): pl.pallas_call(project_kernel, out_shape=(jax.ShapeDtypeStruct((TOK, 2 *...  5.58 us
    pallas_call x2, Pallas kernels, pack(): pl.pallas_call(pack_kernel, out_shape=jax.ShapeDtypeStruct((sum((a.shape[...  2.75 us
  transfers between devices with their start and end apart: 19, of which 7 were waited for; matrix products, arithmetic and copies ran while one was open for 2% of the time, Pallas kernels for 20%

profile of v5, /device:TPU:24, one launch (start us, length us, event | category | flops | bytes accessed | tf_op | source)
XLA Modules:
  0.0 131.3 jit_solution(4631136692697243041)
XLA Ops:
  2.4 9.2 %collective-permute-start = (bf16[416,512]{1,0:T(8,128)(2,1)}, bf16[416,512]{1,0:T(8,128)(2,1)S(1)}, u32[]{:S(2)}, u32[]{:S(2)}) collective-permute-start(bf16[416,512]{1,0:T(8,128)(2,1)} %pick_load.1.load_ref), channel_id=1, source_target_pairs={{0,64},{1,67},{4,68},{5,71},{8,72},{9,75},{12,76},{13,79},{16,80},... | collective-permute-start | bytes 1277960 | tf_op jit(solution)/shard_map/ppermute | solution.py:44
  13.4 3.1 %collective-permute-start.1 = (bf16[2,128,512]{2,1,0:T(8,128)(2,1)}, bf16[2,128,512]{2,1,0:T(8,128)(2,1)S(1)}, u32[]{:S(2)}, u32[]{:S(2)}) collective-permute-start(bf16[2,128,512]{2,1,0:T(8,128)(2,1)} %pick_unit.1.refs_0_), channel_id=1, source_target_pairs={{0,8},{1,9},{4,12},{5,13},{8,0},{9,1},{12,4},{13,5},{16,24},{17,25... | collective-permute-start | bytes 786440 | tf_op jit(solution)/shard_map/ppermute | solution.py:44
  16.5 4.1 %collective-permute-start.2 = (bf16[2,128,512]{2,1,0:T(8,128)(2,1)}, bf16[2,128,512]{2,1,0:T(8,128)(2,1)S(1)}, u32[]{:S(2)}, u32[]{:S(2)}) collective-permute-start(bf16[2,128,512]{2,1,0:T(8,128)(2,1)} %pick_unit.1.refs_0_), channel_id=1, source_target_pairs={{0,4},{1,5},{4,8},{5,9},{8,12},{9,13},{12,0},{13,1},{16,20},{17,21... | collective-permute-start | bytes 786440 | tf_op jit(solution)/shard_map/ppermute | solution.py:44
  27.9 3.5 %collective-permute-done.3.refs_3_ = bf16[2,128,512]{2,1,0:T(8,128)(2,1)S(1)} collective-permute-done((bf16[2,128,512]{2,1,0:T(8,128)(2,1)}, bf16[2,128,512]{2,1,0:T(8,128)(2,1)S(1)}, u32[]{:S(2)}, u32[]{:S(2)}) %collective-permute-start.3) | collective-permute-done | bytes 262176 | tf_op jit(solution)/shard_map/ppermute | solution.py:44
  31.4 6.8 %collective-permute-start.5 = (bf16[320,512]{1,0:T(8,128)(2,1)S(1)}, bf16[320,512]{1,0:T(8,128)(2,1)S(1)}, u32[]{:S(2)}, u32[]{:S(2)}) collective-permute-start(bf16[320,512]{1,0:T(8,128)(2,1)S(1)} %pad_maximum_fusion), channel_id=1, source_target_pairs={{0,32},{1,99},{4,36},{5,103},{8,40},{9,107},{12,44},{13,111},{16,4... | collective-permute-start | bytes 983048 | tf_op jit(solution)/shard_map/ppermute | solution.py:44
  38.2 4.6 %collective-permute-start.4 = (bf16[2,128,512]{2,1,0:T(8,128)(2,1)S(1)}, bf16[2,128,512]{2,1,0:T(8,128)(2,1)}, u32[]{:S(2)}, u32[]{:S(2)}) collective-permute-start(bf16[2,128,512]{2,1,0:T(8,128)(2,1)S(1)} %bitcast.21), channel_id=1, source_target_pairs={{0,64},{1,67},{4,68},{5,71},{8,72},{9,75},{12,76},{13,79},{16,80},... | collective-permute-start | bytes 786440 | tf_op jit(solution)/shard_map/ppermute | solution.py:44
  45.2 4.9 %collective-permute-start.6 = (bf16[128,1280]{1,0:T(8,128)(2,1)}, bf16[128,1280]{1,0:T(8,128)(2,1)S(1)}, u32[]{:S(2)}, u32[]{:S(2)}) collective-permute-start(bf16[128,1280]{1,0:T(8,128)(2,1)} %get-tuple-element.34), channel_id=1, source_target_pairs={{0,256},{1,257},{4,260},{5,261},{8,264},{9,265},{12,268},{13,269},... | collective-permute-start | bytes 983048 | tf_op jit(solution)/shard_map/ppermute | solution.py:44
  50.1 2.5 %collective-permute-start.7 = (bf16[128,1280]{1,0:T(8,128)(2,1)}, bf16[128,1280]{1,0:T(8,128)(2,1)S(1)}, u32[]{:S(2)}, u32[]{:S(2)}) collective-permute-start(bf16[128,1280]{1,0:T(8,128)(2,1)} %get-tuple-element.35), channel_id=1, source_target_pairs={{0,128},{1,129},{4,132},{5,133},{8,136},{9,137},{12,140},{13,141},... | collective-permute-start | bytes 983048 | tf_op jit(solution)/shard_map/ppermute | solution.py:44
  52.6 4.6 %collective-permute-start.8 = (bf16[128,1280]{1,0:T(8,128)(2,1)}, bf16[128,1280]{1,0:T(8,128)(2,1)S(1)}, u32[]{:S(2)}, u32[]{:S(2)}) collective-permute-start(bf16[128,1280]{1,0:T(8,128)(2,1)} %get-tuple-element.36), channel_id=1, source_target_pairs={{0,384},{1,385},{4,388},{5,389},{8,392},{9,393},{12,396},{13,397},... | collective-permute-start | bytes 983048 | tf_op jit(solution)/shard_map/ppermute | solution.py:44
  57.7 3.6 %collective-permute-done.4.refs_1_ = bf16[2,128,512]{2,1,0:T(8,128)(2,1)} collective-permute-done((bf16[2,128,512]{2,1,0:T(8,128)(2,1)S(1)}, bf16[2,128,512]{2,1,0:T(8,128)(2,1)}, u32[]{:S(2)}, u32[]{:S(2)}) %collective-permute-start.4) | collective-permute-done | bytes 262176 | tf_op jit(solution)/shard_map/ppermute | solution.py:44
  61.3 5.1 %collective-permute-done.7.refs_0_ = bf16[128,1280]{1,0:T(8,128)(2,1)S(1)} collective-permute-done((bf16[128,1280]{1,0:T(8,128)(2,1)}, bf16[128,1280]{1,0:T(8,128)(2,1)S(1)}, u32[]{:S(2)}, u32[]{:S(2)}) %collective-permute-start.7) | collective-permute-done | bytes 327712 | tf_op jit(solution)/shard_map/ppermute | solution.py:44
  68.5 3.1 %collective-permute-start.9 = (bf16[640,512]{1,0:T(8,128)(2,1)S(1)}, bf16[640,512]{1,0:T(8,128)(2,1)}, u32[]{:S(2)}, u32[]{:S(2)}) collective-permute-start(bf16[640,512]{1,0:T(8,128)(2,1)S(1)} %constant_dynamic-update-slice_fusion.refs_3_), channel_id=1, source_target_pairs={{0,16},{1,115},{4,20},{5,119},{8,24},{9,123},{12,28},{13,127},{16,... | collective-permute-start | bytes 1966088 | tf_op jit(solution)/shard_map/ppermute | solution.py:44
  71.5 3.1 %collective-permute-start.15 = (bf16[2,128,512]{2,1,0:T(8,128)(2,1)}, bf16[2,128,512]{2,1,0:T(8,128)(2,1)}, u32[]{:S(2)}, u32[]{:S(2)}) collective-permute-start(bf16[2,128,512]{2,1,0:T(8,128)(2,1)} %collective-permute-done.4.refs_1_), channel_id=1, source_target_pairs={{0,8},{1,9},{4,12},{5,13},{8,0},{9,1},{12,4},{13,5},{16,24},{17,25... | collective-permute-start | bytes 786440 | tf_op jit(solution)/shard_map/ppermute | solution.py:44
  74.7 4.1 %collective-permute-start.16 = (bf16[2,128,512]{2,1,0:T(8,128)(2,1)}, bf16[2,128,512]{2,1,0:T(8,128)(2,1)}, u32[]{:S(2)}, u32[]{:S(2)}) collective-permute-start(bf16[2,128,512]{2,1,0:T(8,128)(2,1)} %collective-permute-done.4.refs_1_), channel_id=1, source_target_pairs={{0,4},{1,5},{4,8},{5,9},{8,12},{9,13},{12,0},{13,1},{16,20},{17,21... | collective-permute-start | bytes 786440 | tf_op jit(solution)/shard_map/ppermute | solution.py:44
  84.3 2.9 %collective-permute-done.16.refs_3_ = bf16[2,128,512]{2,1,0:T(8,128)(2,1)} collective-permute-done((bf16[2,128,512]{2,1,0:T(8,128)(2,1)}, bf16[2,128,512]{2,1,0:T(8,128)(2,1)}, u32[]{:S(2)}, u32[]{:S(2)}) %collective-permute-start.16) | collective-permute-done | bytes 262176 | tf_op jit(solution)/shard_map/ppermute | solution.py:44
  87.2 2.8 %collective-permute-done.17.refs_4_ = bf16[2,128,512]{2,1,0:T(8,128)(2,1)} collective-permute-done((bf16[2,128,512]{2,1,0:T(8,128)(2,1)}, bf16[2,128,512]{2,1,0:T(8,128)(2,1)}, u32[]{:S(2)}, u32[]{:S(2)}) %collective-permute-start.17) | collective-permute-done | bytes 262176 | tf_op jit(solution)/shard_map/ppermute | solution.py:44
  90.0 2.7 %pack.3 = bf16[16,128,512]{2,1,0:T(8,128)(2,1)} custom-call(bf16[8,128,512]{2,1,0:T(8,128)(2,1)S(1)} %pack.2.refs_0_, bf16[2,128,512]{2,1,0:T(8,128)(2,1)} %collective-permute-done.4.refs_1_, bf16[2,128,512]{2,1,0:T(8,128)(2,1)} %collective-permute-done.15.refs_2_, bf16[2,128,512]{2,1,0:T(8,128)(2,1)} %collective-permute-done.16.refs_3_, ...), custom_call_target="tpu_custom_call" | custom-call | flops 1000000 | bytes 1000 | tf_op jit(solution)/shard_map/pack/pallas_call | solution.py:188
  94.8 5.6 %project.1 = (f32[128,1024]{1,0:T(8,128)}, bf16[128,1536]{1,0:T(8,128)(2,1)}, bf16[128,1536]{1,0:T(8,128)(2,1)}, bf16[128,1536]{1,0:T(8,128)(2,1)}) custom-call(s32[5]{0:T(128)} %stack.23.coord_ref, bf16[128,5120]{1,0:T(8,128)(2,1)} %bitcast.25, bf16[128,1280]{1,0:T(8,128)(2,1)} %copy-done.13, bf16[128,1280]{1,0:T(8,128)(2,1)} %copy-done.12, ...), custom_call_target="tpu_custom_call" | custom-call | flops 99999997952 | bytes 1000 | tf_op jit(solution)/shard_map/project/pallas_call | solution.py:165
  100.4 4.9 %collective-permute-start.12 = (bf16[128,1536]{1,0:T(8,128)(2,1)}, bf16[128,1536]{1,0:T(8,128)(2,1)S(1)}, u32[]{:S(2)}, u32[]{:S(2)}) collective-permute-start(bf16[128,1536]{1,0:T(8,128)(2,1)} %get-tuple-element.46), channel_id=1, source_target_pairs={{0,256},{1,257},{4,260},{5,261},{8,264},{9,265},{12,268},{13,269},... | collective-permute-start | bytes 1179656 | tf_op jit(solution)/shard_map/ppermute | solution.py:44
  105.2 2.8 %collective-permute-start.13 = (bf16[128,1536]{1,0:T(8,128)(2,1)}, bf16[128,1536]{1,0:T(8,128)(2,1)S(1)}, u32[]{:S(2)}, u32[]{:S(2)}) collective-permute-start(bf16[128,1536]{1,0:T(8,128)(2,1)} %get-tuple-element.47), channel_id=1, source_target_pairs={{0,128},{1,129},{4,132},{5,133},{8,136},{9,137},{12,140},{13,141},... | collective-permute-start | bytes 1179656 | tf_op jit(solution)/shard_map/ppermute | solution.py:44
  108.1 4.4 %collective-permute-start.14 = (bf16[128,1536]{1,0:T(8,128)(2,1)}, bf16[128,1536]{1,0:T(8,128)(2,1)S(1)}, u32[]{:S(2)}, u32[]{:S(2)}) collective-permute-start(bf16[128,1536]{1,0:T(8,128)(2,1)} %get-tuple-element.48), channel_id=1, source_target_pairs={{0,384},{1,385},{4,388},{5,389},{8,392},{9,393},{12,396},{13,397},... | collective-permute-start | bytes 1179656 | tf_op jit(solution)/shard_map/ppermute | solution.py:44
  113.8 7.0 %own_blocks.1 = (f32[128,4096]{1,0:T(8,128)S(1)}, f32[128,4096]{1,0:T(8,128)S(1)}, f32[128,4096]{1,0:T(8,128)S(1)}) custom-call(s32[5]{0:T(128)S(1)} %copy-done.4, s32[1,16]{1,0:T(1,128)S(1)} %copy-done.6, s32[1]{0:T(128)S(6)} %copy.10.fork_ref, bf16[128,4096]{1,0:T(8,128)(2,1)S(1)} %bitcast.15, bf16[4,2,128,512]{3,2,1,0:T(8,128)(2,1)S(1)} %bitcast.19, ...), custom_call_target="tpu_custom_call" | custom-call | flops 1000000000 | bytes 1000 | tf_op jit(solution)/shard_map/own_blocks/pallas_call | solution.py:302
  120.8 6.6 %other_blocks.1 = (f32[128,4096]{1,0:T(8,128)S(1)}, f32[128,4096]{1,0:T(8,128)S(1)}, f32[128,4096]{1,0:T(8,128)S(1)}) custom-call(s32[5]{0:T(128)S(1)} %copy-done.4, s32[1,16]{1,0:T(1,128)S(1)} %copy-done.6, s32[1]{0:T(128)S(6)} %copy.10.fork_ref, bf16[128,4096]{1,0:T(8,128)(2,1)S(1)} %bitcast.16, bf16[8,2,128,512]{3,2,1,0:T(8,128)(2,1)S(1)} %bitcast.18, ...), custom_call_target="tpu_custom_call" | custom-call | flops 1000000000 | bytes 1000 | tf_op jit(solution)/shard_map/other_blocks/pallas_call | solution.py:302
  127.5 3.9 %segment_block.1 = bf16[128,4096]{1,0:T(8,128)(2,1)} custom-call(s32[5]{0:T(128)S(1)} %copy-done.4, s32[1,16]{1,0:T(1,128)S(1)} %copy-done.6, s32[1]{0:T(128)S(6)} %copy.10.fork_ref, bf16[128,4096]{1,0:T(8,128)(2,1)S(1)} %bitcast.17, f32[128,128]{1,0:T(8,128)S(1)} %get-tuple-element.37.refs_0_, f32[128,128]{1,0:T(8,128)S(1)} %get-tuple-element.38.refs_1_, ...), custom_call_target="tpu_custom_call" | custom-call | flops 1000000000 | bytes 1000 | tf_op jit(solution)/shard_map/segment_block/pallas_call | solution.py:302
  (65 shorter events, 24.4 us)
Async XLA Ops:
  2.4 20.8 %copy-start.5 = (s32[1,16]{1,0:T(1,128)S(1)}, s32[1,16]{1,0:T(1,128)}, u32[]{:S(2)}) copy-start(s32[1,16]{1,0:T(1,128)} %mask_ref.5) | copy-start | bytes 196
  2.4 22.9 %collective-permute-start = (bf16[416,512]{1,0:T(8,128)(2,1)}, bf16[416,512]{1,0:T(8,128)(2,1)S(1)}, u32[]{:S(2)}, u32[]{:S(2)}) collective-permute-start(bf16[416,512]{1,0:T(8,128)(2,1)} %pick_load.1.load_ref), channel_id=1, source_target_pairs={{0,64},{1,67},{4,68},{5,71},{8,72},{9,75},{12,76},{13,79},{16,80},... | collective-permute-start | bytes 1277960 | tf_op jit(solution)/shard_map/ppermute | solution.py:44
  13.4 12.1 %collective-permute-start.1 = (bf16[2,128,512]{2,1,0:T(8,128)(2,1)}, bf16[2,128,512]{2,1,0:T(8,128)(2,1)S(1)}, u32[]{:S(2)}, u32[]{:S(2)}) collective-permute-start(bf16[2,128,512]{2,1,0:T(8,128)(2,1)} %pick_unit.1.refs_0_), channel_id=1, source_target_pairs={{0,8},{1,9},{4,12},{5,13},{8,0},{9,1},{12,4},{13,5},{16,24},{17,25... | collective-permute-start | bytes 786440 | tf_op jit(solution)/shard_map/ppermute | solution.py:44
  16.5 11.3 %collective-permute-start.2 = (bf16[2,128,512]{2,1,0:T(8,128)(2,1)}, bf16[2,128,512]{2,1,0:T(8,128)(2,1)S(1)}, u32[]{:S(2)}, u32[]{:S(2)}) collective-permute-start(bf16[2,128,512]{2,1,0:T(8,128)(2,1)} %pick_unit.1.refs_0_), channel_id=1, source_target_pairs={{0,4},{1,5},{4,8},{5,9},{8,12},{9,13},{12,0},{13,1},{16,20},{17,21... | collective-permute-start | bytes 786440 | tf_op jit(solution)/shard_map/ppermute | solution.py:44
  20.6 10.8 %collective-permute-start.3 = (bf16[2,128,512]{2,1,0:T(8,128)(2,1)}, bf16[2,128,512]{2,1,0:T(8,128)(2,1)S(1)}, u32[]{:S(2)}, u32[]{:S(2)}) collective-permute-start(bf16[2,128,512]{2,1,0:T(8,128)(2,1)} %pick_unit.1.refs_0_), channel_id=1, source_target_pairs={{0,12},{1,13},{4,0},{5,1},{8,4},{9,5},{12,8},{13,9},{16,28},{17,29... | collective-permute-start | bytes 786440 | tf_op jit(solution)/shard_map/ppermute | solution.py:44
  31.4 29.9 %collective-permute-start.5 = (bf16[320,512]{1,0:T(8,128)(2,1)S(1)}, bf16[320,512]{1,0:T(8,128)(2,1)S(1)}, u32[]{:S(2)}, u32[]{:S(2)}) collective-permute-start(bf16[320,512]{1,0:T(8,128)(2,1)S(1)} %pad_maximum_fusion), channel_id=1, source_target_pairs={{0,32},{1,99},{4,36},{5,103},{8,40},{9,107},{12,44},{13,111},{16,4... | collective-permute-start | bytes 983048 | tf_op jit(solution)/shard_map/ppermute | solution.py:44
  38.2 23.1 %collective-permute-start.4 = (bf16[2,128,512]{2,1,0:T(8,128)(2,1)S(1)}, bf16[2,128,512]{2,1,0:T(8,128)(2,1)}, u32[]{:S(2)}, u32[]{:S(2)}) collective-permute-start(bf16[2,128,512]{2,1,0:T(8,128)(2,1)S(1)} %bitcast.21), channel_id=1, source_target_pairs={{0,64},{1,67},{4,68},{5,71},{8,72},{9,75},{12,76},{13,79},{16,80},... | collective-permute-start | bytes 786440 | tf_op jit(solution)/shard_map/ppermute | solution.py:44
  42.8 41.4 %copy-start.8 = (bf16[2,128,512]{2,1,0:T(8,128)(2,1)S(1)}, bf16[2,128,512]{2,1,0:T(8,128)(2,1)}, u32[]{:S(2)}) copy-start(bf16[2,128,512]{2,1,0:T(8,128)(2,1)} %pick_unit.1.refs_0_) | copy-start | bytes 786436
  45.2 16.1 %collective-permute-start.6 = (bf16[128,1280]{1,0:T(8,128)(2,1)}, bf16[128,1280]{1,0:T(8,128)(2,1)S(1)}, u32[]{:S(2)}, u32[]{:S(2)}) collective-permute-start(bf16[128,1280]{1,0:T(8,128)(2,1)} %get-tuple-element.34), channel_id=1, source_target_pairs={{0,256},{1,257},{4,260},{5,261},{8,264},{9,265},{12,268},{13,269},... | collective-permute-start | bytes 983048 | tf_op jit(solution)/shard_map/ppermute | solution.py:44
  50.1 16.2 %collective-permute-start.7 = (bf16[128,1280]{1,0:T(8,128)(2,1)}, bf16[128,1280]{1,0:T(8,128)(2,1)S(1)}, u32[]{:S(2)}, u32[]{:S(2)}) collective-permute-start(bf16[128,1280]{1,0:T(8,128)(2,1)} %get-tuple-element.35), channel_id=1, source_target_pairs={{0,128},{1,129},{4,132},{5,133},{8,136},{9,137},{12,140},{13,141},... | collective-permute-start | bytes 983048 | tf_op jit(solution)/shard_map/ppermute | solution.py:44
  52.6 13.7 %collective-permute-start.8 = (bf16[128,1280]{1,0:T(8,128)(2,1)}, bf16[128,1280]{1,0:T(8,128)(2,1)S(1)}, u32[]{:S(2)}, u32[]{:S(2)}) collective-permute-start(bf16[128,1280]{1,0:T(8,128)(2,1)} %get-tuple-element.36), channel_id=1, source_target_pairs={{0,384},{1,385},{4,388},{5,389},{8,392},{9,393},{12,396},{13,397},... | collective-permute-start | bytes 983048 | tf_op jit(solution)/shard_map/ppermute | solution.py:44
  61.3 20.9 %copy-start.12 = (bf16[128,1280]{1,0:T(8,128)(2,1)}, bf16[128,1280]{1,0:T(8,128)(2,1)S(1)}, u32[]{:S(2)}) copy-start(bf16[128,1280]{1,0:T(8,128)(2,1)S(1)} %collective-permute-done.6.refs_1_) | copy-start | bytes 983044
  66.4 14.3 %collective-permute-start.10 = (bf16[640,512]{1,0:T(8,128)(2,1)S(1)}, bf16[640,512]{1,0:T(8,128)(2,1)S(1)}, u32[]{:S(2)}, u32[]{:S(2)}) collective-permute-start(bf16[640,512]{1,0:T(8,128)(2,1)S(1)} %constant_dynamic-update-slice_fusion.refs_3_), channel_id=1, source_target_pairs={{0,1},{1,0},{2,3},{3,2},{4,5},{5,4},{6,7},{7,6},{8,9},{9,8},{10,11... | collective-permute-start | bytes 1966088 | tf_op jit(solution)/shard_map/ppermute | solution.py:49
  68.5 13.8 %collective-permute-start.9 = (bf16[640,512]{1,0:T(8,128)(2,1)S(1)}, bf16[640,512]{1,0:T(8,128)(2,1)}, u32[]{:S(2)}, u32[]{:S(2)}) collective-permute-start(bf16[640,512]{1,0:T(8,128)(2,1)S(1)} %constant_dynamic-update-slice_fusion.refs_3_), channel_id=1, source_target_pairs={{0,16},{1,115},{4,20},{5,119},{8,24},{9,123},{12,28},{13,127},{16,... | collective-permute-start | bytes 1966088 | tf_op jit(solution)/shard_map/ppermute | solution.py:44
  71.5 12.8 %collective-permute-start.15 = (bf16[2,128,512]{2,1,0:T(8,128)(2,1)}, bf16[2,128,512]{2,1,0:T(8,128)(2,1)}, u32[]{:S(2)}, u32[]{:S(2)}) collective-permute-start(bf16[2,128,512]{2,1,0:T(8,128)(2,1)} %collective-permute-done.4.refs_1_), channel_id=1, source_target_pairs={{0,8},{1,9},{4,12},{5,13},{8,0},{9,1},{12,4},{13,5},{16,24},{17,25... | collective-permute-start | bytes 786440 | tf_op jit(solution)/shard_map/ppermute | solution.py:44
  74.7 12.6 %collective-permute-start.16 = (bf16[2,128,512]{2,1,0:T(8,128)(2,1)}, bf16[2,128,512]{2,1,0:T(8,128)(2,1)}, u32[]{:S(2)}, u32[]{:S(2)}) collective-permute-start(bf16[2,128,512]{2,1,0:T(8,128)(2,1)} %collective-permute-done.4.refs_1_), channel_id=1, source_target_pairs={{0,4},{1,5},{4,8},{5,9},{8,12},{9,13},{12,0},{13,1},{16,20},{17,21... | collective-permute-start | bytes 786440 | tf_op jit(solution)/shard_map/ppermute | solution.py:44
  78.8 11.3 %collective-permute-start.17 = (bf16[2,128,512]{2,1,0:T(8,128)(2,1)}, bf16[2,128,512]{2,1,0:T(8,128)(2,1)}, u32[]{:S(2)}, u32[]{:S(2)}) collective-permute-start(bf16[2,128,512]{2,1,0:T(8,128)(2,1)} %collective-permute-done.4.refs_1_), channel_id=1, source_target_pairs={{0,12},{1,13},{4,0},{5,1},{8,4},{9,5},{12,8},{13,9},{16,28},{17,29... | collective-permute-start | bytes 786440 | tf_op jit(solution)/shard_map/ppermute | solution.py:44
  82.3 12.5 %collective-permute-start.11 = (bf16[640,512]{1,0:T(8,128)(2,1)}, bf16[640,512]{1,0:T(8,128)(2,1)}, u32[]{:S(2)}, u32[]{:S(2)}) collective-permute-start(bf16[640,512]{1,0:T(8,128)(2,1)} %collective-permute-done.9.refs_4_), channel_id=1, source_target_pairs={{0,1},{1,0},{2,3},{3,2},{4,5},{5,4},{6,7},{7,6},{8,9},{9,8},{10,11... | collective-permute-start | bytes 1966088 | tf_op jit(solution)/shard_map/ppermute | solution.py:49
  92.7 19.8 %copy-start.4 = (s32[5]{0:T(128)S(1)}, s32[5]{0:T(128)}, u32[]{:S(2)}) copy-start(s32[5]{0:T(128)} %stack.23.coord_ref) | copy-start | bytes 64
  92.7 19.8 %copy-start.6 = (s32[1,16]{1,0:T(1,128)S(1)}, s32[1,16]{1,0:T(1,128)}, u32[]{:S(2)}) copy-start(s32[1,16]{1,0:T(1,128)} %mask_ref.5) | copy-start | bytes 196
  92.7 28.0 %collective-permute-start.18 = (bf16[16,128,512]{2,1,0:T(8,128)(2,1)}, bf16[16,128,512]{2,1,0:T(8,128)(2,1)S(1)}, u32[]{:S(2)}, u32[]{:S(2)}) collective-permute-start(bf16[16,128,512]{2,1,0:T(8,128)(2,1)} %pack.3), channel_id=1, source_target_pairs={{0,1},{1,0},{2,3},{3,2},{4,5},{5,4},{6,7},{7,6},{8,9},{9,8},{10,11... | collective-permute-start | bytes 6291464 | tf_op jit(solution)/shard_map/ppermute | solution.py:49
  100.4 27.0 %collective-permute-start.12 = (bf16[128,1536]{1,0:T(8,128)(2,1)}, bf16[128,1536]{1,0:T(8,128)(2,1)S(1)}, u32[]{:S(2)}, u32[]{:S(2)}) collective-permute-start(bf16[128,1536]{1,0:T(8,128)(2,1)} %get-tuple-element.46), channel_id=1, source_target_pairs={{0,256},{1,257},{4,260},{5,261},{8,264},{9,265},{12,268},{13,269},... | collective-permute-start | bytes 1179656 | tf_op jit(solution)/shard_map/ppermute | solution.py:44
  105.2 22.2 %collective-permute-start.13 = (bf16[128,1536]{1,0:T(8,128)(2,1)}, bf16[128,1536]{1,0:T(8,128)(2,1)S(1)}, u32[]{:S(2)}, u32[]{:S(2)}) collective-permute-start(bf16[128,1536]{1,0:T(8,128)(2,1)} %get-tuple-element.47), channel_id=1, source_target_pairs={{0,128},{1,129},{4,132},{5,133},{8,136},{9,137},{12,140},{13,141},... | collective-permute-start | bytes 1179656 | tf_op jit(solution)/shard_map/ppermute | solution.py:44
  108.1 19.3 %collective-permute-start.14 = (bf16[128,1536]{1,0:T(8,128)(2,1)}, bf16[128,1536]{1,0:T(8,128)(2,1)S(1)}, u32[]{:S(2)}, u32[]{:S(2)}) collective-permute-start(bf16[128,1536]{1,0:T(8,128)(2,1)} %get-tuple-element.48), channel_id=1, source_target_pairs={{0,384},{1,385},{4,388},{5,389},{8,392},{9,393},{12,396},{13,397},... | collective-permute-start | bytes 1179656 | tf_op jit(solution)/shard_map/ppermute | solution.py:44
  (10 other events, 109.3 us)
